TPU v7x, 1024 devices: a whole 4x4x32 slice. The times are simulated.
1024 devices in a mesh: dp: 64 (over z, core), expert: 16 (over x, y).
Axes of the slice: x: 4, y: 4, z: 32, core: 2. Of those that a mesh axis runs over, the one named last changes fastest.
Arguments:
- tokens: bfloat16 [4096, 4096], P('dp', 'expert'), may hold values from -6 to 6
- grad_out: bfloat16 [4096, 4096], P('dp', 'expert'), may hold values from -6 to 6
- picked: int32 [64, 16, 3], P('dp'), may hold values from 0 to 63, as said below
- pick_counts: int32 [64, 16], P('dp'), may hold values from 1 to 3, as said below
- router_weights: float32 [64, 16, 3], P('dp'), may hold values from 0.1 to 1
- saved_gate: bfloat16 [16, 192, 2048], P('expert', 'dp'), may hold values from -6 to 6
- saved_up: bfloat16 [16, 192, 2048], P('expert', 'dp'), may hold values from -6 to 6
- w_gate: bfloat16 [16, 4096, 2048], P('expert', 'dp'), may hold values from -0.09375 to 0.09375
- w_up: bfloat16 [16, 4096, 2048], P('expert', 'dp'), may hold values from -0.09375 to 0.09375
- w_down: bfloat16 [16, 2048, 4096], P('expert', None, 'dp'), may hold values from -0.125 to 0.125
Outputs:
- token_grad: bfloat16 [4096, 4096], P('dp', 'expert')
- w_gate_grad: float32 [16, 4096, 2048], P('expert', 'dp')
- w_up_grad: float32 [16, 4096, 2048], P('expert', 'dp')
- w_down_grad: float32 [16, 2048, 4096], P('expert', None, 'dp')
Inputs may be any that keep to these rules, and one draw needn't show every extreme that they name: `picked`: the 3 entries for one shard and one expert are distinct token numbers of that shard; only the first pick_counts of them are picks. `pick_counts`: in every draw some expert has 3 picks from every shard, and every shard gives 3 picks to some expert.
All inputs are finite; a program needn't handle non-finite values.
Results may differ from a plain program's by a relative error of at most 0.0067.
Values may be sent and summed in bfloat16 or wider, within the bound.
No kernel may reach another device: no remote copies, remote signals or barrier semaphores. Data moves between devices by JAX's collectives and lax.ppermute only.
A program may use at most 32 MiB of HBM per device.

v0:
```python
import jax
import jax.numpy as jnp
from jax import lax
from jax.sharding import PartitionSpec as P


def hidden_terms(hidden_grad, gate_value, up_value):
    gate_float = gate_value.astype(jnp.float32)
    up_float = up_value.astype(jnp.float32)
    hidden_float = hidden_grad.astype(jnp.float32)
    sigmoid_gate = jax.nn.sigmoid(gate_float)
    activated = (gate_float * sigmoid_gate * up_float).astype(jnp.bfloat16)
    gate_grad = (
        hidden_float * up_float * sigmoid_gate * (1.0 + gate_float * (1.0 - sigmoid_gate))
    ).astype(jnp.bfloat16)
    up_grad = (hidden_float * gate_float * sigmoid_gate).astype(jnp.bfloat16)
    return (activated, gate_grad, up_grad)


def weight_terms(input_piece, output_piece, activated, gate_grad, up_grad, gate_local, up_local):
    gate_part = jnp.einsum("rd,rf->df", input_piece, gate_grad, preferred_element_type=jnp.float32)
    up_part = jnp.einsum("rd,rf->df", input_piece, up_grad, preferred_element_type=jnp.float32)
    down_part = jnp.einsum("rf,rd->fd", activated, output_piece, preferred_element_type=jnp.float32)
    slot_part = jnp.einsum(
        "rf,df->rd", gate_grad, gate_local, preferred_element_type=jnp.float32
    ) + jnp.einsum("rf,df->rd", up_grad, up_local, preferred_element_type=jnp.float32)
    return (gate_part, up_part, down_part, slot_part)


def local(
    tokens,
    grad_out,
    picked,
    pick_counts,
    router_weights,
    saved_gate,
    saved_up,
    w_gate,
    w_up,
    w_down,
):
    capacity = picked.shape[2]
    experts_here = picked.shape[1]
    token_count = tokens.shape[0]
    gate_local = w_gate[0]
    up_local = w_up[0]
    down_local = w_down[0]
    slot_index = jnp.arange(capacity, dtype=jnp.int32)
    live_slots = slot_index[None, :] < pick_counts[0][:, None]
    scales = jnp.where(live_slots, router_weights[0], jnp.float32(0.0))
    flat_picks = picked[0].reshape(-1)
    input_rows = jnp.take(tokens, flat_picks, axis=0).reshape(experts_here, capacity, -1)
    output_rows = jnp.take(grad_out, flat_picks, axis=0).reshape(experts_here, capacity, -1)
    output_rows = (output_rows.astype(jnp.float32) * scales[:, :, None]).astype(jnp.bfloat16)
    outgoing = jnp.stack([input_rows, output_rows])
    turned = lax.all_to_all(down_local, "dp", split_axis=0, concat_axis=1, tiled=True)
    arrived = lax.all_to_all(
        lax.all_to_all(outgoing, "expert", split_axis=1, concat_axis=3, tiled=True),
        "dp",
        split_axis=3,
        concat_axis=1,
        tiled=True,
    )
    slot_total = arrived.shape[1] * capacity
    gathered_in = arrived[0].reshape(slot_total, arrived.shape[3])
    gathered_out = arrived[1].reshape(slot_total, arrived.shape[3])
    narrow = jnp.einsum(
        "rd,fd->rf",
        lax.all_gather(gathered_out, "dp", axis=1, tiled=True),
        turned,
        preferred_element_type=jnp.float32,
    )
    hidden_grad = lax.all_to_all(
        narrow.astype(jnp.bfloat16), "dp", split_axis=0, concat_axis=1, tiled=True
    )
    width_slice = gathered_in.shape[1]
    activated, gate_grad, up_grad = hidden_terms(hidden_grad, saved_gate[0], saved_up[0])
    gate_part, up_part, down_part, slot_part = weight_terms(
        gathered_in,
        gathered_out,
        lax.all_gather(activated, "dp", axis=0, tiled=True),
        lax.all_gather(gate_grad, "dp", axis=0, tiled=True),
        lax.all_gather(up_grad, "dp", axis=0, tiled=True),
        gate_local,
        up_local,
    )
    slot_grad = slot_part.astype(jnp.bfloat16).reshape(arrived.shape[1], capacity, width_slice)
    returned = lax.all_to_all(
        lax.all_to_all(slot_grad, "dp", split_axis=0, concat_axis=2, tiled=True),
        "expert",
        split_axis=2,
        concat_axis=0,
        tiled=True,
    )
    returned = returned.reshape(experts_here * capacity, returned.shape[2])
    owner_table = (flat_picks[None, :] == jnp.arange(token_count, dtype=jnp.int32)[:, None]).astype(
        jnp.bfloat16
    )
    token_grad = jnp.dot(owner_table, returned, preferred_element_type=jnp.float32).astype(
        jnp.bfloat16
    )
    return (token_grad, gate_part[None], up_part[None], down_part[None])


def solution(mesh):
    placed = (
        P("dp", "expert"),
        P("dp", "expert"),
        P("dp", None, None),
        P("dp", None),
        P("dp", None, None),
        P("expert", "dp", None),
        P("expert", "dp", None),
        P("expert", "dp", None),
        P("expert", "dp", None),
        P("expert", None, "dp"),
    )
    return jax.shard_map(
        local,
        mesh=mesh,
        in_specs=placed,
        out_specs=(
            P("dp", "expert"),
            P("expert", "dp", None),
            P("expert", "dp", None),
            P("expert", None, "dp"),
        ),
        check_vma=False,
    )
```

profile of v0, /device:TPU:1, one launch (start us, length us, event | category | flops | bytes accessed | tf_op | source)
XLA Modules:
  0.0 499.2 jit_solution(12153883119031880469)
XLA Ops:
  7.2 0.0 copy-start
  7.2 0.0 all-gather.5.cloned.1.call-start
  7.2 0.8 copy.75
  8.0 0.1 eq.15
  8.1 0.7 bitcast_select_fusion
  8.8 0.1 copy.76
  8.9 1.4 gather_fusion.1
  10.3 1.4 gather_fusion
  11.7 0.1 broadcast_select_fusion
  11.8 0.1 multiply_convert_fusion
  12.0 0.1 copy.77
  12.1 13.9 %all_to_all.98 = bf16[2,16,3,256]{3,0,2,1:T(2,128)(2,1)S(1)} all-to-all(bf16[2,16,3,256]{3,0,2,1:T(2,128)(2,1)S(1)} %copy.77), channel_id=1, replica_groups=mesh['dp'=64,'expert'=16] {'expert'}, dimensions={1} | all-to-all | bytes 98304 | tf_op jit(solution)/shard_map/all_to_all | solution.py:58
  25.9 1.8 copy.93
  27.7 3.3 reshape.122
  31.1 56.0 %all_to_all.99 = bf16[64,2,192]{2,1,0:T(2,128)(2,1)S(1)} all-to-all(bf16[64,2,192]{2,1,0:T(2,128)(2,1)S(1)} %reshape.122), channel_id=1, replica_groups=mesh['dp'=64,'expert'=16] {'dp'}, dimensions={0} | all-to-all | bytes 98304 | tf_op jit(solution)/shard_map/all_to_all | solution.py:57
  87.1 4.6 reshape.123
  91.7 1.8 copy.94
  93.6 0.7 copy.82
  94.3 0.0 all-gather.5.cloned.1.call-update
  94.4 0.0 copy-done.1
  94.4 0.3 copy.83
  94.6 0.3 reshape.120
  95.0 48.8 %all_to_all.100 = bf16[64,2,1024]{2,1,0:T(2,128)(2,1)S(1)} all-to-all(bf16[64,2,1024]{2,1,0:T(2,128)(2,1)S(1)} %reshape.120), channel_id=1, replica_groups=mesh['dp'=64,'expert'=16] {'dp'}, dimensions={0} | all-to-all | bytes 524288 | tf_op jit(solution)/shard_map/all_to_all | solution.py:56
  143.7 0.3 reshape.121
  144.1 0.2 copy.84
  144.3 0.0 copy-start.3
  144.3 0.0 copy-start.4
  144.3 0.5 all_to_all.82
  144.8 72.2 %all-gather.5.cloned.1.call-done = bf16[192,4096]{0,1:T(8,128)(2,1)} async-done(((bf16[192,64]{0,1:T(8,128)(2,1)}), bf16[192,4096]{0,1:T(8,128)(2,1)}) %all-gather.5.cloned.1.call-update) | async-done | bytes 1572880 | tf_op jit(solution)/shard_map/all_gather | solution.py:69
  216.9 2.0 convolution_convert_fusion.1
  219.0 0.1 copy.85
  219.1 0.7 all_to_all.83
  219.8 13.4 %all-to-all-start.3 = ((bf16[64,3,32]{2,1,0:T(4,128)(2,1)}), bf16[64,3,32]{2,1,0:T(4,128)(2,1)S(1)}, u32[]{:S(2)}, u32[]{:S(2)}) async-start(bf16[64,3,32]{2,1,0:T(4,128)(2,1)} %all_to_all.83), calls=%async_computation.3 | async-start | bytes 131072 | tf_op jit(solution)/shard_map/all_to_all | solution.py:73
  233.3 24.9 %all-to-all-done.3 = bf16[64,3,32]{2,1,0:T(4,128)(2,1)S(1)} async-done(((bf16[64,3,32]{2,1,0:T(4,128)(2,1)}), bf16[64,3,32]{2,1,0:T(4,128)(2,1)S(1)}, u32[]{:S(2)}, u32[]{:S(2)}) %all-to-all-start.3) | async-done | bytes 12320 | tf_op jit(solution)/shard_map/all_to_all | solution.py:73
  258.2 0.1 reshape.89
  258.4 0.1 fusion.14
  258.4 57.2 %all-gather.1 = bf16[64,3,2048]{2,1,0:T(4,128)(2,1)S(1)} all-gather(bf16[1,3,2048]{2,1,0:T(4,128)(2,1)S(1)} %get-tuple-element.7), channel_id=1, replica_groups=mesh['dp'=64,'expert'=16] {'dp'}, dimensions={0}, use_global_device_ids=true | all-gather | bytes 798720 | tf_op jit(solution)/shard_map/all_gather | solution.py:83
  315.7 0.7 reshape.113
  316.3 0.0 copy-start.2
  316.4 56.3 %all-gather = bf16[64,3,2048]{2,1,0:T(4,128)(2,1)S(1)} all-gather(bf16[1,3,2048]{2,1,0:T(4,128)(2,1)S(1)} %get-tuple-element.8), channel_id=1, replica_groups=mesh['dp'=64,'expert'=16] {'dp'}, dimensions={0}, use_global_device_ids=true | all-gather | bytes 798720 | tf_op jit(solution)/shard_map/all_gather | solution.py:82
  372.7 0.7 reshape.111
  373.4 0.0 copy-done
  373.4 0.4 fusion.2
  373.8 0.0 copy-done.2
  373.8 0.4 fusion
  374.2 0.1 copy.87
  374.3 0.7 reshape.86
  375.0 6.3 %all-to-all-start.4 = ((bf16[64,3,64]{2,1,0:T(4,128)(2,1)}), bf16[64,3,64]{2,1,0:T(4,128)(2,1)S(1)}, u32[]{:S(2)}, u32[]{:S(2)}) async-start(bf16[64,3,64]{2,1,0:T(4,128)(2,1)} %reshape.86), calls=%async_computation.4 | async-start | bytes 131072 | tf_op jit(solution)/shard_map/all_to_all | solution.py:89
  381.3 62.1 %all-gather.2 = bf16[64,3,2048]{2,1,0:T(4,128)(2,1)S(1)} all-gather(bf16[1,3,2048]{2,1,0:T(4,128)(2,1)S(1)} %get-tuple-element.9), channel_id=1, replica_groups=mesh['dp'=64,'expert'=16] {'dp'}, dimensions={0}, use_global_device_ids=true | all-gather | bytes 798720 | tf_op jit(solution)/shard_map/all_gather | solution.py:81
  443.4 1.1 convolution_bitcast_fusion.1
  444.5 1.4 reshape.115
  445.9 1.1 convolution_bitcast_fusion.2
  447.0 0.0 all-to-all-done.4
  447.0 0.1 all_to_all.88
  447.1 2.8 copy.89
  449.9 0.5 broadcast.47
  450.5 22.4 %reduce = bf16[4096,3]{1,0:T(8,128)(2,1)S(1)} reduce(bf16[4096,1,3]{2,1,0:T(2,128)(2,1)S(1)} %bitcast.86, bf16[]{:T(256)} %broadcast.47), dimensions={1}, to_apply=%bitcast.71.reduce_sub_computation | reduce | bytes 49154
  472.9 2.1 reshape.124
  475.0 5.6 %all-to-all-start.5 = ((bf16[16,2,384]{2,1,0:T(2,128)(2,1)}), bf16[16,2,384]{2,1,0:T(2,128)(2,1)S(1)}, u32[]{:S(2)}, u32[]{:S(2)}) async-start(bf16[16,2,384]{2,1,0:T(2,128)(2,1)} %reshape.124), calls=%async_computation.5 | async-start | bytes 49152 | tf_op jit(solution)/shard_map/all_to_all | solution.py:88
  480.6 2.2 convolution_bitcast_fusion
  482.9 4.2 all-to-all-done.5
  487.1 2.4 reshape.125
  489.5 2.0 copy.90
  491.6 0.7 convolution_convert_fusion
  (20 shorter events, 0.4 us)
Async XLA Ops:
  7.2 366.2 %copy-start = (bf16[1,64,2048]{2,1,0:T(8,128)(2,1)S(1)}, bf16[1,64,2048]{2,1,0:T(8,128)(2,1)}, u32[]{:S(2)}) copy-start(bf16[1,64,2048]{2,1,0:T(8,128)(2,1)} %param.19) | copy-start | bytes 786436
  7.2 209.8 %all-gather.5.cloned.1.call-start = ((), (), s32[]{:S(2)}) async-start(), calls=%async_computation.6 | async-start | bytes 2129920 | tf_op jit(solution)/shard_map/all_gather | solution.py:69
  87.1 7.3 %copy-start.1 = (bf16[1,2048,64]{1,2,0:T(8,128)(2,1)S(1)}, bf16[1,2048,64]{1,2,0:T(8,128)(2,1)}, u32[]{:S(2)}) copy-start(bf16[1,2048,64]{1,2,0:T(8,128)(2,1)} %param.21) | copy-start | bytes 786436
  144.3 114.1 %copy-start.3 = (bf16[1,3,2048]{2,1,0:T(4,128)(2,1)S(1)}, bf16[1,3,2048]{2,1,0:T(4,128)(2,1)}, u32[]{:S(2)}) copy-start(bf16[1,3,2048]{2,1,0:T(4,128)(2,1)} %param.17) | copy-start | bytes 36868
  144.3 114.1 %copy-start.4 = (bf16[1,3,2048]{2,1,0:T(4,128)(2,1)S(1)}, bf16[1,3,2048]{2,1,0:T(4,128)(2,1)}, u32[]{:S(2)}) copy-start(bf16[1,3,2048]{2,1,0:T(4,128)(2,1)} %param.18) | copy-start | bytes 36868
  219.8 38.4 %all-to-all-start.3 = ((bf16[64,3,32]{2,1,0:T(4,128)(2,1)}), bf16[64,3,32]{2,1,0:T(4,128)(2,1)S(1)}, u32[]{:S(2)}, u32[]{:S(2)}) async-start(bf16[64,3,32]{2,1,0:T(4,128)(2,1)} %all_to_all.83), calls=%async_computation.3 | async-start | bytes 131072 | tf_op jit(solution)/shard_map/all_to_all | solution.py:73
  316.3 57.4 %copy-start.2 = (bf16[1,64,2048]{2,1,0:T(8,128)(2,1)S(1)}, bf16[1,64,2048]{2,1,0:T(8,128)(2,1)}, u32[]{:S(2)}) copy-start(bf16[1,64,2048]{2,1,0:T(8,128)(2,1)} %param.20) | copy-start | bytes 786436
  375.0 72.0 %all-to-all-start.4 = ((bf16[64,3,64]{2,1,0:T(4,128)(2,1)}), bf16[64,3,64]{2,1,0:T(4,128)(2,1)S(1)}, u32[]{:S(2)}, u32[]{:S(2)}) async-start(bf16[64,3,64]{2,1,0:T(4,128)(2,1)} %reshape.86), calls=%async_computation.4 | async-start | bytes 131072 | tf_op jit(solution)/shard_map/all_to_all | solution.py:89
  475.0 12.1 %all-to-all-start.5 = ((bf16[16,2,384]{2,1,0:T(2,128)(2,1)}), bf16[16,2,384]{2,1,0:T(2,128)(2,1)S(1)}, u32[]{:S(2)}, u32[]{:S(2)}) async-start(bf16[16,2,384]{2,1,0:T(2,128)(2,1)} %reshape.124), calls=%async_computation.5 | async-start | bytes 49152 | tf_op jit(solution)/shard_map/all_to_all | solution.py:88
Sparse Core Ops, SparseCore 0:
  94.5 122.4 all-gather.4
where the time goes:
time: 500 us; the launch traced here: 499 us
  blocking collectives  294 us (59%)
  waiting for transfers between devices  101 us (20%)
  local copies, waits for them, and re-layouts  32.4 us (6%)
  starting transfers between devices  25.4 us (5%)
  other arithmetic  23.4 us (5%)
  between operations  14.4 us (3%)
  matrix products  7.94 us (2%)
    all_gather x1, waiting for transfers between devices, local(): lax.all_gather(gathered_out, 'dp', axis=1, tiled=True)  72.2 us
    all_gather x1, blocking collectives, local(): lax.all_gather(activated, 'dp', axis=0, tiled=True)  62.1 us
    all_gather x1, blocking collectives, local(): lax.all_gather(up_grad, 'dp', axis=0, tiled=True)  57.2 us
    all_gather x1, blocking collectives, local(): lax.all_gather(gate_grad, 'dp', axis=0, tiled=True)  56.3 us
    all_to_all x1, blocking collectives, local(): lax.all_to_all(lax.all_to_all(outgoing, 'expert', split_axis=1, concat_ax...  56 us
    all_to_all x1, blocking collectives, local(): lax.all_to_all(down_local, 'dp', split_axis=0, concat_axis=1, tiled=True)  48.8 us
    all_to_all x1, waiting for transfers between devices, local(): lax.all_to_all(narrow.astype(jnp.bfloat16), 'dp', split_axis=0, concat_ax...  24.9 us
    unnamed x2, other arithmetic  22.5 us
  transfers between devices with their start and end apart: 4, of which 3 were waited for; matrix products, arithmetic and copies ran while one was open for 1% of the time, Pallas kernels for 0%

commit v1 on v0

v1 whole, which is shorter than its diff:
```python
import functools

import jax
import jax.numpy as jnp
from jax import lax
from jax.experimental import pallas as pl
from jax.experimental.pallas import tpu as pltpu
from jax.sharding import Mesh
from jax.sharding import PartitionSpec as P

BF16 = jnp.bfloat16
F32 = jnp.float32
CAP = 3
HALF = 64
LANES = 128
NT = (((1,), (1,)), ((), ()))
TN = (((0,), (0,)), ((), ()))
VMEM = pl.BlockSpec(memory_space=pltpu.VMEM)
SMEM = pl.BlockSpec(memory_space=pltpu.SMEM)


def call(body, outs, ins, scratch=(), cost=None):
    return pl.pallas_call(
        body,
        out_shape=outs,
        in_specs=ins,
        out_specs=jax.tree.map(lambda _: VMEM, outs),
        scratch_shapes=list(scratch),
        compiler_params=pltpu.CompilerParams(vmem_limit_bytes=40 * 1024 * 1024),
        cost_estimate=cost,
    )


def struct(*shape, dtype=BF16):
    return jax.ShapeDtypeStruct(shape, dtype)


def weave(first, second):
    low = lax.broadcasted_iota(jnp.int32, first.shape, 1) < HALF
    return (
        jnp.where(low, first, pltpu.roll(second, HALF, 1)),
        jnp.where(low, pltpu.roll(first, HALF, 1), second),
    )


def pick_body(picked_ref, counts_ref, weights_ref, tokens_ref, grads_ref, out_ref, wide_in, wide_out, rows):
    wide_in[...] = tokens_ref[...].astype(F32)
    wide_out[...] = grads_ref[...].astype(F32)
    rows[...] = jnp.zeros_like(rows)
    for expert in range(out_ref.shape[0]):
        for c in range(CAP):
            token = picked_ref[c, expert]
            scale = jnp.where(c < counts_ref[0, expert], weights_ref[c, expert], 0.0)
            rows[pl.ds(8 * expert + c, 1), :] = wide_out[pl.ds(token, 1), :] * scale
            rows[pl.ds(8 * expert + 4 + c, 1), :] = wide_in[pl.ds(token, 1), :]
    out_ref[...] = rows[...].reshape(out_ref.shape).astype(BF16)


def turn_body(down_ref, gate_ref, up_ref, out_ref):
    for pair in range(down_ref.shape[1] // LANES):
        columns = slice(pair * LANES, (pair + 1) * LANES)
        block = down_ref[:, columns].astype(F32)
        one, two = weave(block[:32], block[32:])
        out_ref[2 * pair, 0:32, :] = one.astype(BF16)
        out_ref[2 * pair + 1, 0:32, :] = two.astype(BF16)
        one, two = weave(gate_ref[:, columns].astype(F32), up_ref[:, columns].astype(F32))
        blank = jnp.zeros((8 - CAP, LANES), F32)
        out_ref[2 * pair, 32:40, :] = jnp.concatenate([one, blank]).astype(BF16)
        out_ref[2 * pair + 1, 32:40, :] = jnp.concatenate([two, blank]).astype(BF16)


def weave_body(gate_ref, up_ref, out_ref):
    for pair in range(gate_ref.shape[1] // LANES):
        columns = slice(pair * LANES, (pair + 1) * LANES)
        one, two = weave(gate_ref[:, columns].astype(F32), up_ref[:, columns].astype(F32))
        out_ref[:, 2 * pair * LANES : (2 * pair + 1) * LANES] = one.astype(BF16)
        out_ref[:, (2 * pair + 1) * LANES : (2 * pair + 2) * LANES] = two.astype(BF16)


def row_body(blocks_ref, out_ref):
    width = blocks_ref.shape[2]
    for f in range(blocks_ref.shape[0]):
        out_ref[0, :, f * width : (f + 1) * width] = blocks_ref[f, 0:CAP, :]


def spread_body(core_ref, own_ref, other_ref, out_ref):
    first = core_ref[0] == 0
    for z in range(own_ref.shape[0]):
        own = own_ref[z, 0:32, :].astype(F32)
        other = other_ref[z, 0:32, :].astype(F32)
        zero, one = jnp.where(first, own, other), jnp.where(first, other, own)
        parts = [zero, pltpu.roll(zero, HALF, 1), one, pltpu.roll(one, HALF, 1)]
        out_ref[z * LANES : (z + 1) * LANES, :] = jnp.concatenate(parts).astype(BF16)


def hidden_body(sent_ref, down_ref, saved_ref, out_ref):
    hidden = jnp.dot(sent_ref[...], down_ref[...], preferred_element_type=F32)
    hidden = hidden.astype(BF16).astype(F32)
    saved = saved_ref[...].astype(F32)
    a, b = saved, pltpu.roll(saved, HALF, 1)
    q = jax.nn.sigmoid(a)
    gate_grad = hidden * b * q * (1.0 + a * (1.0 - q))
    up_grad = hidden * a * q
    low = lax.broadcasted_iota(jnp.int32, hidden.shape, 1) < HALF
    both = jnp.where(low, gate_grad, pltpu.roll(up_grad, HALF, 1))
    out_ref[...] = both.T.astype(BF16)


def slot_body(core_ref, grads_ref, own_ref, other_ref, blocks_ref, out_ref):
    grads = grads_ref[...]
    own = jnp.dot(own_ref[...], grads, preferred_element_type=F32)
    other = jnp.dot(other_ref[...], grads, preferred_element_type=F32)
    first = core_ref[0] == 0
    whole = jnp.concatenate([jnp.where(first, own, other), jnp.where(first, other, own)]).astype(BF16)
    chips = out_ref.shape[0]
    row = lax.broadcasted_iota(jnp.int32, (8 * chips, CAP * chips), 0)
    slot = lax.broadcasted_iota(jnp.int32, (8 * chips, CAP * chips), 1)
    place = (row // 8 * CAP + row % 8 == slot) & (row % 8 < CAP)
    placed = lax.dot_general(place.astype(BF16), whole, NT, preferred_element_type=F32)
    lower = lax.broadcasted_iota(jnp.int32, (8, LANES), 0) >= 4
    for z in range(chips):
        rows = blocks_ref[z // 2, :, z % 2 * LANES : (z % 2 + 1) * LANES].astype(F32)
        out_ref[z] = jnp.where(lower, rows, placed[8 * z : 8 * z + 8]).astype(BF16)


def weight_body(in_own, in_other, own_ref, other_ref, gate_ref, up_ref):
    chips = own_ref.shape[0]
    for pair in range(chips // 2):
        columns = slice(pair * LANES, (pair + 1) * LANES)
        for start, out_ref in ((0, gate_ref), (HALF, up_ref)):
            total = None
            for rows, grads in ((in_own, own_ref), (in_other, other_ref)):
                block = jnp.concatenate(
                    [grads[2 * pair, start : start + HALF, :], grads[2 * pair + 1, start : start + HALF, :]]
                )
                part = lax.dot_general(rows[...], block, NT, preferred_element_type=F32)
                total = part if total is None else total + part
            out_ref[:, columns] = total


def down_body(sent_ref, act_ref, out_ref):
    out_ref[...] = lax.dot_general(sent_ref[...], act_ref[...], TN, preferred_element_type=F32)


def token_body(index_ref, rows_ref, out_ref):
    tokens = lax.broadcasted_iota(jnp.int32, (out_ref.shape[0], index_ref.shape[1]), 0)
    for half in range(2):
        owner = (tokens == index_ref[half : half + 1, :]).astype(BF16)
        total = jnp.dot(owner, rows_ref[...], preferred_element_type=F32)
        out_ref[:, half * LANES : (half + 1) * LANES] = total.astype(BF16)


def swap(x):
    return lax.ppermute(x, "core", [(0, 1), (1, 0)])


def local(chips, tokens, grad_out, picked, pick_counts, router_weights, saved_gate, saved_up, w_gate, w_up, w_down):
    experts = picked.shape[1]
    token_count, width = tokens.shape
    hidden = w_gate.shape[2]
    slots = CAP * chips
    core = lax.axis_index("core")
    core_word = core.astype(jnp.int32).reshape(1)
    gate_value, up_value = saved_gate[0], saved_up[0]
    picks = picked[0].T

    gate_float = gate_value.astype(F32)
    activated = gate_float * jax.nn.sigmoid(gate_float) * up_value.astype(F32)
    activated = jnp.pad(activated.astype(BF16), ((0, 1), (0, 0)))
    activated = lax.all_gather(activated, ("z", "core"), axis=0, tiled=False)

    turned = call(turn_body, struct(chips, 40, LANES), [VMEM] * 3)(w_down[0].T, gate_value, up_value)
    turned = lax.all_to_all(turned, "z", split_axis=0, concat_axis=0, tiled=True)

    woven = call(weave_body, struct(HALF, 2 * hidden), [VMEM] * 2)(w_gate[0], w_up[0])
    woven_other = swap(woven)

    outgoing = call(
        pick_body,
        struct(experts, 8, width),
        [SMEM] * 3 + [VMEM] * 2,
        scratch=(
            pltpu.VMEM((token_count, width), F32),
            pltpu.VMEM((token_count, width), F32),
            pltpu.VMEM((8 * experts, width), F32),
        ),
    )(picks, pick_counts, router_weights[0].T, tokens, grad_out)
    arrived = lax.all_to_all(outgoing, "expert", split_axis=0, concat_axis=0, tiled=True)
    sent = call(row_body, struct(1, CAP, experts * width), [VMEM])(arrived)
    sent = lax.all_gather(sent, "z", axis=0, tiled=True).reshape(slots, experts * width)

    turned_other = swap(turned[:, 0:32, :])
    down = call(spread_body, struct(experts * width, LANES), [SMEM, VMEM, VMEM])(core_word, turned, turned_other)
    saved = turned[:, 32 : 32 + CAP, :].reshape(slots, LANES)
    grads = call(hidden_body, struct(LANES, slots), [VMEM] * 3)(sent, down, saved)
    grads = lax.all_gather(grads[None], "z", axis=0, tiled=True)

    returned = call(slot_body, struct(chips, 8, LANES), [SMEM] + [VMEM] * 4)(
        core_word, grads.reshape(chips * LANES, slots), woven, woven_other, arrived
    )
    returned = lax.all_to_all(returned, "z", split_axis=0, concat_axis=0, tiled=True)
    back = lax.all_to_all(
        returned.reshape(experts, 16, LANES), "expert", split_axis=0, concat_axis=0, tiled=True
    )

    lane = jnp.arange(16 * experts, dtype=jnp.int32)
    index = jnp.repeat(jnp.pad(picked[0], ((0, 0), (0, 8 - CAP)), constant_values=-1), 2, axis=0).reshape(1, -1)
    index = jnp.where(lane[None, :] // 8 % 2 == jnp.arange(2)[:, None], index, -1)
    token_grad = call(token_body, struct(token_count, width), [VMEM] * 2)(
        index, back.reshape(16 * experts, LANES)
    )

    grads_other = swap(grads)
    chip_width = lax.dynamic_slice_in_dim(sent, lax.axis_index("z") * LANES, LANES, axis=1)

    def parts(x):
        kept = jnp.where(core == 0, x[:, :HALF], x[:, HALF:])
        given = jnp.where(core == 0, x[:, HALF:], x[:, :HALF])
        return kept, swap(given)

    sent_own, sent_other = parts(chip_width)
    both = jnp.stack([jnp.where(core == 0, sent_own, sent_other), jnp.where(core == 0, sent_other, sent_own)], axis=1)
    both = both.reshape(chips, CAP, 2, HALF).transpose(0, 2, 1, 3)
    both = jnp.pad(both, ((0, 0), (0, 0), (0, 1), (0, 0))).reshape(8 * chips, HALF)
    down_grad = call(down_body, struct(HALF, hidden, dtype=F32), [VMEM] * 2)(
        both, activated.reshape(8 * chips, hidden)
    )

    in_own, in_other = parts(returned[:, 4 : 4 + CAP, :].reshape(slots, LANES))
    gate_grad, up_grad = call(
        weight_body, (struct(HALF, hidden, dtype=F32), struct(HALF, hidden, dtype=F32)), [VMEM] * 4
    )(in_own.T, in_other.T, grads, grads_other)
    return (token_grad, gate_grad[None], up_grad[None], down_grad.T[None])


def solution(mesh):
    chips = mesh.shape["dp"] // 2
    fine = Mesh(mesh.devices.reshape(chips, 2, mesh.shape["expert"]), ("z", "core", "expert"))
    dp = ("z", "core")
    placed = (
        P(dp, "expert"),
        P(dp, "expert"),
        P(dp, None, None),
        P(dp, None),
        P(dp, None, None),
        P("expert", dp, None),
        P("expert", dp, None),
        P("expert", dp, None),
        P("expert", dp, None),
        P("expert", None, dp),
    )
    return jax.shard_map(
        functools.partial(local, chips),
        mesh=fine,
        in_specs=placed,
        out_specs=(
            P(dp, "expert"),
            P("expert", dp, None),
            P("expert", dp, None),
            P("expert", None, dp),
        ),
        check_vma=False,
    )
```

time: 500 us -> 284 us (0.57)
  blocking collectives: 294 us -> 93.1 us
  starting transfers between devices: 25.4 us -> 108 us
  waiting for transfers between devices: 101 us -> 46.7 us
  other arithmetic: 23.4 us -> 0.13 us
  local copies, waits for them, and re-layouts: 32.4 us -> 11.6 us
  Pallas kernels: 0 us -> 8.87 us
  matrix products: 7.94 us -> 0 us
    all_to_all x3 -> x0, blocking collectives: 119 us -> none  [the longest x1 56 us: local(): lax.all_to_all(lax.all_to_all(outgoing, 'expert', split_axis=1, concat_ax...]
    all_gather x3 -> x2, blocking collectives: 176 us -> 93.1 us  [the longest x1 47.1 us: local(): grads = lax.all_gather(grads[None], 'z', axis=0, tiled=True)]
    all_gather x1, waiting for transfers between devices: 72.2 us -> 0.02 us  [local(): activated = lax.all_gather(activated, ('z', 'core'), axis=0, tiled=False)]
    ppermute x0 -> x5, starting transfers between devices: none -> 59.8 us  [swap(): return lax.ppermute(x, 'core', [(0, 1), (1, 0)])]
    all_to_all x3 -> x4, starting transfers between devices: 25.4 us -> 48.4 us  [the longest x1 28.5 us: local(): lax.all_to_all(turned, 'z', split_axis=0, concat_axis=0, tiled=True)]
    unnamed x2 -> x0, other arithmetic: 22.5 us -> none
    all_to_all x3 -> x4, waiting for transfers between devices: 29.1 us -> 46.6 us  [the longest x1 37.9 us: local(): lax.all_to_all(turned, 'z', split_axis=0, concat_axis=0, tiled=True)]
    unnamed x23 -> x28, local copies, waits for them, and re-layouts: 17.5 us -> 6.73 us
  transfers between devices with their start and end apart: 4 -> 10, of which waited for: 3 -> 3; matrix products, arithmetic and copies ran while one was open for 1% -> 3% of each run, Pallas kernels for 0% -> 2%
where the time goes in v1:
time: 284 us; the launch traced here: 283 us
  starting transfers between devices  108 us (38%)
  blocking collectives  93.1 us (33%)
  waiting for transfers between devices  46.7 us (16%)
  between operations  14.4 us (5%)
  local copies, waits for them, and re-layouts  11.6 us (4%)
  Pallas kernels  8.87 us (3%)
    ppermute x5, starting transfers between devices, swap(): return lax.ppermute(x, 'core', [(0, 1), (1, 0)])  59.8 us
    all_gather x1, blocking collectives, local(): grads = lax.all_gather(grads[None], 'z', axis=0, tiled=True)  47.1 us
    all_gather x1, blocking collectives, local(): lax.all_gather(sent, 'z', axis=0, tiled=True)  46 us
    all_to_all x1, waiting for transfers between devices, local(): lax.all_to_all(turned, 'z', split_axis=0, concat_axis=0, tiled=True)  37.9 us
    all_to_all x1, starting transfers between devices, local(): lax.all_to_all(turned, 'z', split_axis=0, concat_axis=0, tiled=True)  28.5 us
    all_to_all x1, starting transfers between devices, local(): lax.all_to_all(returned, 'z', split_axis=0, concat_axis=0, tiled=True)  8.75 us
    all_to_all x1, starting transfers between devices, local(): lax.all_to_all(outgoing, 'expert', split_axis=0, concat_axis=0, tiled=True)  7.72 us
    unnamed x28, local copies, waits for them, and re-layouts  6.73 us
  transfers between devices with their start and end apart: 10, of which 3 were waited for; matrix products, arithmetic and copies ran while one was open for 3% of the time, Pallas kernels for 2%

profile of v1, /device:TPU:1, one launch (start us, length us, event | category | flops | bytes accessed | tf_op | source)
XLA Modules:
  0.0 283.0 jit_solution(3699468238987129898)
XLA Ops:
  7.2 0.0 copy-start
  7.2 0.7 copy.48
  7.9 0.7 copy.49
  8.6 0.0 copy-start.6
  8.6 0.8 copy-done.6
  9.3 0.8 copy-done.7
  10.1 0.7 copy-done.8
  10.8 1.4 shard_map.129
  12.2 7.7 %all-to-all-start = ((bf16[16,8,256]{2,1,0:T(8,128)(2,1)}), bf16[16,8,256]{2,1,0:T(8,128)(2,1)S(1)}, u32[]{:S(2)}, u32[]{:S(2)}) async-start(bf16[16,8,256]{2,1,0:T(8,128)(2,1)} %shard_map.129), calls=%async_computation | async-start | bytes 131072 | tf_op jit(solution)/shard_map/all_to_all | solution.py:188
  19.9 0.0 copy-done
  19.9 0.0 copy-done.3
  19.9 0.0 copy-start.4
  19.9 0.7 copy-done.4
  20.6 0.9 shard_map.131
  21.5 4.9 %all-to-all-done.blocks_ref = bf16[16,8,256]{2,1,0:T(8,128)(2,1)S(1)} async-done(((bf16[16,8,256]{2,1,0:T(8,128)(2,1)}), bf16[16,8,256]{2,1,0:T(8,128)(2,1)S(1)}, u32[]{:S(2)}, u32[]{:S(2)}) %all-to-all-start) | async-done | bytes 65568 | tf_op jit(solution)/shard_map/all_to_all | solution.py:188
  26.4 28.5 %all-to-all-start.1 = ((bf16[32,40,128]{2,1,0:T(8,128)(2,1)}), bf16[32,40,128]{2,1,0:T(8,128)(2,1)S(1)}, u32[]{:S(2)}, u32[]{:S(2)}) async-start(bf16[32,40,128]{2,1,0:T(8,128)(2,1)} %shard_map.131), calls=%async_computation.1 | async-start | bytes 655360 | tf_op jit(solution)/shard_map/all_to_all | solution.py:173
  54.9 0.0 all-gather.5.cloned.1.call-start
  54.9 0.0 copy-done.5
  55.0 0.6 pad_bitcast_fusion
  55.6 0.0 all-gather.5.cloned.1.call-update
  55.6 0.0 copy-done.1
  55.6 0.0 copy-done.2
  55.6 0.2 shard_map.134.own_ref
  55.8 4.3 %collective-permute-start.1 = (bf16[64,4096]{1,0:T(8,128)(2,1)S(1)}, bf16[64,4096]{1,0:T(8,128)(2,1)S(1)}, u32[]{:S(2)}, u32[]{:S(2)}) collective-permute-start(bf16[64,4096]{1,0:T(8,128)(2,1)S(1)} %shard_map.134.own_ref), channel_id=1, source_target_pairs={{0,16},{16,0},{1,17},{17,1},{2,18},{18,2},{3,19},{19,3},{4,20},{20... | collective-permute-start | bytes 1572872 | tf_op jit(solution)/shard_map/ppermute | solution.py:154
  60.2 0.1 copy.43
  60.3 0.1 broadcast_in_dim.32
  60.4 37.9 %all-to-all-done.1.own_ref = bf16[32,40,128]{2,1,0:T(8,128)(2,1)S(1)} async-done(((bf16[32,40,128]{2,1,0:T(8,128)(2,1)}), bf16[32,40,128]{2,1,0:T(8,128)(2,1)S(1)}, u32[]{:S(2)}, u32[]{:S(2)}) %all-to-all-start.1) | async-done | bytes 327712 | tf_op jit(solution)/shard_map/all_to_all | solution.py:173
  98.3 0.7 slice.32
  99.0 7.7 %collective-permute-start = (bf16[32,32,128]{2,1,0:T(8,128)(2,1)}, bf16[32,32,128]{2,1,0:T(8,128)(2,1)S(1)}, u32[]{:S(2)}, u32[]{:S(2)}) collective-permute-start(bf16[32,32,128]{2,1,0:T(8,128)(2,1)} %slice.32), channel_id=1, source_target_pairs={{0,16},{16,0},{1,17},{17,1},{2,18},{18,2},{3,19},{19,3},{4,20},{20... | collective-permute-start | bytes 786440 | tf_op jit(solution)/shard_map/ppermute | solution.py:154
  106.7 46.0 %all_gather.12 = bf16[32,3,4096]{2,1,0:T(4,128)(2,1)S(1)} all-gather(bf16[1,3,4096]{2,1,0:T(4,128)(2,1)S(1)} %shard_map.130), channel_id=1, replica_groups=mesh['z'=32,'core'=2,'expert'=16] {'z'}, dimensions={0}, use_global_device_ids=true | all-gather | bytes 811008 | tf_op jit(solution)/shard_map/all_gather | solution.py:190
  152.7 0.7 reshape.96.sent_ref
  153.4 0.1 constant_dynamic-slice_fusion
  153.5 0.1 copy.41
  153.6 0.1 copy.42
  153.7 0.0 collective-permute-done.other_ref
  153.8 0.2 shard_map.132.down_ref
  154.0 0.5 shard_map.133
  154.5 47.1 %all-gather.grads_ref = bf16[4096,96]{1,0:T(8,128)(2,1)S(1)} all-gather(bf16[128,96]{1,0:T(8,128)(2,1)S(1)} %shard_map.133), channel_id=2, replica_groups=mesh['z'=32,'core'=2,'expert'=16] {'z'}, dimensions={0}, use_global_device_ids=true | all-gather | bytes 811008 | tf_op jit(solution)/shard_map/all_gather | solution.py:196
  201.6 0.0 collective-permute-done.1.other_ref
  201.6 1.3 shard_map.135
  202.8 8.8 %all-to-all-start.2 = ((bf16[32,8,128]{2,1,0:T(8,128)(2,1)}), bf16[32,8,128]{2,1,0:T(8,128)(2,1)}, u32[]{:S(2)}, u32[]{:S(2)}) async-start(bf16[32,8,128]{2,1,0:T(8,128)(2,1)} %shard_map.135), calls=%async_computation.2 | async-start | bytes 131072 | tf_op jit(solution)/shard_map/all_to_all | solution.py:201
  211.6 24.9 %collective-permute-start.4 = (bf16[96,64]{0,1:T(8,128)(2,1)S(1)}, bf16[96,64]{0,1:T(8,128)(2,1)S(1)}, u32[]{:S(2)}, u32[]{:S(2)}) collective-permute-start(bf16[96,64]{0,1:T(8,128)(2,1)S(1)} %broadcast_select_fusion.2), channel_id=1, source_target_pairs={{0,16},{16,0},{1,17},{17,1},{2,18},{18,2},{3,19},{19,3},{4,20},{20... | collective-permute-start | bytes 36872 | tf_op jit(solution)/shard_map/ppermute | solution.py:154
  236.6 1.3 copy.30
  237.8 1.9 collective-permute-start.3
  239.7 0.0 collective-permute-done.4
  239.8 0.1 copy.34
  239.9 0.1 copy.33
  240.1 0.0 all-to-all-done.2
  240.1 0.9 slice.34
  241.0 0.1 fusion.5
  241.0 0.1 copy.38
  241.1 0.1 copy.39
  241.2 21.0 %collective-permute-start.2 = (bf16[96,64]{0,1:T(8,128)(2,1)S(1)}, bf16[96,64]{0,1:T(8,128)(2,1)S(1)}, u32[]{:S(2)}, u32[]{:S(2)}) collective-permute-start(bf16[96,64]{0,1:T(8,128)(2,1)S(1)} %get-tuple-element.12), channel_id=1, source_target_pairs={{0,16},{16,0},{1,17},{17,1},{2,18},{18,2},{3,19},{19,3},{4,20},{20... | collective-permute-start | bytes 36872 | tf_op jit(solution)/shard_map/ppermute | solution.py:154
  262.3 3.5 %all-to-all-start.3 = ((bf16[16,16,128]{2,1,0:T(8,128)(2,1)}), bf16[16,16,128]{2,1,0:T(8,128)(2,1)S(1)}, u32[]{:S(2)}, u32[]{:S(2)}) async-start(bf16[16,16,128]{2,1,0:T(8,128)(2,1)} %bitcast.9), calls=%async_computation.3 | async-start | bytes 131072 | tf_op jit(solution)/shard_map/all_to_all | solution.py:202
  265.8 0.1 maximum_bitcast_fusion
  265.9 0.0 all-gather.5.cloned.1.call-done
  265.9 1.3 reshape.109.act_ref
  267.3 1.1 shard_map.138
  268.4 3.8 %all-to-all-done.3 = bf16[16,16,128]{2,1,0:T(8,128)(2,1)S(1)} async-done(((bf16[16,16,128]{2,1,0:T(8,128)(2,1)}), bf16[16,16,128]{2,1,0:T(8,128)(2,1)S(1)}, u32[]{:S(2)}, u32[]{:S(2)}) %all-to-all-start.3) | async-done | bytes 65568 | tf_op jit(solution)/shard_map/all_to_all | solution.py:202
  272.2 0.8 shard_map.136
  273.0 0.0 collective-permute-done.3
  273.0 0.6 copy.31.other_ref
  273.7 0.0 collective-permute-done.2
  273.7 2.5 shard_map.137
  (22 shorter events, 0.3 us)
Async XLA Ops:
  7.2 12.7 %copy-start = (bf16[1,2048,64]{1,2,0:T(8,128)(2,1)S(1)}, bf16[1,2048,64]{1,2,0:T(8,128)(2,1)}, u32[]{:S(2)}) copy-start(bf16[1,2048,64]{1,2,0:T(8,128)(2,1)} %param.19) | copy-start | bytes 786436
  8.6 0.8 copy-start.6
  9.3 0.8 copy-start.7
  10.1 0.7 copy-start.8
  12.1 7.7 %copy-start.3 = (bf16[1,3,2048]{2,1,0:T(4,128)(2,1)S(1)}, bf16[1,3,2048]{2,1,0:T(4,128)(2,1)}, u32[]{:S(2)}) copy-start(bf16[1,3,2048]{2,1,0:T(4,128)(2,1)} %param.15) | copy-start | bytes 36868
  12.2 14.2 %all-to-all-start = ((bf16[16,8,256]{2,1,0:T(8,128)(2,1)}), bf16[16,8,256]{2,1,0:T(8,128)(2,1)S(1)}, u32[]{:S(2)}, u32[]{:S(2)}) async-start(bf16[16,8,256]{2,1,0:T(8,128)(2,1)} %shard_map.129), calls=%async_computation | async-start | bytes 131072 | tf_op jit(solution)/shard_map/all_to_all | solution.py:188
  19.9 0.7 copy-start.4
  21.5 33.4 %copy-start.5 = (bf16[1,3,2048]{2,1,0:T(4,128)(2,1)S(1)}, bf16[1,3,2048]{2,1,0:T(4,128)(2,1)}, u32[]{:S(2)}) copy-start(bf16[1,3,2048]{2,1,0:T(4,128)(2,1)} %param.16) | copy-start | bytes 36868
  21.5 34.1 %copy-start.1 = (bf16[1,64,2048]{2,1,0:T(8,128)(2,1)S(1)}, bf16[1,64,2048]{2,1,0:T(8,128)(2,1)}, u32[]{:S(2)}) copy-start(bf16[1,64,2048]{2,1,0:T(8,128)(2,1)} %param.17) | copy-start | bytes 786436
  21.5 34.1 %copy-start.2 = (bf16[1,64,2048]{2,1,0:T(8,128)(2,1)S(1)}, bf16[1,64,2048]{2,1,0:T(8,128)(2,1)}, u32[]{:S(2)}) copy-start(bf16[1,64,2048]{2,1,0:T(8,128)(2,1)} %param.18) | copy-start | bytes 786436
  26.4 71.9 %all-to-all-start.1 = ((bf16[32,40,128]{2,1,0:T(8,128)(2,1)}), bf16[32,40,128]{2,1,0:T(8,128)(2,1)S(1)}, u32[]{:S(2)}, u32[]{:S(2)}) async-start(bf16[32,40,128]{2,1,0:T(8,128)(2,1)} %shard_map.131), calls=%async_computation.1 | async-start | bytes 655360 | tf_op jit(solution)/shard_map/all_to_all | solution.py:173
  54.9 211.1 %all-gather.5.cloned.1.call-start = ((), (), s32[]{:S(2)}) async-start(), calls=%async_computation.4 | async-start | bytes 1064960 | tf_op jit(solution)/shard_map/all_gather | solution.py:170
  55.8 145.7 %collective-permute-start.1 = (bf16[64,4096]{1,0:T(8,128)(2,1)S(1)}, bf16[64,4096]{1,0:T(8,128)(2,1)S(1)}, u32[]{:S(2)}, u32[]{:S(2)}) collective-permute-start(bf16[64,4096]{1,0:T(8,128)(2,1)S(1)} %shard_map.134.own_ref), channel_id=1, source_target_pairs={{0,16},{16,0},{1,17},{17,1},{2,18},{18,2},{3,19},{19,3},{4,20},{20... | collective-permute-start | bytes 1572872 | tf_op jit(solution)/shard_map/ppermute | solution.py:154
  99.0 54.7 %collective-permute-start = (bf16[32,32,128]{2,1,0:T(8,128)(2,1)}, bf16[32,32,128]{2,1,0:T(8,128)(2,1)S(1)}, u32[]{:S(2)}, u32[]{:S(2)}) collective-permute-start(bf16[32,32,128]{2,1,0:T(8,128)(2,1)} %slice.32), channel_id=1, source_target_pairs={{0,16},{16,0},{1,17},{17,1},{2,18},{18,2},{3,19},{19,3},{4,20},{20... | collective-permute-start | bytes 786440 | tf_op jit(solution)/shard_map/ppermute | solution.py:154
  202.8 37.2 %all-to-all-start.2 = ((bf16[32,8,128]{2,1,0:T(8,128)(2,1)}), bf16[32,8,128]{2,1,0:T(8,128)(2,1)}, u32[]{:S(2)}, u32[]{:S(2)}) async-start(bf16[32,8,128]{2,1,0:T(8,128)(2,1)} %shard_map.135), calls=%async_computation.2 | async-start | bytes 131072 | tf_op jit(solution)/shard_map/all_to_all | solution.py:201
  211.6 28.1 %collective-permute-start.4 = (bf16[96,64]{0,1:T(8,128)(2,1)S(1)}, bf16[96,64]{0,1:T(8,128)(2,1)S(1)}, u32[]{:S(2)}, u32[]{:S(2)}) collective-permute-start(bf16[96,64]{0,1:T(8,128)(2,1)S(1)} %broadcast_select_fusion.2), channel_id=1, source_target_pairs={{0,16},{16,0},{1,17},{17,1},{2,18},{18,2},{3,19},{19,3},{4,20},{20... | collective-permute-start | bytes 36872 | tf_op jit(solution)/shard_map/ppermute | solution.py:154
  237.8 35.2 %collective-permute-start.3 = (bf16[32,128,96]{1,2,0:T(8,128)(2,1)}, bf16[32,128,96]{1,2,0:T(8,128)(2,1)S(1)}, u32[]{:S(2)}, u32[]{:S(2)}) collective-permute-start(bf16[32,128,96]{1,2,0:T(8,128)(2,1)} %copy.30), channel_id=1, source_target_pairs={{0,16},{16,0},{1,17},{17,1},{2,18},{18,2},{3,19},{19,3},{4,20},{20... | collective-permute-start | bytes 2359304 | tf_op jit(solution)/shard_map/ppermute | solution.py:154
  241.2 32.4 %collective-permute-start.2 = (bf16[96,64]{0,1:T(8,128)(2,1)S(1)}, bf16[96,64]{0,1:T(8,128)(2,1)S(1)}, u32[]{:S(2)}, u32[]{:S(2)}) collective-permute-start(bf16[96,64]{0,1:T(8,128)(2,1)S(1)} %get-tuple-element.12), channel_id=1, source_target_pairs={{0,16},{16,0},{1,17},{17,1},{2,18},{18,2},{3,19},{19,3},{4,20},{20... | collective-permute-start | bytes 36872 | tf_op jit(solution)/shard_map/ppermute | solution.py:154
  262.3 10.0 %all-to-all-start.3 = ((bf16[16,16,128]{2,1,0:T(8,128)(2,1)}), bf16[16,16,128]{2,1,0:T(8,128)(2,1)S(1)}, u32[]{:S(2)}, u32[]{:S(2)}) async-start(bf16[16,16,128]{2,1,0:T(8,128)(2,1)} %bitcast.9), calls=%async_computation.3 | async-start | bytes 131072 | tf_op jit(solution)/shard_map/all_to_all | solution.py:202
Sparse Core Ops, SparseCore 0:
  59.0 134.5 all-gather.4

commit v2 on v1

v2 whole, which is shorter than its diff:
```python
import functools

import jax
import jax.numpy as jnp
from jax import lax
from jax.experimental import pallas as pl
from jax.experimental.pallas import tpu as pltpu
from jax.sharding import Mesh
from jax.sharding import PartitionSpec as P

BF16 = jnp.bfloat16
F32 = jnp.float32
CAP = 3
HALF = 64
LANES = 128
NT = (((1,), (1,)), ((), ()))
VMEM = pl.BlockSpec(memory_space=pltpu.VMEM)
SMEM = pl.BlockSpec(memory_space=pltpu.SMEM)


def call(body, outs, ins, scratch=()):
    return pl.pallas_call(
        body,
        out_shape=outs,
        in_specs=ins,
        out_specs=jax.tree.map(lambda _: VMEM, outs),
        scratch_shapes=list(scratch),
        compiler_params=pltpu.CompilerParams(vmem_limit_bytes=40 * 1024 * 1024),
    )


def struct(*shape, dtype=BF16):
    return jax.ShapeDtypeStruct(shape, dtype)


def iota(shape, dim):
    return lax.broadcasted_iota(jnp.int32, shape, dim)


def weave(first, second):
    low = iota(first.shape, 1) < HALF
    return (
        jnp.where(low, first, pltpu.roll(second, HALF, 1)),
        jnp.where(low, pltpu.roll(first, HALF, 1), second),
    )


def relative(place_ref, x):
    parity, core = place_ref[0], place_ref[1]
    near = jnp.where(parity == 0, x[:, :LANES], x[:, LANES:])
    far = jnp.where(parity == 0, x[:, LANES:], x[:, :LANES])
    return [jnp.where(core == 0, y, pltpu.roll(y, HALF, 1)) for y in (near, far)]


def pick_body(picked_ref, counts_ref, weights_ref, tokens_ref, grads_ref, out_ref, wide_in, wide_out, rows):
    wide_in[...] = tokens_ref[...].astype(F32)
    wide_out[...] = grads_ref[...].astype(F32)
    rows[...] = jnp.zeros_like(rows)
    for expert in range(out_ref.shape[0]):
        for c in range(CAP):
            token = picked_ref[c, expert]
            scale = jnp.where(c < counts_ref[0, expert], weights_ref[c, expert], 0.0)
            rows[pl.ds(8 * expert + c, 1), :] = wide_out[pl.ds(token, 1), :] * scale
            rows[pl.ds(8 * expert + 4 + c, 1), :] = wide_in[pl.ds(token, 1), :]
    out_ref[...] = rows[...].reshape(out_ref.shape).astype(BF16)


def weight_body(place_ref, down_ref, gate_ref, up_ref, keep_ref, give_ref):
    half = down_ref.shape[1] // 2
    parity = place_ref[0]
    for side, out_ref in ((parity, keep_ref), (1 - parity, give_ref)):
        for k in range(half // LANES):
            columns = pl.ds(pl.multiple_of(side * half + k * LANES, LANES), LANES)
            out_ref[:, k * LANES : (k + 1) * LANES] = down_ref[:, columns]
            one, two = weave(gate_ref[:, columns].astype(F32), up_ref[:, columns].astype(F32))
            start = half + 2 * k * LANES
            out_ref[:, start : start + LANES] = one.astype(BF16)
            out_ref[:, start + LANES : start + 2 * LANES] = two.astype(BF16)


def send_body(blocks_ref, gate_ref, up_ref, out_ref):
    half = gate_ref.shape[1] // 2
    pairs = blocks_ref.shape[0]
    row = iota((8, 2 * LANES), 0)
    for side in range(2):
        for k in range(pairs // 2):
            columns = slice(side * half + k * LANES, side * half + (k + 1) * LANES)
            woven = weave(gate_ref[:, columns].astype(F32), up_ref[:, columns].astype(F32))
            for pair, saved in zip((2 * k, 2 * k + 1), woven):
                early = jnp.concatenate([saved[0:1], saved[1:2]], axis=1)
                late = jnp.concatenate([saved[2:3], saved[2:3]], axis=1)
                block = blocks_ref[pair].astype(F32)
                block = jnp.where(row == 3, early, jnp.where(row == 7, late, block))
                out_ref[2 * pair + side] = block.astype(BF16)


def partial_body(place_ref, rows_ref, own_ref, pair_ref, other_ref, out_ref, saved_ref, keep_ref, give_ref):
    total = rows_ref.shape[0]
    chips = total // 8
    half = own_ref.shape[1]
    row, column = iota((total, total), 0), iota((total, total), 1)
    order = (row % chips == column // 8) & (row // chips == column % 8)
    rows = jnp.dot(order.astype(BF16), rows_ref[...], preferred_element_type=F32)
    slots = CAP * chips
    sent_near, sent_far = relative(place_ref, rows[:slots])
    in_near, _ = relative(place_ref, rows[4 * chips : 4 * chips + slots])
    saved_ref[...] = jnp.concatenate(
        [rows[slots : 4 * chips, :LANES], rows[slots : 4 * chips, LANES:], rows[7 * chips :, :LANES]]
    ).astype(BF16)
    keep, give = weave(sent_near, in_near)
    keep_ref[...] = keep.astype(BF16)
    give_ref[...] = give.astype(BF16)
    sent = jnp.concatenate([sent_near, sent_far], axis=1).astype(BF16)
    down = jnp.concatenate([own_ref[...], other_ref[:HALF], pair_ref[...], other_ref[HALF:]])
    product = jnp.dot(sent, down, preferred_element_type=F32)
    for k in range(half // LANES):
        block = product[:, k * LANES : (k + 1) * LANES]
        one, two = weave(block[: slots // 2], block[slots // 2 :])
        out_ref[2 * k] = one.astype(BF16)
        out_ref[2 * k + 1] = two.astype(BF16)


def hidden_body(parts_ref, saved_ref, out_ref):
    folded = jnp.sum(parts_ref[...].astype(F32), axis=0)
    hidden = jnp.concatenate([folded, pltpu.roll(folded, HALF, 1)])
    hidden = hidden.astype(BF16).astype(F32)
    a = saved_ref[...].astype(F32)
    b = pltpu.roll(a, HALF, 1)
    q = jax.nn.sigmoid(a)
    gate_grad = hidden * b * q * (1.0 + a * (1.0 - q))
    up_grad = hidden * a * q
    activated = a * q * b
    slots = hidden.shape[0]
    out_ref[0, :slots, :] = weave(gate_grad, up_grad)[0].astype(BF16)
    out_ref[0, slots:, :] = weave(activated[: slots // 2], activated[slots // 2 :])[0].astype(BF16)


def slot_body(grads_ref, own_ref, pair_ref, other_ref, out_ref):
    slots = grads_ref.shape[1] * 2 // 3
    chips = out_ref.shape[0]
    half = own_ref.shape[1] // 3
    grads = jnp.concatenate([grads_ref[m, :slots, :] for m in range(grads_ref.shape[0])], axis=1)
    row, slot = iota((8 * chips, slots), 0), iota((8 * chips, slots), 1)
    total = None
    for side, ref, rows in ((0, own_ref, slice(0, HALF)), (1, pair_ref, slice(HALF, LANES))):
        weights = jnp.concatenate([ref[:, half:], other_ref[rows, half:]])
        part = lax.dot_general(grads, weights, NT, preferred_element_type=F32).astype(BF16)
        place = (slot % chips == row // 8) & (row % 8 == 4 * side + slot // chips)
        placed = jnp.dot(place.astype(BF16), part, preferred_element_type=F32)
        total = placed if total is None else total + placed
    out_ref[...] = total.astype(BF16).reshape(out_ref.shape)


def grad_body(place_ref, keep_ref, got_ref, own_ref, pair_ref, other_ref, gate_ref, up_ref, down_ref):
    parity = place_ref[0]
    members = own_ref.shape[0]
    slots = keep_ref.shape[0]
    half = members * HALF
    lefts = [ref[...].astype(F32).T.astype(BF16) for ref in (keep_ref, got_ref)]
    for side, first, second in ((parity, own_ref, other_ref.at[:members]), (1 - parity, pair_ref, other_ref.at[members:])):
        for k in range(members // 2):
            columns = pl.ds(pl.multiple_of(side * half + k * LANES, LANES), LANES)
            both, down = [0.0, 0.0], 0.0
            for left, ref in zip(lefts, (first, second)):
                acts = weave(ref[2 * k, slots:, :].astype(F32), ref[2 * k + 1, slots:, :].astype(F32))
                acts = jnp.concatenate(acts).astype(BF16)
                down = down + jnp.dot(left[:HALF], acts, preferred_element_type=F32)
                for j in range(2):
                    grads = ref[2 * k + j, :slots, :]
                    both[j] = both[j] + jnp.dot(left[HALF:], grads, preferred_element_type=F32)
            gate, up = weave(*both)
            gate_ref[:, columns] = gate
            up_ref[:, columns] = up
            down_ref[:, columns] = down


def token_body(place_ref, index_ref, rows_ref, out_ref):
    tokens = iota((out_ref.shape[0], index_ref.shape[1]), 0)
    for half in range(2):
        owner = (tokens == index_ref[half : half + 1, :]).astype(BF16)
        total = jnp.dot(owner, rows_ref[...], preferred_element_type=F32)
        total = jnp.where(place_ref[1] == 0, total, pltpu.roll(total, HALF, 1))
        out_ref[:, half * LANES : (half + 1) * LANES] = total.astype(BF16)


def swap(x, axis):
    return lax.ppermute(x, axis, [(0, 1), (1, 0)])


def spread(x, axis):
    return lax.all_to_all(x, axis, split_axis=0, concat_axis=0, tiled=True)


def local(pairs, tokens, grad_out, picked, pick_counts, router_weights, saved_gate, saved_up, w_gate, w_up, w_down):
    chips = 2 * pairs
    experts = picked.shape[1]
    token_count, width = tokens.shape
    hidden = w_gate.shape[2]
    slots = CAP * chips
    z = ("m", "p")
    place = jnp.stack([lax.axis_index("p"), lax.axis_index("core")]).astype(jnp.int32)

    outgoing = call(
        pick_body,
        struct(experts, 8, width),
        [SMEM] * 3 + [VMEM] * 2,
        scratch=(
            pltpu.VMEM((token_count, width), F32),
            pltpu.VMEM((token_count, width), F32),
            pltpu.VMEM((8 * experts, width), F32),
        ),
    )(picked[0].T, pick_counts, router_weights[0].T, tokens, grad_out)
    blocks = spread(outgoing, "expert")

    w_keep, w_give = call(weight_body, (struct(HALF, 3 * hidden // 2),) * 2, [SMEM] + [VMEM] * 3)(
        place, w_down[0].T, w_gate[0], w_up[0]
    )
    w_pair = swap(w_give, "p")
    w_other = swap(jnp.concatenate([w_keep, w_pair]), "core")

    rows = call(send_body, struct(chips, 8, width), [VMEM] * 3)(blocks, saved_gate[0], saved_up[0])
    rows = spread(rows, z)
    half = hidden // 2
    parts, saved, keep, give = call(
        partial_body,
        (struct(pairs, slots // 2, LANES),) + (struct(slots, LANES),) * 3,
        [SMEM] + [VMEM] * 4,
    )(place, rows.reshape(8 * chips, width), w_keep[:, :half], w_pair[:, :half], w_other[:, :half])
    got = swap(give, "core")
    parts = spread(parts, "m")
    grads = call(hidden_body, struct(1, 3 * slots // 2, LANES), [VMEM] * 2)(parts, saved)
    grads = lax.all_gather(grads, "m", axis=0, tiled=True)

    back = call(slot_body, struct(chips, 8, LANES), [VMEM] * 4)(grads, w_keep, w_pair, w_other)
    back = spread(back, z)
    back = spread(back.reshape(experts, 16, LANES), "expert")

    lane = jnp.arange(16 * experts, dtype=jnp.int32)
    index = jnp.pad(picked[0], ((0, 0), (0, 1)), constant_values=-1)
    index = jnp.tile(index, (1, 4)).reshape(1, -1)
    far = (lane // 8 % 2) ^ (lane // 4 % 2)
    index = jnp.where(far[None, :] == jnp.arange(2)[:, None], index, -1)
    token_grad = call(token_body, struct(token_count, width), [SMEM] + [VMEM] * 2)(
        place, index, back.reshape(16 * experts, LANES)
    )

    grads_pair = swap(grads, "p")
    grads_other = swap(jnp.concatenate([grads, grads_pair]), "core")
    gate_grad, up_grad, down_grad = call(
        grad_body, (struct(HALF, hidden, dtype=F32),) * 3, [SMEM] + [VMEM] * 5
    )(place, keep, got, grads, grads_pair, grads_other)
    return (token_grad, gate_grad[None], up_grad[None], down_grad.T[None])


def solution(mesh):
    pairs = mesh.shape["dp"] // 4
    fine = Mesh(mesh.devices.reshape(pairs, 2, 2, mesh.shape["expert"]), ("m", "p", "core", "expert"))
    dp = ("m", "p", "core")
    placed = (
        P(dp, "expert"),
        P(dp, "expert"),
        P(dp, None, None),
        P(dp, None),
        P(dp, None, None),
        P("expert", dp, None),
        P("expert", dp, None),
        P("expert", dp, None),
        P("expert", dp, None),
        P("expert", None, dp),
    )
    return jax.shard_map(
        functools.partial(local, pairs),
        mesh=fine,
        in_specs=placed,
        out_specs=(
            P(dp, "expert"),
            P("expert", dp, None),
            P("expert", dp, None),
            P("expert", None, dp),
        ),
        check_vma=False,
    )
```

time: 284 us -> 229 us (0.81)
  starting transfers between devices: 108 us -> 70.8 us
  blocking collectives: 93.1 us -> 78.6 us
  between operations: 14.4 us -> 0.78 us
  waiting for transfers between devices: 46.7 us -> 58.2 us
  local copies, waits for them, and re-layouts: 11.6 us -> 8.07 us
    all_gather x2 -> x1, blocking collectives: 93.1 us -> 36.6 us  [local(): grads = lax.all_gather(grads, 'm', axis=0, tiled=True)]
    all_to_all x0 -> x2, blocking collectives: none -> 42 us  [spread(): return lax.all_to_all(x, axis, split_axis=0, concat_axis=0, tiled=True)]
    ppermute x5, starting transfers between devices: 59.8 us -> 29.1 us  [swap(): return lax.ppermute(x, axis, [(0, 1), (1, 0)])]
    ppermute x5, waiting for transfers between devices: 0.01 us -> 9.85 us  [swap(): return lax.ppermute(x, axis, [(0, 1), (1, 0)])]
    all_to_all x4 -> x3, starting transfers between devices: 48.4 us -> 41.7 us  [spread(): return lax.all_to_all(x, axis, split_axis=0, concat_axis=0, tiled=True)]
    all_to_all x4 -> x3, waiting for transfers between devices: 46.6 us -> 48.3 us  [spread(): return lax.all_to_all(x, axis, split_axis=0, concat_axis=0, tiled=True)]
    pallas_call x9 -> x7, Pallas kernels: 7.47 us -> 8.92 us  [the longest x1 3.34 us: local(): call(grad_body, (struct(HALF, hidden, dtype=F32),) * 3, [SMEM] + [VMEM] * 5)]
    unnamed x28 -> x19, local copies, waits for them, and re-layouts: 6.73 us -> 7.9 us
  transfers between devices with their start and end apart: 10 -> 8, of which waited for: 3 -> 5; matrix products, arithmetic and copies ran while one was open for 3% -> 1% of each run, Pallas kernels for 2% -> 2%
where the time goes in v2:
time: 229 us; the launch traced here: 227 us
  blocking collectives  78.6 us (34%)
  starting transfers between devices  70.8 us (31%)
  waiting for transfers between devices  58.2 us (25%)
  Pallas kernels  9.68 us (4%)
  local copies, waits for them, and re-layouts  8.07 us (4%)
    all_to_all x3, waiting for transfers between devices, spread(): return lax.all_to_all(x, axis, split_axis=0, concat_axis=0, tiled=True)  48.3 us
    all_to_all x2, blocking collectives, spread(): return lax.all_to_all(x, axis, split_axis=0, concat_axis=0, tiled=True)  42 us
    all_to_all x3, starting transfers between devices, spread(): return lax.all_to_all(x, axis, split_axis=0, concat_axis=0, tiled=True)  41.7 us
    all_gather x1, blocking collectives, local(): grads = lax.all_gather(grads, 'm', axis=0, tiled=True)  36.6 us
    ppermute x5, starting transfers between devices, swap(): return lax.ppermute(x, axis, [(0, 1), (1, 0)])  29.1 us
    ppermute x5, waiting for transfers between devices, swap(): return lax.ppermute(x, axis, [(0, 1), (1, 0)])  9.85 us
    unnamed x19, local copies, waits for them, and re-layouts  7.9 us
  transfers between devices with their start and end apart: 8, of which 5 were waited for; matrix products, arithmetic and copies ran while one was open for 1% of the time, Pallas kernels for 2%

profile of v2, /device:TPU:1, one launch (start us, length us, event | category | flops | bytes accessed | tf_op | source)
XLA Modules:
  0.0 227.4 jit_solution(11696993122423238023)
XLA Ops:
  0.6 0.1 pad_add_fusion.place_ref
  0.7 0.0 copy-start
  0.7 0.9 copy-done
  1.7 0.0 copy-start.1
  1.7 0.9 copy-done.1
  2.6 0.0 copy-start.2
  2.6 0.9 copy-done.2
  3.6 0.9 shard_map.131
  4.4 4.4 %collective-permute-start = (bf16[64,3072]{1,0:T(8,128)(2,1)S(1)}, bf16[64,3072]{1,0:T(8,128)(2,1)S(1)}, u32[]{:S(2)}, u32[]{:S(2)}) collective-permute-start(bf16[64,3072]{1,0:T(8,128)(2,1)S(1)} %get-tuple-element.14), channel_id=1, source_target_pairs={{0,32},{32,0},{1,33},{33,1},{2,34},{34,2},{3,35},{35,3},{4,36},{36... | collective-permute-start | bytes 1179656 | tf_op jit(solution)/shard_map/ppermute | solution.py:187
  8.8 0.7 copy.23
  9.5 0.7 copy.24
  10.2 0.0 copy-start.3
  10.2 0.8 copy-done.3
  10.9 0.0 copy-start.4
  10.9 0.8 copy-done.4
  11.7 0.0 copy-start.7
  11.7 0.7 copy-done.7
  12.4 0.8 shard_map.129
  13.1 13.1 %all_to_all.25.blocks_ref = bf16[16,8,256]{2,1,0:T(8,128)(2,1)S(1)} all-to-all(bf16[16,8,256]{2,1,0:T(8,128)(2,1)S(1)} %shard_map.129), channel_id=1, replica_groups=mesh['m'=16,'p'=2,'core'=2,'expert'=16] {'expert'}, dimensions={0} | all-to-all | bytes 131072 | tf_op jit(solution)/shard_map/all_to_all | solution.py:191
  26.2 0.0 copy-start.5
  26.2 0.7 copy-done.5
  26.9 0.0 copy-start.6
  26.9 0.7 copy-done.6
  27.6 0.8 shard_map.130
  28.4 27.6 %all-to-all-start.1 = ((bf16[32,8,256]{2,1,0:T(8,128)(2,1)}), bf16[32,8,256]{2,1,0:T(8,128)(2,1)S(1)}, u32[]{:S(2)}, u32[]{:S(2)}) async-start(bf16[32,8,256]{2,1,0:T(8,128)(2,1)} %shard_map.130), calls=%async_computation.1 | async-start | bytes 262144 | tf_op jit(solution)/shard_map/all_to_all | solution.py:191
  56.0 0.0 collective-permute-done.pair_ref
  56.0 0.1 pad_maximum_fusion.1
  56.0 4.6 %collective-permute-start.1 = (bf16[128,3072]{1,0:T(8,128)(2,1)S(1)}, bf16[128,3072]{1,0:T(8,128)(2,1)S(1)}, u32[]{:S(2)}, u32[]{:S(2)}) collective-permute-start(bf16[128,3072]{1,0:T(8,128)(2,1)S(1)} %pad_maximum_fusion.1), channel_id=1, source_target_pairs={{0,16},{16,0},{1,17},{17,1},{2,18},{18,2},{3,19},{19,3},{4,20},{20... | collective-permute-start | bytes 2359304 | tf_op jit(solution)/shard_map/ppermute | solution.py:187
  60.7 1.9 collective-permute-done.1.other_ref
  62.5 19.4 %all-to-all-done.1 = bf16[32,8,256]{2,1,0:T(8,128)(2,1)S(1)} async-done(((bf16[32,8,256]{2,1,0:T(8,128)(2,1)}), bf16[32,8,256]{2,1,0:T(8,128)(2,1)S(1)}, u32[]{:S(2)}, u32[]{:S(2)}) %all-to-all-start.1) | async-done | bytes 131104 | tf_op jit(solution)/shard_map/all_to_all | solution.py:191
  82.0 1.1 shard_map.132
  83.0 28.9 %all_to_all.26.parts_ref = bf16[16,48,128]{2,1,0:T(8,128)(2,1)S(1)} all-to-all(bf16[16,48,128]{2,1,0:T(8,128)(2,1)S(1)} %get-tuple-element.15), channel_id=1, replica_groups=mesh['m'=16,'p'=2,'core'=2,'expert'=16] {'m'}, dimensions={0} | all-to-all | bytes 393216 | tf_op jit(solution)/shard_map/all_to_all | solution.py:191
  111.9 0.2 shard_map.133
  112.1 36.6 %all_gather.3.grads_ref.own_ref = bf16[16,144,128]{2,1,0:T(8,128)(2,1)S(1)} all-gather(bf16[1,144,128]{2,1,0:T(8,128)(2,1)S(1)} %shard_map.133), channel_id=1, replica_groups=mesh['m'=16,'p'=2,'core'=2,'expert'=16] {'m'}, dimensions={0}, use_global_device_ids=true | all-gather | bytes 626688 | tf_op jit(solution)/shard_map/all_gather | solution.py:232
  148.7 4.9 %collective-permute-start.3 = (bf16[16,144,128]{2,1,0:T(8,128)(2,1)S(1)}, bf16[16,144,128]{2,1,0:T(8,128)(2,1)S(1)}, u32[]{:S(2)}, u32[]{:S(2)}) collective-permute-start(bf16[16,144,128]{2,1,0:T(8,128)(2,1)S(1)} %all_gather.3.grads_ref.own_ref), channel_id=1, source_target_pairs={{0,32},{32,0},{1,33},{33,1},{2,34},{34,2},{3,35},{35,3},{4,36},{36... | collective-permute-start | bytes 1769480 | tf_op jit(solution)/shard_map/ppermute | solution.py:187
  153.6 8.0 %collective-permute-done.3.pair_ref = bf16[16,144,128]{2,1,0:T(8,128)(2,1)S(1)} collective-permute-done((bf16[16,144,128]{2,1,0:T(8,128)(2,1)S(1)}, bf16[16,144,128]{2,1,0:T(8,128)(2,1)S(1)}, u32[]{:S(2)}, u32[]{:S(2)}) %collective-permute-start.3) | collective-permute-done | bytes 589856 | tf_op jit(solution)/shard_map/ppermute | solution.py:187
  161.6 1.1 pad_maximum_fusion
  162.8 13.1 %collective-permute-start.4 = (bf16[32,144,128]{2,1,0:T(8,128)(2,1)}, bf16[32,144,128]{2,1,0:T(8,128)(2,1)}, u32[]{:S(2)}, u32[]{:S(2)}) collective-permute-start(bf16[32,144,128]{2,1,0:T(8,128)(2,1)} %pad_maximum_fusion), channel_id=1, source_target_pairs={{0,16},{16,0},{1,17},{17,1},{2,18},{18,2},{3,19},{19,3},{4,20},{20... | collective-permute-start | bytes 3538952 | tf_op jit(solution)/shard_map/ppermute | solution.py:187
  175.8 1.3 shard_map.134
  177.1 9.4 %all-to-all-start.3 = ((bf16[32,8,128]{2,1,0:T(8,128)(2,1)}), bf16[32,8,128]{2,1,0:T(8,128)(2,1)}, u32[]{:S(2)}, u32[]{:S(2)}) async-start(bf16[32,8,128]{2,1,0:T(8,128)(2,1)} %shard_map.134), calls=%async_computation.3 | async-start | bytes 131072 | tf_op jit(solution)/shard_map/all_to_all | solution.py:191
  186.6 0.1 copy.19
  186.7 0.1 tile.9
  186.8 2.2 collective-permute-start.2
  189.0 22.3 %all-to-all-done.3 = bf16[32,8,128]{2,1,0:T(8,128)(2,1)} async-done(((bf16[32,8,128]{2,1,0:T(8,128)(2,1)}), bf16[32,8,128]{2,1,0:T(8,128)(2,1)}, u32[]{:S(2)}, u32[]{:S(2)}) %all-to-all-start.3) | async-done | bytes 65568 | tf_op jit(solution)/shard_map/all_to_all | solution.py:191
  211.4 4.7 %all-to-all-start.4 = ((bf16[16,16,128]{2,1,0:T(8,128)(2,1)}), bf16[16,16,128]{2,1,0:T(8,128)(2,1)S(1)}, u32[]{:S(2)}, u32[]{:S(2)}) async-start(bf16[16,16,128]{2,1,0:T(8,128)(2,1)} %bitcast.11), calls=%async_computation.4 | async-start | bytes 131072 | tf_op jit(solution)/shard_map/all_to_all | solution.py:191
  216.1 6.5 %all-to-all-done.4 = bf16[16,16,128]{2,1,0:T(8,128)(2,1)S(1)} async-done(((bf16[16,16,128]{2,1,0:T(8,128)(2,1)}), bf16[16,16,128]{2,1,0:T(8,128)(2,1)S(1)}, u32[]{:S(2)}, u32[]{:S(2)}) %all-to-all-start.4) | async-done | bytes 65568 | tf_op jit(solution)/shard_map/all_to_all | solution.py:191
  222.7 1.4 shard_map.135
  224.1 0.0 collective-permute-done.2.got_ref
  224.1 0.0 collective-permute-done.4.other_ref
  224.1 3.3 %shard_map.136 = (f32[64,2048]{1,0:T(8,128)}, f32[64,2048]{1,0:T(8,128)}, f32[64,2048]{1,0:T(8,128)}) custom-call(s32[2]{0:T(128)S(1)} %pad_add_fusion.place_ref, bf16[96,128]{1,0:T(8,128)(2,1)S(1)} %get-tuple-element.17.keep_ref, bf16[96,128]{1,0:T(8,128)(2,1)S(1)} %collective-permute-done.2.got_ref, bf16[16,144,128]{2,1,0:T(8,128)(2,1)S(1)} %all_gather.3.grads_ref.own_ref, ...), custom_call_target="tpu_custom_call" | custom-call | tf_op jit(solution)/shard_map/pallas_call | solution.py:249
  (7 shorter events, 0.1 us)
Async XLA Ops:
  0.7 1.0 copy-start
  1.7 0.9 copy-start.1
  2.6 0.9 copy-start.2
  4.4 51.5 %collective-permute-start = (bf16[64,3072]{1,0:T(8,128)(2,1)S(1)}, bf16[64,3072]{1,0:T(8,128)(2,1)S(1)}, u32[]{:S(2)}, u32[]{:S(2)}) collective-permute-start(bf16[64,3072]{1,0:T(8,128)(2,1)S(1)} %get-tuple-element.14), channel_id=1, source_target_pairs={{0,32},{32,0},{1,33},{33,1},{2,34},{34,2},{3,35},{35,3},{4,36},{36... | collective-permute-start | bytes 1179656 | tf_op jit(solution)/shard_map/ppermute | solution.py:187
  10.2 0.8 copy-start.3
  10.9 0.8 copy-start.4
  11.7 0.7 copy-start.7
  26.2 0.7 copy-start.5
  26.9 0.7 copy-start.6
  28.4 53.6 %all-to-all-start.1 = ((bf16[32,8,256]{2,1,0:T(8,128)(2,1)}), bf16[32,8,256]{2,1,0:T(8,128)(2,1)S(1)}, u32[]{:S(2)}, u32[]{:S(2)}) async-start(bf16[32,8,256]{2,1,0:T(8,128)(2,1)} %shard_map.130), calls=%async_computation.1 | async-start | bytes 262144 | tf_op jit(solution)/shard_map/all_to_all | solution.py:191
  56.0 6.5 %collective-permute-start.1 = (bf16[128,3072]{1,0:T(8,128)(2,1)S(1)}, bf16[128,3072]{1,0:T(8,128)(2,1)S(1)}, u32[]{:S(2)}, u32[]{:S(2)}) collective-permute-start(bf16[128,3072]{1,0:T(8,128)(2,1)S(1)} %pad_maximum_fusion.1), channel_id=1, source_target_pairs={{0,16},{16,0},{1,17},{17,1},{2,18},{18,2},{3,19},{19,3},{4,20},{20... | collective-permute-start | bytes 2359304 | tf_op jit(solution)/shard_map/ppermute | solution.py:187
  148.7 12.9 %collective-permute-start.3 = (bf16[16,144,128]{2,1,0:T(8,128)(2,1)S(1)}, bf16[16,144,128]{2,1,0:T(8,128)(2,1)S(1)}, u32[]{:S(2)}, u32[]{:S(2)}) collective-permute-start(bf16[16,144,128]{2,1,0:T(8,128)(2,1)S(1)} %all_gather.3.grads_ref.own_ref), channel_id=1, source_target_pairs={{0,32},{32,0},{1,33},{33,1},{2,34},{34,2},{3,35},{35,3},{4,36},{36... | collective-permute-start | bytes 1769480 | tf_op jit(solution)/shard_map/ppermute | solution.py:187
  162.8 61.3 %collective-permute-start.4 = (bf16[32,144,128]{2,1,0:T(8,128)(2,1)}, bf16[32,144,128]{2,1,0:T(8,128)(2,1)}, u32[]{:S(2)}, u32[]{:S(2)}) collective-permute-start(bf16[32,144,128]{2,1,0:T(8,128)(2,1)} %pad_maximum_fusion), channel_id=1, source_target_pairs={{0,16},{16,0},{1,17},{17,1},{2,18},{18,2},{3,19},{19,3},{4,20},{20... | collective-permute-start | bytes 3538952 | tf_op jit(solution)/shard_map/ppermute | solution.py:187
  177.1 34.2 %all-to-all-start.3 = ((bf16[32,8,128]{2,1,0:T(8,128)(2,1)}), bf16[32,8,128]{2,1,0:T(8,128)(2,1)}, u32[]{:S(2)}, u32[]{:S(2)}) async-start(bf16[32,8,128]{2,1,0:T(8,128)(2,1)} %shard_map.134), calls=%async_computation.3 | async-start | bytes 131072 | tf_op jit(solution)/shard_map/all_to_all | solution.py:191
  186.8 37.2 %collective-permute-start.2 = (bf16[96,128]{1,0:T(8,128)(2,1)S(1)}, bf16[96,128]{1,0:T(8,128)(2,1)S(1)}, u32[]{:S(2)}, u32[]{:S(2)}) collective-permute-start(bf16[96,128]{1,0:T(8,128)(2,1)S(1)} %get-tuple-element.18), channel_id=1, source_target_pairs={{0,16},{16,0},{1,17},{17,1},{2,18},{18,2},{3,19},{19,3},{4,20},{20... | collective-permute-start | bytes 73736 | tf_op jit(solution)/shard_map/ppermute | solution.py:187
  211.4 11.3 %all-to-all-start.4 = ((bf16[16,16,128]{2,1,0:T(8,128)(2,1)}), bf16[16,16,128]{2,1,0:T(8,128)(2,1)S(1)}, u32[]{:S(2)}, u32[]{:S(2)}) async-start(bf16[16,16,128]{2,1,0:T(8,128)(2,1)} %bitcast.11), calls=%async_computation.4 | async-start | bytes 131072 | tf_op jit(solution)/shard_map/all_to_all | solution.py:191

commit v3 on v0

v3 whole, which is shorter than its diff:
```python
import functools

import jax
import jax.numpy as jnp
from jax import lax
from jax.experimental import pallas as pl
from jax.experimental.pallas import tpu as pltpu
from jax.sharding import Mesh
from jax.sharding import PartitionSpec as P

BF16 = jnp.bfloat16
F32 = jnp.float32
CAP = 3
HALF = 64
LANES = 128
NT = (((1,), (1,)), ((), ()))
TN = (((0,), (0,)), ((), ()))
VMEM = pl.BlockSpec(memory_space=pltpu.VMEM)
SMEM = pl.BlockSpec(memory_space=pltpu.SMEM)
ANY = pl.BlockSpec(memory_space=pl.ANY)
FETCH = pl.BlockSpec()


def call(body, outs, ins, out_specs=None, scratch=(), limit=40):
    return pl.pallas_call(
        body,
        out_shape=outs,
        in_specs=ins,
        out_specs=jax.tree.map(lambda _: VMEM, outs) if out_specs is None else out_specs,
        scratch_shapes=list(scratch),
        compiler_params=pltpu.CompilerParams(vmem_limit_bytes=limit * 1024 * 1024),
    )


def struct(*shape, dtype=BF16):
    return jax.ShapeDtypeStruct(shape, dtype)


def iota(shape, dim):
    return lax.broadcasted_iota(jnp.int32, shape, dim)


def matmul(left, right, dims=(((1,), (0,)), ((), ()))):
    return lax.dot_general(left, right, dims, preferred_element_type=F32)


def ordered(x, groups):
    total = x.shape[0]
    each = total // groups
    row, column = iota((total, total), 0), iota((total, total), 1)
    order = (row % groups == column // each) & (row // groups == column % each)
    return matmul(order.astype(BF16), x)


def pick_body(picked_ref, counts_ref, weights_ref, tokens_ref, grads_ref, gate_ref, up_ref, out_ref, saved_ref, rows):
    blank = jnp.zeros((4 - CAP, LANES), F32)
    for k in range(saved_ref.shape[0]):
        columns = slice(k * LANES, (k + 1) * LANES)
        parts = [gate_ref[:, columns].astype(F32), blank, up_ref[:, columns].astype(F32), blank]
        saved_ref[k] = jnp.concatenate(parts).astype(BF16)
    experts = out_ref.shape[0]
    diagonal = iota((experts, experts), 0) == iota((experts, experts), 1)
    rows[...] = jnp.zeros_like(rows)
    for c in range(CAP):
        chosen = (iota((tokens_ref.shape[0], experts), 0) == picked_ref[c]).astype(BF16)
        scale = jnp.where(c < counts_ref[...], weights_ref[c], 0.0)
        scale = jnp.sum(jnp.where(diagonal, scale, 0.0), axis=1, keepdims=True)
        sent = matmul(chosen, grads_ref[...], TN) * scale
        taken = matmul(chosen, tokens_ref[...], TN)
        for row, value in ((c, sent), (4 + c, taken)):
            for j in range(rows.shape[0]):
                rows[j, pl.ds(row, experts, stride=8), :] = value[:, j * LANES : (j + 1) * LANES]
    for j in range(rows.shape[0]):
        out_ref[:, :, j * LANES : (j + 1) * LANES] = rows[j].reshape(experts, 8, LANES).astype(BF16)


def send_body(blocks_ref, saved_ref, out_ref):
    for j in range(2):
        out_ref[:, 8 * j : 8 * j + 8, :] = blocks_ref[:, :, j * LANES : (j + 1) * LANES]
    out_ref[:, 16:, :] = saved_ref[...]


def partial_body(place_ref, rows_ref, own_ref, pair_ref, core_ref, out_ref, saved_ref, inner_ref, outer_ref):
    parity, core = place_ref[0], place_ref[1]
    pairs = out_ref.shape[0]
    slots = CAP * pairs
    rows = ordered(rows_ref[...], pairs)
    piece = lambda k: rows[k * pairs : k * pairs + slots]
    saved_ref[0] = piece(16).astype(BF16)
    saved_ref[1] = piece(20).astype(BF16)
    low = iota((slots, LANES), 1) < HALF
    turn = lambda x: jnp.where(core == 0, x, pltpu.roll(x, HALF, 1))
    product = 0.0
    for side, mine_ref, out in ((0, own_ref, inner_ref), (1, pair_ref, outer_ref)):
        here = parity == side
        sent = turn(jnp.where(here, piece(0), piece(8)))
        taken = turn(jnp.where(here, piece(4), piece(12)))
        product = product + matmul(sent.astype(BF16), jnp.concatenate([mine_ref[0], core_ref[side, 0]]))
        out[0] = jnp.where(low, sent, pltpu.roll(taken, HALF, 1)).astype(BF16)
        out[1] = jnp.where(low, pltpu.roll(sent, HALF, 1), taken).astype(BF16)
    for k in range(pairs):
        out_ref[k] = product[:, k * LANES : (k + 1) * LANES].astype(BF16)


def hidden_body(parts_ref, saved_ref, out_ref):
    slots = parts_ref.shape[1]
    hidden = jnp.sum(parts_ref[...].astype(F32), axis=0).astype(BF16).astype(F32)
    a, b = saved_ref[0].astype(F32), saved_ref[1].astype(F32)
    q = jax.nn.sigmoid(a)
    out_ref[0, :slots, :] = (hidden * b * q * (1.0 + a * (1.0 - q))).astype(BF16)
    out_ref[0, slots : 2 * slots, :] = (hidden * a * q).astype(BF16)
    out_ref[0, 2 * slots :, :] = (a * q * b).astype(BF16)


def slot_body(grads_ref, outer_ref, own_ref, pair_ref, core_ref, out_ref, packed_ref):
    pairs = grads_ref.shape[0]
    packed_ref[: -2 * CAP * pairs, :] = grads_ref[...].reshape(-1, LANES)
    packed_ref[-2 * CAP * pairs :, :] = outer_ref[...].reshape(-1, LANES)
    slots = CAP * pairs
    total = [0.0, 0.0]
    for kind in range(2):
        grads = jnp.concatenate(
            [grads_ref[m, kind * slots : (kind + 1) * slots, :] for m in range(pairs)], axis=1
        )
        for side, mine_ref in enumerate((own_ref, pair_ref)):
            weights = jnp.concatenate([mine_ref[1 + kind], core_ref[side, 1 + kind]])
            total[side] = total[side] + matmul(grads, weights, NT)
    row, slot = iota((8 * pairs, slots), 0), iota((8 * pairs, slots), 1)
    placed = 0.0
    for half in range(2):
        place = (slot % pairs == row // 8) & (row % 8 == 4 * half + slot // pairs)
        placed = placed + matmul(place.astype(BF16), total[half].astype(BF16))
    out_ref[...] = placed.astype(BF16).reshape(out_ref.shape)


def join_body(_, own_ref, inner_ref, pair_ref, out_ref):
    slots = inner_ref.shape[1]
    split = own_ref.shape[0] - 2 * slots
    out_ref[0, :split, :] = own_ref[:split, :]
    out_ref[0, split:, :] = inner_ref[1]
    out_ref[1, :split, :] = pair_ref[:split, :]
    out_ref[1, split:, :] = pair_ref[split + slots :, :]


def grad_body(inner_ref, own_ref, pair_ref, core_ref, gate_ref, up_ref, down_ref, done_ref):
    slots = inner_ref.shape[1]
    split = own_ref.shape[0] - 2 * slots
    lefts = [inner_ref[0], pair_ref[split : split + slots, :], core_ref[0, split:, :], core_ref[1, split:, :]]
    left = jnp.concatenate(lefts).astype(F32).T.astype(BF16)
    sent, taken = left[:HALF], left[HALF:]
    rights = (own_ref, pair_ref, core_ref.at[0], core_ref.at[1])
    for m in range(split // (3 * slots)):
        columns = slice(m * LANES, (m + 1) * LANES)
        for kind, (rows, out_ref) in enumerate(((taken, gate_ref), (taken, up_ref), (sent, down_ref))):
            start = (3 * m + kind) * slots
            right = jnp.concatenate([ref[start : start + slots, :] for ref in rights])
            out_ref[:, columns] = matmul(rows, right)
    done_ref[...] = jnp.zeros_like(done_ref)


def token_body(place_ref, _, index_ref, rows_ref, out_ref):
    parity, core = place_ref[0], place_ref[1]
    tokens = iota((out_ref.shape[0], index_ref.shape[1]), 0)
    sides = []
    for side in range(2):
        owner = (tokens == index_ref[side : side + 1, :]).astype(BF16)
        total = matmul(owner, rows_ref[...])
        sides.append(jnp.where(core == 0, total, pltpu.roll(total, HALF, 1)))
    near, far = sides
    out_ref[:, :LANES] = jnp.where(parity == 0, near, far).astype(BF16)
    out_ref[:, LANES:] = jnp.where(parity == 0, far, near).astype(BF16)


def swap(x, axis):
    return lax.ppermute(x, axis, [(0, 1), (1, 0)])


def spread(x, axis):
    return lax.all_to_all(x, axis, split_axis=0, concat_axis=0, tiled=True)


def local(pairs, tokens, grad_out, picked, pick_counts, router_weights, saved_gate, saved_up, w_gate, w_up, w_down):
    experts = picked.shape[1]
    token_count, width = tokens.shape
    hidden = w_gate.shape[2]
    slots = CAP * pairs
    place = jnp.stack([lax.axis_index("p"), lax.axis_index("core")]).astype(jnp.int32)

    outgoing, saved = call(
        pick_body,
        (struct(experts, 8, width), struct(pairs, 8, LANES)),
        [FETCH] * 7,
        scratch=(pltpu.VMEM((width // LANES, 8 * experts, LANES), F32),),
        limit=60,
    )(picked.transpose(2, 0, 1), pick_counts, router_weights.transpose(2, 0, 1), tokens, grad_out, saved_gate[0], saved_up[0])
    blocks = spread(outgoing, "expert")

    own = jnp.stack([w_down[0].T, w_gate[0], w_up[0]])
    pair = swap(own, "p")

    rows = call(send_body, struct(pairs, 24, LANES), [VMEM] * 2)(blocks, saved)
    core = swap(jnp.stack([own, pair]) + rows[0, 0, 0] * 0, "core")
    rows = spread(rows, "m")
    parts, saved, inner, outer = call(
        partial_body,
        (struct(pairs, slots, LANES),) + (struct(2, slots, LANES),) * 3,
        [SMEM] + [VMEM] * 4,
    )(place, rows.reshape(24 * pairs, LANES), own, pair, core)

    parts = spread(parts, "m")
    grads = call(hidden_body, struct(1, 3 * slots, LANES), [VMEM] * 2)(parts, saved)
    grads = lax.all_gather(grads, "m", axis=0, tiled=True)
    packed_rows = 3 * slots * pairs + 2 * slots
    back, packed = call(
        slot_body, (struct(pairs, 8, LANES), struct(packed_rows, LANES)), [VMEM] * 5
    )(grads, outer, own, pair, core)
    packed_pair = swap(packed, "p")
    back = spread(back, "m")
    packed_core = call(join_body, struct(2, packed_rows - slots, LANES), [ANY] + [VMEM] * 3)(
        back, packed, inner, packed_pair
    )
    packed_core = swap(packed_core, "core")
    back = spread(back, "expert")

    gate_grad, up_grad, down_grad, done = call(
        grad_body, (struct(HALF, hidden, dtype=F32),) * 3 + (struct(8, LANES, dtype=F32),), [VMEM] * 4
    )(inner, packed, packed_pair, packed_core)

    index = jnp.pad(picked[0], ((0, 0), (0, 1)), constant_values=-1)
    index = jnp.tile(index, (1, 2)).reshape(1, -1)
    upper = jnp.arange(8 * experts, dtype=jnp.int32)[None, :] // 4 % 2
    index = jnp.where(upper == jnp.arange(2)[:, None], index, -1)
    token_grad = call(token_body, struct(token_count, width), [SMEM] + [VMEM] * 3)(
        place, done, index, back.reshape(8 * experts, LANES)
    )
    return (token_grad, gate_grad[None], up_grad[None], down_grad.T[None])


def solution(mesh):
    pairs = mesh.shape["dp"] // 4
    fine = Mesh(mesh.devices.reshape(pairs, 2, 2, mesh.shape["expert"]), ("m", "p", "core", "expert"))
    dp = ("m", "p", "core")
    placed = (
        P(dp, "expert"),
        P(dp, "expert"),
        P(dp, None, None),
        P(dp, None),
        P(dp, None, None),
        P("expert", dp, None),
        P("expert", dp, None),
        P("expert", dp, None),
        P("expert", dp, None),
        P("expert", None, dp),
    )
    return jax.shard_map(
        functools.partial(local, pairs),
        mesh=fine,
        in_specs=placed,
        out_specs=(
            P(dp, "expert"),
            P("expert", dp, None),
            P("expert", dp, None),
            P("expert", None, dp),
        ),
        check_vma=False,
    )
```

time: 500 us -> 214 us (0.43)
  blocking collectives: 294 us -> 117 us
  waiting for transfers between devices: 101 us -> 25.1 us
  starting transfers between devices: 25.4 us -> 55 us
  local copies, waits for them, and re-layouts: 32.4 us -> 4.07 us
  other arithmetic: 23.4 us -> 2.63 us
  between operations: 14.4 us -> 1.44 us
  Pallas kernels: 0 us -> 8.21 us
  matrix products: 7.94 us -> 0 us
    all_gather x3 -> x1, blocking collectives: 176 us -> 40 us  [local(): grads = lax.all_gather(grads, 'm', axis=0, tiled=True)]
    all_gather x1 -> x0, waiting for transfers between devices: 72.2 us -> none  [local(): lax.all_gather(gathered_out, 'dp', axis=1, tiled=True)]
    all_to_all x3, blocking collectives: 119 us -> 77 us  [spread(): return lax.all_to_all(x, axis, split_axis=0, concat_axis=0, tiled=True)]
    ppermute x0 -> x4, starting transfers between devices: none -> 28.7 us  [swap(): return lax.ppermute(x, axis, [(0, 1), (1, 0)])]
    unnamed x2 -> x0, other arithmetic: 22.5 us -> none
    unnamed x23 -> x10, local copies, waits for them, and re-layouts: 17.5 us -> 2.74 us
    all_to_all x10 -> x0, local copies, waits for them, and re-layouts: 9.93 us -> none  [the longest x3 2.96 us: local(): lax.all_to_all(slot_grad, 'dp', split_axis=0, concat_axis=2, tiled=True)]
    pallas_call x0 -> x8, Pallas kernels: none -> 8.21 us  [the longest x1 2.16 us: local(): call(grad_body, (struct(HALF, hidden, dtype=F32),) * 3 + (struct(8, LANES...]
  transfers between devices with their start and end apart: 4 -> 6, of which waited for: 3 -> 2; matrix products, arithmetic and copies ran while one was open for 1% -> 1% of each run, Pallas kernels for 0% -> 2%
where the time goes in v3:
time: 214 us; the launch traced here: 213 us
  blocking collectives  117 us (55%)
  starting transfers between devices  55 us (26%)
  waiting for transfers between devices  25.1 us (12%)
  Pallas kernels  8.21 us (4%)
  local copies, waits for them, and re-layouts  4.07 us (2%)
  other arithmetic  2.63 us (1%)
    all_to_all x3, blocking collectives, spread(): return lax.all_to_all(x, axis, split_axis=0, concat_axis=0, tiled=True)  77 us
    all_gather x1, blocking collectives, local(): grads = lax.all_gather(grads, 'm', axis=0, tiled=True)  40 us
    ppermute x4, starting transfers between devices, swap(): return lax.ppermute(x, axis, [(0, 1), (1, 0)])  28.7 us
    all_to_all x2, starting transfers between devices, spread(): return lax.all_to_all(x, axis, split_axis=0, concat_axis=0, tiled=True)  26.3 us
    all_to_all x2, waiting for transfers between devices, spread(): return lax.all_to_all(x, axis, split_axis=0, concat_axis=0, tiled=True)  25.1 us
  transfers between devices with their start and end apart: 6, of which 2 were waited for; matrix products, arithmetic and copies ran while one was open for 1% of the time, Pallas kernels for 2%

profile of v3, /device:TPU:1, one launch (start us, length us, event | category | flops | bytes accessed | tf_op | source)
XLA Modules:
  0.0 213.4 jit_solution(7435450757485729251)
XLA Ops:
  0.6 1.2 fusion.1
  1.9 4.4 %collective-permute-start = (bf16[3,64,2048]{2,1,0:T(8,128)(2,1)S(1)}, bf16[3,64,2048]{2,1,0:T(8,128)(2,1)S(1)}, u32[]{:S(2)}, u32[]{:S(2)}) collective-permute-start(bf16[3,64,2048]{2,1,0:T(8,128)(2,1)S(1)} %get-tuple-element.29.own_ref), channel_id=1, source_target_pairs={{0,32},{32,0},{1,33},{33,1},{2,34},{34,2},{3,35},{35,3},{4,36},{36... | collective-permute-start | bytes 2359304 | tf_op jit(solution)/shard_map/ppermute | solution.py:175
  6.2 1.7 shard_map.129
  7.9 13.3 %all_to_all.25.blocks_ref = bf16[16,8,256]{2,1,0:T(8,128)(2,1)S(1)} all-to-all(bf16[16,8,256]{2,1,0:T(8,128)(2,1)} %get-tuple-element.16), channel_id=1, replica_groups=mesh['m'=16,'p'=2,'core'=2,'expert'=16] {'expert'}, dimensions={0} | all-to-all | bytes 131072 | tf_op jit(solution)/shard_map/all_to_all | solution.py:179
  21.2 0.0 copy-start.2
  21.2 0.8 copy-done.2
  22.0 0.7 shard_map.130
  22.6 1.2 slice.4
  24.5 0.0 collective-permute-done.pair_ref
  24.5 1.3 maximum_add_fusion
  25.8 11.4 %collective-permute-start.1 = (bf16[2,3,64,2048]{3,2,1,0:T(8,128)(2,1)}, bf16[2,3,64,2048]{3,2,1,0:T(8,128)(2,1)S(1)}, u32[]{:S(2)}, u32[]{:S(2)}) collective-permute-start(bf16[2,3,64,2048]{3,2,1,0:T(8,128)(2,1)} %maximum_add_fusion), channel_id=1, source_target_pairs={{0,16},{16,0},{1,17},{17,1},{2,18},{18,2},{3,19},{19,3},{4,20},{20... | collective-permute-start | bytes 4718600 | tf_op jit(solution)/shard_map/ppermute | solution.py:175
  37.2 20.1 %all-to-all-start.1 = ((bf16[16,24,128]{2,1,0:T(8,128)(2,1)}), bf16[16,24,128]{2,1,0:T(8,128)(2,1)S(1)}, u32[]{:S(2)}, u32[]{:S(2)}) async-start(bf16[16,24,128]{2,1,0:T(8,128)(2,1)} %shard_map.130), calls=%async_computation.1 | async-start | bytes 196608 | tf_op jit(solution)/shard_map/all_to_all | solution.py:179
  57.4 0.1 pad_add_fusion.place_ref
  57.5 21.9 %all-to-all-done.1 = bf16[16,24,128]{2,1,0:T(8,128)(2,1)S(1)} async-done(((bf16[16,24,128]{2,1,0:T(8,128)(2,1)}), bf16[16,24,128]{2,1,0:T(8,128)(2,1)S(1)}, u32[]{:S(2)}, u32[]{:S(2)}) %all-to-all-start.1) | async-done | bytes 98336 | tf_op jit(solution)/shard_map/all_to_all | solution.py:179
  79.3 0.0 collective-permute-done.1.core_ref
  79.3 1.2 shard_map.131
  80.6 31.0 %all_to_all.26.parts_ref = bf16[16,48,128]{2,1,0:T(8,128)(2,1)S(1)} all-to-all(bf16[16,48,128]{2,1,0:T(8,128)(2,1)S(1)} %get-tuple-element.19), channel_id=1, replica_groups=mesh['m'=16,'p'=2,'core'=2,'expert'=16] {'m'}, dimensions={0} | all-to-all | bytes 393216 | tf_op jit(solution)/shard_map/all_to_all | solution.py:179
  111.6 40.0 %all_gather.3.grads_ref = bf16[16,144,128]{2,1,0:T(8,128)(2,1)S(1)} all-gather(bf16[1,144,128]{2,1,0:T(8,128)(2,1)S(1)} %shard_map.132), channel_id=1, replica_groups=mesh['m'=16,'p'=2,'core'=2,'expert'=16] {'m'}, dimensions={0}, use_global_device_ids=true | all-gather | bytes 626688 | tf_op jit(solution)/shard_map/all_gather | solution.py:212
  151.6 1.0 shard_map.133
  152.6 0.0 copy-start.3
  152.6 2.6 %collective-permute-start.2 = (bf16[2400,128]{1,0:T(8,128)(2,1)S(1)}, bf16[2400,128]{1,0:T(8,128)(2,1)S(1)}, u32[]{:S(2)}, u32[]{:S(2)}) collective-permute-start(bf16[2400,128]{1,0:T(8,128)(2,1)S(1)} %get-tuple-element.22.own_ref), channel_id=1, source_target_pairs={{0,32},{32,0},{1,33},{33,1},{2,34},{34,2},{3,35},{35,3},{4,36},{36... | collective-permute-start | bytes 1843208 | tf_op jit(solution)/shard_map/ppermute | solution.py:175
  155.3 32.7 %all_to_all.27._ = bf16[16,8,128]{2,1,0:T(8,128)(2,1)} all-to-all(bf16[16,8,128]{2,1,0:T(8,128)(2,1)S(1)} %get-tuple-element.23), channel_id=1, replica_groups=mesh['m'=16,'p'=2,'core'=2,'expert'=16] {'m'}, dimensions={0} | all-to-all | bytes 65536 | tf_op jit(solution)/shard_map/all_to_all | solution.py:179
  188.0 0.0 collective-permute-done.2.pair_ref
  188.0 0.1 shard_map.134
  188.1 0.0 copy-start
  188.1 0.8 copy-done
  188.9 10.2 %collective-permute-start.3 = (bf16[2,2352,128]{2,1,0:T(8,128)(2,1)S(1)}, bf16[2,2352,128]{2,1,0:T(8,128)(2,1)S(1)}, u32[]{:S(2)}, u32[]{:S(2)}) collective-permute-start(bf16[2,2352,128]{2,1,0:T(8,128)(2,1)S(1)} %shard_map.134), channel_id=1, source_target_pairs={{0,16},{16,0},{1,17},{17,1},{2,18},{18,2},{3,19},{19,3},{4,20},{20... | collective-permute-start | bytes 3612680 | tf_op jit(solution)/shard_map/ppermute | solution.py:175
  199.2 0.0 copy-done.3
  199.2 0.1 copy.18
  199.3 0.1 tile.9
  199.4 6.2 %all-to-all-start.4 = ((bf16[16,8,128]{2,1,0:T(8,128)(2,1)}), bf16[16,8,128]{2,1,0:T(8,128)(2,1)S(1)}, u32[]{:S(2)}, u32[]{:S(2)}) async-start(bf16[16,8,128]{2,1,0:T(8,128)(2,1)} %all_to_all.27._), calls=%async_computation.4 | async-start | bytes 65536 | tf_op jit(solution)/shard_map/all_to_all | solution.py:179
  205.6 0.0 collective-permute-done.3.core_ref
  205.6 0.0 copy-start.1
  205.6 1.1 copy-done.1
  206.7 2.2 %shard_map.135 = (f32[64,2048]{1,0:T(8,128)}, f32[64,2048]{1,0:T(8,128)}, f32[64,2048]{1,0:T(8,128)}, f32[8,128]{1,0:T(8,128)S(1)}) custom-call(bf16[2,48,128]{2,1,0:T(8,128)(2,1)S(1)} %get-tuple-element.18.inner_ref, bf16[2400,128]{1,0:T(8,128)(2,1)S(1)} %copy-done.1, bf16[2400,128]{1,0:T(8,128)(2,1)S(1)} %collective-permute-done.2.pair_ref, ...), custom_call_target="tpu_custom_call" | custom-call | tf_op jit(solution)/shard_map/pallas_call | solution.py:225
  208.9 3.2 %all-to-all-done.4 = bf16[16,8,128]{2,1,0:T(8,128)(2,1)S(1)} async-done(((bf16[16,8,128]{2,1,0:T(8,128)(2,1)}), bf16[16,8,128]{2,1,0:T(8,128)(2,1)S(1)}, u32[]{:S(2)}, u32[]{:S(2)}) %all-to-all-start.4) | async-done | bytes 32800 | tf_op jit(solution)/shard_map/all_to_all | solution.py:179
  212.1 1.4 shard_map.136
  (6 shorter events, 0.1 us)
Async XLA Ops:
  1.9 22.6 %collective-permute-start = (bf16[3,64,2048]{2,1,0:T(8,128)(2,1)S(1)}, bf16[3,64,2048]{2,1,0:T(8,128)(2,1)S(1)}, u32[]{:S(2)}, u32[]{:S(2)}) collective-permute-start(bf16[3,64,2048]{2,1,0:T(8,128)(2,1)S(1)} %get-tuple-element.29.own_ref), channel_id=1, source_target_pairs={{0,32},{32,0},{1,33},{33,1},{2,34},{34,2},{3,35},{35,3},{4,36},{36... | collective-permute-start | bytes 2359304 | tf_op jit(solution)/shard_map/ppermute | solution.py:175
  21.2 0.8 copy-start.2
  25.8 53.6 %collective-permute-start.1 = (bf16[2,3,64,2048]{3,2,1,0:T(8,128)(2,1)}, bf16[2,3,64,2048]{3,2,1,0:T(8,128)(2,1)S(1)}, u32[]{:S(2)}, u32[]{:S(2)}) collective-permute-start(bf16[2,3,64,2048]{3,2,1,0:T(8,128)(2,1)} %maximum_add_fusion), channel_id=1, source_target_pairs={{0,16},{16,0},{1,17},{17,1},{2,18},{18,2},{3,19},{19,3},{4,20},{20... | collective-permute-start | bytes 4718600 | tf_op jit(solution)/shard_map/ppermute | solution.py:175
  37.2 42.1 %all-to-all-start.1 = ((bf16[16,24,128]{2,1,0:T(8,128)(2,1)}), bf16[16,24,128]{2,1,0:T(8,128)(2,1)S(1)}, u32[]{:S(2)}, u32[]{:S(2)}) async-start(bf16[16,24,128]{2,1,0:T(8,128)(2,1)} %shard_map.130), calls=%async_computation.1 | async-start | bytes 196608 | tf_op jit(solution)/shard_map/all_to_all | solution.py:179
  152.6 46.6 %copy-start.3 = (s32[1,16,3]{1,0,2:T(1,128)S(1)}, s32[1,16,3]{1,0,2:T(1,128)}, u32[]{:S(2)}) copy-start(s32[1,16,3]{1,0,2:T(1,128)} %param.12) | copy-start | bytes 580
  152.6 35.4 %collective-permute-start.2 = (bf16[2400,128]{1,0:T(8,128)(2,1)S(1)}, bf16[2400,128]{1,0:T(8,128)(2,1)S(1)}, u32[]{:S(2)}, u32[]{:S(2)}) collective-permute-start(bf16[2400,128]{1,0:T(8,128)(2,1)S(1)} %get-tuple-element.22.own_ref), channel_id=1, source_target_pairs={{0,32},{32,0},{1,33},{33,1},{2,34},{34,2},{3,35},{35,3},{4,36},{36... | collective-permute-start | bytes 1843208 | tf_op jit(solution)/shard_map/ppermute | solution.py:175
  188.1 0.8 copy-start
  188.9 16.7 %collective-permute-start.3 = (bf16[2,2352,128]{2,1,0:T(8,128)(2,1)S(1)}, bf16[2,2352,128]{2,1,0:T(8,128)(2,1)S(1)}, u32[]{:S(2)}, u32[]{:S(2)}) collective-permute-start(bf16[2,2352,128]{2,1,0:T(8,128)(2,1)S(1)} %shard_map.134), channel_id=1, source_target_pairs={{0,16},{16,0},{1,17},{17,1},{2,18},{18,2},{3,19},{19,3},{4,20},{20... | collective-permute-start | bytes 3612680 | tf_op jit(solution)/shard_map/ppermute | solution.py:175
  199.4 12.7 %all-to-all-start.4 = ((bf16[16,8,128]{2,1,0:T(8,128)(2,1)}), bf16[16,8,128]{2,1,0:T(8,128)(2,1)S(1)}, u32[]{:S(2)}, u32[]{:S(2)}) async-start(bf16[16,8,128]{2,1,0:T(8,128)(2,1)} %all_to_all.27._), calls=%async_computation.4 | async-start | bytes 65536 | tf_op jit(solution)/shard_map/all_to_all | solution.py:179
  205.6 1.1 copy-start.1

commit v4 on v3

--- a/solution.py
+++ b/solution.py
@@ -21,7 +21,7 @@
 FETCH = pl.BlockSpec()
 
 
-def call(body, outs, ins, out_specs=None, scratch=(), limit=40):
+def call(body, outs, ins, out_specs=None, scratch=(), limit=24):
     return pl.pallas_call(
         body,
         out_shape=outs,
@@ -95,7 +95,7 @@
         here = parity == side
         sent = turn(jnp.where(here, piece(0), piece(8)))
         taken = turn(jnp.where(here, piece(4), piece(12)))
-        product = product + matmul(sent.astype(BF16), jnp.concatenate([mine_ref[0], core_ref[side, 0]]))
+        product = product + matmul(sent.astype(BF16), jnp.concatenate([mine_ref[...], core_ref[side]]))
         out[0] = jnp.where(low, sent, pltpu.roll(taken, HALF, 1)).astype(BF16)
         out[1] = jnp.where(low, pltpu.roll(sent, HALF, 1), taken).astype(BF16)
     for k in range(pairs):
@@ -123,7 +123,7 @@
             [grads_ref[m, kind * slots : (kind + 1) * slots, :] for m in range(pairs)], axis=1
         )
         for side, mine_ref in enumerate((own_ref, pair_ref)):
-            weights = jnp.concatenate([mine_ref[1 + kind], core_ref[side, 1 + kind]])
+            weights = jnp.concatenate([mine_ref[kind], core_ref[side, kind]])
             total[side] = total[side] + matmul(grads, weights, NT)
     row, slot = iota((8 * pairs, slots), 0), iota((8 * pairs, slots), 1)
     placed = 0.0
@@ -135,8 +135,8 @@
 
 def join_body(_, own_ref, inner_ref, pair_ref, out_ref):
     slots = inner_ref.shape[1]
-    split = own_ref.shape[0] - 2 * slots
-    out_ref[0, :split, :] = own_ref[:split, :]
+    split = own_ref.shape[0]
+    out_ref[0, :split, :] = own_ref[...]
     out_ref[0, split:, :] = inner_ref[1]
     out_ref[1, :split, :] = pair_ref[:split, :]
     out_ref[1, split:, :] = pair_ref[split + slots :, :]
@@ -144,7 +144,7 @@
 
 def grad_body(inner_ref, own_ref, pair_ref, core_ref, gate_ref, up_ref, down_ref, done_ref):
     slots = inner_ref.shape[1]
-    split = own_ref.shape[0] - 2 * slots
+    split = own_ref.shape[0]
     lefts = [inner_ref[0], pair_ref[split : split + slots, :], core_ref[0, split:, :], core_ref[1, split:, :]]
     left = jnp.concatenate(lefts).astype(F32).T.astype(BF16)
     sent, taken = left[:HALF], left[HALF:]
@@ -195,21 +195,25 @@
     )(picked.transpose(2, 0, 1), pick_counts, router_weights.transpose(2, 0, 1), tokens, grad_out, saved_gate[0], saved_up[0])
     blocks = spread(outgoing, "expert")
 
-    own = jnp.stack([w_down[0].T, w_gate[0], w_up[0]])
+    down = w_down[0].T
+    down_pair = swap(down, "p")
+    down_core = swap(jnp.stack([down, down_pair]), "core")
+    own = jnp.stack([w_gate[0], w_up[0]])
     pair = swap(own, "p")
+    core = swap(jnp.stack([own, pair]), "core")
 
     rows = call(send_body, struct(pairs, 24, LANES), [VMEM] * 2)(blocks, saved)
-    core = swap(jnp.stack([own, pair]) + rows[0, 0, 0] * 0, "core")
     rows = spread(rows, "m")
     parts, saved, inner, outer = call(
         partial_body,
         (struct(pairs, slots, LANES),) + (struct(2, slots, LANES),) * 3,
         [SMEM] + [VMEM] * 4,
-    )(place, rows.reshape(24 * pairs, LANES), own, pair, core)
+    )(place, rows.reshape(24 * pairs, LANES), down, down_pair, down_core)
 
     parts = spread(parts, "m")
     grads = call(hidden_body, struct(1, 3 * slots, LANES), [VMEM] * 2)(parts, saved)
     grads = lax.all_gather(grads, "m", axis=0, tiled=True)
+    flat = grads.reshape(3 * slots * pairs, LANES)
     packed_rows = 3 * slots * pairs + 2 * slots
     back, packed = call(
         slot_body, (struct(pairs, 8, LANES), struct(packed_rows, LANES)), [VMEM] * 5
@@ -217,14 +221,14 @@
     packed_pair = swap(packed, "p")
     back = spread(back, "m")
     packed_core = call(join_body, struct(2, packed_rows - slots, LANES), [ANY] + [VMEM] * 3)(
-        back, packed, inner, packed_pair
+        back, flat, inner, packed_pair
     )
     packed_core = swap(packed_core, "core")
     back = spread(back, "expert")
 
     gate_grad, up_grad, down_grad, done = call(
         grad_body, (struct(HALF, hidden, dtype=F32),) * 3 + (struct(8, LANES, dtype=F32),), [VMEM] * 4
-    )(inner, packed, packed_pair, packed_core)
+    )(inner, flat, packed_pair, packed_core)
 
     index = jnp.pad(picked[0], ((0, 0), (0, 1)), constant_values=-1)
     index = jnp.tile(index, (1, 2)).reshape(1, -1)

time: 214 us -> 203 us (0.949)
  blocking collectives: 117 us -> 79.1 us
  starting transfers between devices: 55 us -> 73.7 us
  waiting for transfers between devices: 25.1 us -> 35.9 us
  local copies, waits for them, and re-layouts: 4.07 us -> 1.03 us
    all_to_all x3 -> x2, blocking collectives: 77 us -> 43.2 us  [spread(): return lax.all_to_all(x, axis, split_axis=0, concat_axis=0, tiled=True)]
    all_to_all x2 -> x3, starting transfers between devices: 26.3 us -> 38.8 us  [spread(): return lax.all_to_all(x, axis, split_axis=0, concat_axis=0, tiled=True)]
    all_to_all x2 -> x3, waiting for transfers between devices: 25.1 us -> 35.9 us  [spread(): return lax.all_to_all(x, axis, split_axis=0, concat_axis=0, tiled=True)]
    ppermute x4 -> x6, starting transfers between devices: 28.7 us -> 34.9 us  [swap(): return lax.ppermute(x, axis, [(0, 1), (1, 0)])]
    all_gather x1, blocking collectives: 40 us -> 35.9 us  [local(): grads = lax.all_gather(grads, 'm', axis=0, tiled=True)]
  transfers between devices with their start and end apart: 6 -> 9, of which waited for: 2 -> 3; matrix products, arithmetic and copies ran while one was open for 1% -> 1% of each run, Pallas kernels for 2% -> 3%
where the time goes in v4:
time: 203 us
  blocking collectives  79.1 us (39%)
  starting transfers between devices  73.7 us (36%)
  waiting for transfers between devices  35.9 us (18%)
  Pallas kernels  9.92 us (5%)
  other arithmetic  2.17 us (1%)
    all_to_all x2, blocking collectives, spread(): return lax.all_to_all(x, axis, split_axis=0, concat_axis=0, tiled=True)  43.2 us
    all_to_all x3, starting transfers between devices, spread(): return lax.all_to_all(x, axis, split_axis=0, concat_axis=0, tiled=True)  38.8 us
    all_to_all x3, waiting for transfers between devices, spread(): return lax.all_to_all(x, axis, split_axis=0, concat_axis=0, tiled=True)  35.9 us
    all_gather x1, blocking collectives, local(): grads = lax.all_gather(grads, 'm', axis=0, tiled=True)  35.9 us
    ppermute x6, starting transfers between devices, swap(): return lax.ppermute(x, axis, [(0, 1), (1, 0)])  34.9 us
  transfers between devices with their start and end apart: 9, of which 3 were waited for; matrix products, arithmetic and copies ran while one was open for 1% of the time, Pallas kernels for 3%

profile of v4, /device:TPU:1, one launch (start us, length us, event | category | flops | bytes accessed | tf_op | source)
XLA Modules:
  0.0 202.7 jit_solution(5813716319815044393)
XLA Ops:
  0.6 4.4 %collective-permute-start = (bf16[64,2048]{1,0:T(8,128)(2,1)}, bf16[64,2048]{1,0:T(8,128)(2,1)S(1)}, u32[]{:S(2)}, u32[]{:S(2)}) collective-permute-start(bf16[64,2048]{1,0:T(8,128)(2,1)} %bitcast.29), channel_id=1, source_target_pairs={{0,32},{32,0},{1,33},{33,1},{2,34},{34,2},{3,35},{35,3},{4,36},{36... | collective-permute-start | bytes 786440 | tf_op jit(solution)/shard_map/ppermute | solution.py:175
  5.0 1.7 shard_map.129
  6.7 13.3 %all_to_all.25.blocks_ref = bf16[16,8,256]{2,1,0:T(8,128)(2,1)S(1)} all-to-all(bf16[16,8,256]{2,1,0:T(8,128)(2,1)} %get-tuple-element.16), channel_id=1, replica_groups=mesh['m'=16,'p'=2,'core'=2,'expert'=16] {'expert'}, dimensions={0} | all-to-all | bytes 131072 | tf_op jit(solution)/shard_map/all_to_all | solution.py:179
  20.0 0.0 copy-start.1
  20.0 0.8 copy-done.1
  20.7 0.0 copy-start.2
  20.7 0.0 copy-start.3
  20.7 0.7 shard_map.130
  21.4 0.0 copy-start
  21.4 27.4 %all-to-all-start.1 = ((bf16[16,24,128]{2,1,0:T(8,128)(2,1)}), bf16[16,24,128]{2,1,0:T(8,128)(2,1)S(1)}, u32[]{:S(2)}, u32[]{:S(2)}) async-start(bf16[16,24,128]{2,1,0:T(8,128)(2,1)} %shard_map.130), calls=%async_computation.1 | async-start | bytes 196608 | tf_op jit(solution)/shard_map/all_to_all | solution.py:179
  48.8 0.0 collective-permute-done.pair_ref
  48.8 1.0 pad_maximum_fusion.1
  49.8 4.6 %collective-permute-start.1 = (bf16[2,64,2048]{2,1,0:T(8,128)(2,1)S(1)}, bf16[2,64,2048]{2,1,0:T(8,128)(2,1)S(1)}, u32[]{:S(2)}, u32[]{:S(2)}) collective-permute-start(bf16[2,64,2048]{2,1,0:T(8,128)(2,1)S(1)} %pad_maximum_fusion.1), channel_id=1, source_target_pairs={{0,16},{16,0},{1,17},{17,1},{2,18},{18,2},{3,19},{19,3},{4,20},{20... | collective-permute-start | bytes 1572872 | tf_op jit(solution)/shard_map/ppermute | solution.py:175
  54.4 0.0 copy-done.2
  54.4 0.0 copy-done.3
  54.5 2.6 %collective-permute-start.2 = (bf16[2,64,2048]{2,1,0:T(8,128)(2,1)S(1)}, bf16[2,64,2048]{2,1,0:T(8,128)(2,1)S(1)}, u32[]{:S(2)}, u32[]{:S(2)}) collective-permute-start(bf16[2,64,2048]{2,1,0:T(8,128)(2,1)S(1)} %constant_dynamic-update-slice_fusion.own_ref), channel_id=1, source_target_pairs={{0,32},{32,0},{1,33},{33,1},{2,34},{34,2},{3,35},{35,3},{4,36},{36... | collective-permute-start | bytes 1572872 | tf_op jit(solution)/shard_map/ppermute | solution.py:175
  57.1 0.1 pad_add_fusion.place_ref
  57.2 0.0 collective-permute-done.1.core_ref
  57.2 13.5 %all-to-all-done.1 = bf16[16,24,128]{2,1,0:T(8,128)(2,1)S(1)} async-done(((bf16[16,24,128]{2,1,0:T(8,128)(2,1)}), bf16[16,24,128]{2,1,0:T(8,128)(2,1)S(1)}, u32[]{:S(2)}, u32[]{:S(2)}) %all-to-all-start.1) | async-done | bytes 98336 | tf_op jit(solution)/shard_map/all_to_all | solution.py:179
  70.7 0.0 copy-done
  70.7 1.9 shard_map.131
  72.6 7.9 %all-to-all-start.2 = ((bf16[16,48,128]{2,1,0:T(8,128)(2,1)}), bf16[16,48,128]{2,1,0:T(8,128)(2,1)S(1)}, u32[]{:S(2)}, u32[]{:S(2)}) async-start(bf16[16,48,128]{2,1,0:T(8,128)(2,1)} %get-tuple-element.19), calls=%async_computation.2 | async-start | bytes 393216 | tf_op jit(solution)/shard_map/all_to_all | solution.py:179
  80.5 0.0 collective-permute-done.2.pair_ref
  80.5 1.1 pad_maximum_fusion
  81.6 4.0 %collective-permute-start.3 = (bf16[2,2,64,2048]{3,2,1,0:T(8,128)(2,1)}, bf16[2,2,64,2048]{3,2,1,0:T(8,128)(2,1)S(1)}, u32[]{:S(2)}, u32[]{:S(2)}) collective-permute-start(bf16[2,2,64,2048]{3,2,1,0:T(8,128)(2,1)} %pad_maximum_fusion), channel_id=1, source_target_pairs={{0,16},{16,0},{1,17},{17,1},{2,18},{18,2},{3,19},{19,3},{4,20},{20... | collective-permute-start | bytes 3145736 | tf_op jit(solution)/shard_map/ppermute | solution.py:175
  85.6 18.2 %all-to-all-done.2.parts_ref = bf16[16,48,128]{2,1,0:T(8,128)(2,1)S(1)} async-done(((bf16[16,48,128]{2,1,0:T(8,128)(2,1)}), bf16[16,48,128]{2,1,0:T(8,128)(2,1)S(1)}, u32[]{:S(2)}, u32[]{:S(2)}) %all-to-all-start.2) | async-done | bytes 196640 | tf_op jit(solution)/shard_map/all_to_all | solution.py:179
  103.9 35.9 %all_gather.3.grads_ref = bf16[16,144,128]{2,1,0:T(8,128)(2,1)S(1)} all-gather(bf16[1,144,128]{2,1,0:T(8,128)(2,1)S(1)} %shard_map.132), channel_id=1, replica_groups=mesh['m'=16,'p'=2,'core'=2,'expert'=16] {'m'}, dimensions={0}, use_global_device_ids=true | all-gather | bytes 626688 | tf_op jit(solution)/shard_map/all_gather | solution.py:215
  139.8 0.0 collective-permute-done.3.core_ref
  139.8 1.0 shard_map.133
  140.8 5.3 %collective-permute-start.4 = (bf16[2400,128]{1,0:T(8,128)(2,1)S(1)}, bf16[2400,128]{1,0:T(8,128)(2,1)S(1)}, u32[]{:S(2)}, u32[]{:S(2)}) collective-permute-start(bf16[2400,128]{1,0:T(8,128)(2,1)S(1)} %get-tuple-element.22), channel_id=1, source_target_pairs={{0,32},{32,0},{1,33},{33,1},{2,34},{34,2},{3,35},{35,3},{4,36},{36... | collective-permute-start | bytes 1843208 | tf_op jit(solution)/shard_map/ppermute | solution.py:175
  146.1 30.0 %all_to_all.26._ = bf16[16,8,128]{2,1,0:T(8,128)(2,1)} all-to-all(bf16[16,8,128]{2,1,0:T(8,128)(2,1)S(1)} %get-tuple-element.23), channel_id=1, replica_groups=mesh['m'=16,'p'=2,'core'=2,'expert'=16] {'m'}, dimensions={0} | all-to-all | bytes 65536 | tf_op jit(solution)/shard_map/all_to_all | solution.py:179
  176.1 0.0 collective-permute-done.4.pair_ref
  176.1 0.0 copy-start.4
  176.1 1.1 shard_map.134
  177.2 13.9 %collective-permute-start.5 = (bf16[2,2352,128]{2,1,0:T(8,128)(2,1)}, bf16[2,2352,128]{2,1,0:T(8,128)(2,1)S(1)}, u32[]{:S(2)}, u32[]{:S(2)}) collective-permute-start(bf16[2,2352,128]{2,1,0:T(8,128)(2,1)} %shard_map.134), channel_id=1, source_target_pairs={{0,16},{16,0},{1,17},{17,1},{2,18},{18,2},{3,19},{19,3},{4,20},{20... | collective-permute-start | bytes 3612680 | tf_op jit(solution)/shard_map/ppermute | solution.py:175
  191.1 0.0 copy-done.4
  191.2 0.1 copy.18
  191.3 0.1 tile.9
  191.4 3.5 %all-to-all-start.4 = ((bf16[16,8,128]{2,1,0:T(8,128)(2,1)}), bf16[16,8,128]{2,1,0:T(8,128)(2,1)S(1)}, u32[]{:S(2)}, u32[]{:S(2)}) async-start(bf16[16,8,128]{2,1,0:T(8,128)(2,1)} %all_to_all.26._), calls=%async_computation.4 | async-start | bytes 65536 | tf_op jit(solution)/shard_map/all_to_all | solution.py:179
  194.9 0.0 collective-permute-done.5.core_ref
  194.9 2.2 %shard_map.135 = (f32[64,2048]{1,0:T(8,128)}, f32[64,2048]{1,0:T(8,128)}, f32[64,2048]{1,0:T(8,128)}, f32[8,128]{1,0:T(8,128)S(1)}) custom-call(bf16[2,48,128]{2,1,0:T(8,128)(2,1)S(1)} %get-tuple-element.18.inner_ref, bf16[2304,128]{1,0:T(8,128)(2,1)S(1)} %bitcast.26, bf16[2400,128]{1,0:T(8,128)(2,1)S(1)} %collective-permute-done.4.pair_ref, ...), custom_call_target="tpu_custom_call" | custom-call | tf_op jit(solution)/shard_map/pallas_call | solution.py:229
  197.1 4.2 %all-to-all-done.4 = bf16[16,8,128]{2,1,0:T(8,128)(2,1)S(1)} async-done(((bf16[16,8,128]{2,1,0:T(8,128)(2,1)}), bf16[16,8,128]{2,1,0:T(8,128)(2,1)S(1)}, u32[]{:S(2)}, u32[]{:S(2)}) %all-to-all-start.4) | async-done | bytes 32800 | tf_op jit(solution)/shard_map/all_to_all | solution.py:179
  201.3 1.4 shard_map.136
  (8 shorter events, 0.1 us)
Async XLA Ops:
  0.6 48.2 %collective-permute-start = (bf16[64,2048]{1,0:T(8,128)(2,1)}, bf16[64,2048]{1,0:T(8,128)(2,1)S(1)}, u32[]{:S(2)}, u32[]{:S(2)}) collective-permute-start(bf16[64,2048]{1,0:T(8,128)(2,1)} %bitcast.29), channel_id=1, source_target_pairs={{0,32},{32,0},{1,33},{33,1},{2,34},{34,2},{3,35},{35,3},{4,36},{36... | collective-permute-start | bytes 786440 | tf_op jit(solution)/shard_map/ppermute | solution.py:175
  20.0 0.8 copy-start.1
  20.7 33.7 %copy-start.2 = (bf16[1,64,2048]{2,1,0:T(8,128)(2,1)S(1)}, bf16[1,64,2048]{2,1,0:T(8,128)(2,1)}, u32[]{:S(2)}) copy-start(bf16[1,64,2048]{2,1,0:T(8,128)(2,1)} %param.17) | copy-start | bytes 786436
  20.7 33.7 %copy-start.3 = (bf16[1,64,2048]{2,1,0:T(8,128)(2,1)S(1)}, bf16[1,64,2048]{2,1,0:T(8,128)(2,1)}, u32[]{:S(2)}) copy-start(bf16[1,64,2048]{2,1,0:T(8,128)(2,1)} %param.18) | copy-start | bytes 786436
  21.4 49.3 %copy-start = (bf16[1,2048,64]{1,2,0:T(8,128)(2,1)S(1)}, bf16[1,2048,64]{1,2,0:T(8,128)(2,1)}, u32[]{:S(2)}) copy-start(bf16[1,2048,64]{1,2,0:T(8,128)(2,1)} %param.19) | copy-start | bytes 786436
  21.4 49.3 %all-to-all-start.1 = ((bf16[16,24,128]{2,1,0:T(8,128)(2,1)}), bf16[16,24,128]{2,1,0:T(8,128)(2,1)S(1)}, u32[]{:S(2)}, u32[]{:S(2)}) async-start(bf16[16,24,128]{2,1,0:T(8,128)(2,1)} %shard_map.130), calls=%async_computation.1 | async-start | bytes 196608 | tf_op jit(solution)/shard_map/all_to_all | solution.py:179
  49.8 7.4 %collective-permute-start.1 = (bf16[2,64,2048]{2,1,0:T(8,128)(2,1)S(1)}, bf16[2,64,2048]{2,1,0:T(8,128)(2,1)S(1)}, u32[]{:S(2)}, u32[]{:S(2)}) collective-permute-start(bf16[2,64,2048]{2,1,0:T(8,128)(2,1)S(1)} %pad_maximum_fusion.1), channel_id=1, source_target_pairs={{0,16},{16,0},{1,17},{17,1},{2,18},{18,2},{3,19},{19,3},{4,20},{20... | collective-permute-start | bytes 1572872 | tf_op jit(solution)/shard_map/ppermute | solution.py:175
  54.5 26.0 %collective-permute-start.2 = (bf16[2,64,2048]{2,1,0:T(8,128)(2,1)S(1)}, bf16[2,64,2048]{2,1,0:T(8,128)(2,1)S(1)}, u32[]{:S(2)}, u32[]{:S(2)}) collective-permute-start(bf16[2,64,2048]{2,1,0:T(8,128)(2,1)S(1)} %constant_dynamic-update-slice_fusion.own_ref), channel_id=1, source_target_pairs={{0,32},{32,0},{1,33},{33,1},{2,34},{34,2},{3,35},{35,3},{4,36},{36... | collective-permute-start | bytes 1572872 | tf_op jit(solution)/shard_map/ppermute | solution.py:175
  72.6 31.3 %all-to-all-start.2 = ((bf16[16,48,128]{2,1,0:T(8,128)(2,1)}), bf16[16,48,128]{2,1,0:T(8,128)(2,1)S(1)}, u32[]{:S(2)}, u32[]{:S(2)}) async-start(bf16[16,48,128]{2,1,0:T(8,128)(2,1)} %get-tuple-element.19), calls=%async_computation.2 | async-start | bytes 393216 | tf_op jit(solution)/shard_map/all_to_all | solution.py:179
  81.6 58.2 %collective-permute-start.3 = (bf16[2,2,64,2048]{3,2,1,0:T(8,128)(2,1)}, bf16[2,2,64,2048]{3,2,1,0:T(8,128)(2,1)S(1)}, u32[]{:S(2)}, u32[]{:S(2)}) collective-permute-start(bf16[2,2,64,2048]{3,2,1,0:T(8,128)(2,1)} %pad_maximum_fusion), channel_id=1, source_target_pairs={{0,16},{16,0},{1,17},{17,1},{2,18},{18,2},{3,19},{19,3},{4,20},{20... | collective-permute-start | bytes 3145736 | tf_op jit(solution)/shard_map/ppermute | solution.py:175
  140.8 35.3 %collective-permute-start.4 = (bf16[2400,128]{1,0:T(8,128)(2,1)S(1)}, bf16[2400,128]{1,0:T(8,128)(2,1)S(1)}, u32[]{:S(2)}, u32[]{:S(2)}) collective-permute-start(bf16[2400,128]{1,0:T(8,128)(2,1)S(1)} %get-tuple-element.22), channel_id=1, source_target_pairs={{0,32},{32,0},{1,33},{33,1},{2,34},{34,2},{3,35},{35,3},{4,36},{36... | collective-permute-start | bytes 1843208 | tf_op jit(solution)/shard_map/ppermute | solution.py:175
  176.1 15.1 %copy-start.4 = (s32[1,16,3]{1,0,2:T(1,128)S(1)}, s32[1,16,3]{1,0,2:T(1,128)}, u32[]{:S(2)}) copy-start(s32[1,16,3]{1,0,2:T(1,128)} %param.12) | copy-start | bytes 580
  177.2 17.7 %collective-permute-start.5 = (bf16[2,2352,128]{2,1,0:T(8,128)(2,1)}, bf16[2,2352,128]{2,1,0:T(8,128)(2,1)S(1)}, u32[]{:S(2)}, u32[]{:S(2)}) collective-permute-start(bf16[2,2352,128]{2,1,0:T(8,128)(2,1)} %shard_map.134), channel_id=1, source_target_pairs={{0,16},{16,0},{1,17},{17,1},{2,18},{18,2},{3,19},{19,3},{4,20},{20... | collective-permute-start | bytes 3612680 | tf_op jit(solution)/shard_map/ppermute | solution.py:175
  191.4 9.9 %all-to-all-start.4 = ((bf16[16,8,128]{2,1,0:T(8,128)(2,1)}), bf16[16,8,128]{2,1,0:T(8,128)(2,1)S(1)}, u32[]{:S(2)}, u32[]{:S(2)}) async-start(bf16[16,8,128]{2,1,0:T(8,128)(2,1)} %all_to_all.26._), calls=%async_computation.4 | async-start | bytes 65536 | tf_op jit(solution)/shard_map/all_to_all | solution.py:179

commit v5 on v4

--- a/solution.py
+++ b/solution.py
@@ -175,6 +175,11 @@
     return lax.ppermute(x, axis, [(0, 1), (1, 0)])
 
 
+def transpose(x, pairs):
+    moves = [(m * pairs + f, f * pairs + m) for m in range(pairs) for f in range(pairs)]
+    return lax.ppermute(x, ("m", "expert"), moves)
+
+
 def spread(x, axis):
     return lax.all_to_all(x, axis, split_axis=0, concat_axis=0, tiled=True)
 
@@ -219,12 +224,12 @@
         slot_body, (struct(pairs, 8, LANES), struct(packed_rows, LANES)), [VMEM] * 5
     )(grads, outer, own, pair, core)
     packed_pair = swap(packed, "p")
-    back = spread(back, "m")
+    back = spread(back, "expert")
     packed_core = call(join_body, struct(2, packed_rows - slots, LANES), [ANY] + [VMEM] * 3)(
         back, flat, inner, packed_pair
     )
     packed_core = swap(packed_core, "core")
-    back = spread(back, "expert")
+    back = transpose(back, pairs)
 
     gate_grad, up_grad, down_grad, done = call(
         grad_body, (struct(HALF, hidden, dtype=F32),) * 3 + (struct(8, LANES, dtype=F32),), [VMEM] * 4

time: 203 us -> 196 us (0.966)
  the two profiles are of different devices: /device:TPU:1 before, /device:TPU:4 now
where the time goes in v5:
time: 196 us; the launch traced here: 195 us
  blocking collectives  68.1 us (35%)
  waiting for transfers between devices  57.2 us (29%)
  starting transfers between devices  55.6 us (28%)
  Pallas kernels  9.93 us (5%)
  other arithmetic  2.16 us (1%)
    all_to_all x2, waiting for transfers between devices, spread(): return lax.all_to_all(x, axis, split_axis=0, concat_axis=0, tiled=True)  45 us
    all_gather x1, blocking collectives, local(): grads = lax.all_gather(grads, 'm', axis=0, tiled=True)  37.3 us
    all_to_all x2, blocking collectives, spread(): return lax.all_to_all(x, axis, split_axis=0, concat_axis=0, tiled=True)  30.8 us
    all_to_all x2, starting transfers between devices, spread(): return lax.all_to_all(x, axis, split_axis=0, concat_axis=0, tiled=True)  25.7 us
    ppermute x6, starting transfers between devices, swap(): return lax.ppermute(x, axis, [(0, 1), (1, 0)])  17.8 us
    ppermute x1, starting transfers between devices, transpose(): return lax.ppermute(x, ('m', 'expert'), moves)  12.2 us
    ppermute x1, waiting for transfers between devices, transpose(): return lax.ppermute(x, ('m', 'expert'), moves)  12.2 us
  transfers between devices with their start and end apart: 9, of which 3 were waited for; matrix products, arithmetic and copies ran while one was open for 1% of the time, Pallas kernels for 3%

profile of v5, /device:TPU:4, one launch (start us, length us, event | category | flops | bytes accessed | tf_op | source)
XLA Modules:
  0.0 194.8 jit_solution(484420181652913865)
XLA Ops:
  0.6 3.8 %collective-permute-start = (bf16[64,2048]{1,0:T(8,128)(2,1)}, bf16[64,2048]{1,0:T(8,128)(2,1)S(1)}, u32[]{:S(2)}, u32[]{:S(2)}) collective-permute-start(bf16[64,2048]{1,0:T(8,128)(2,1)} %bitcast.29), channel_id=1, source_target_pairs={{0,32},{32,0},{1,33},{33,1},{2,34},{34,2},{3,35},{35,3},{4,36},{36... | collective-permute-start | bytes 786440 | tf_op jit(solution)/shard_map/ppermute | solution.py:175
  4.5 1.7 shard_map.129
  6.2 20.1 %all_to_all.20.blocks_ref = bf16[16,8,256]{2,1,0:T(8,128)(2,1)S(1)} all-to-all(bf16[16,8,256]{2,1,0:T(8,128)(2,1)} %get-tuple-element.16), channel_id=1, replica_groups=mesh['m'=16,'p'=2,'core'=2,'expert'=16] {'expert'}, dimensions={0} | all-to-all | bytes 131072 | tf_op jit(solution)/shard_map/all_to_all | solution.py:184
  26.2 0.0 copy-start.1
  26.2 0.8 copy-done.1
  27.0 0.0 copy-start.2
  27.0 0.0 copy-start.3
  27.0 0.7 shard_map.130
  27.6 0.0 copy-start
  27.6 20.5 %all-to-all-start.1 = ((bf16[16,24,128]{2,1,0:T(8,128)(2,1)}), bf16[16,24,128]{2,1,0:T(8,128)(2,1)S(1)}, u32[]{:S(2)}, u32[]{:S(2)}) async-start(bf16[16,24,128]{2,1,0:T(8,128)(2,1)} %shard_map.130), calls=%async_computation.1 | async-start | bytes 196608 | tf_op jit(solution)/shard_map/all_to_all | solution.py:184
  48.1 0.0 collective-permute-done.pair_ref
  48.2 1.0 pad_maximum_fusion.1
  49.2 1.9 collective-permute-start.1
  51.1 0.0 copy-done.2
  51.1 0.0 copy-done.3
  51.2 2.9 %collective-permute-start.2 = (bf16[2,64,2048]{2,1,0:T(8,128)(2,1)S(1)}, bf16[2,64,2048]{2,1,0:T(8,128)(2,1)S(1)}, u32[]{:S(2)}, u32[]{:S(2)}) collective-permute-start(bf16[2,64,2048]{2,1,0:T(8,128)(2,1)S(1)} %constant_dynamic-update-slice_fusion.own_ref), channel_id=1, source_target_pairs={{0,32},{32,0},{1,33},{33,1},{2,34},{34,2},{3,35},{35,3},{4,36},{36... | collective-permute-start | bytes 1572872 | tf_op jit(solution)/shard_map/ppermute | solution.py:175
  54.1 0.1 pad_add_fusion.place_ref
  54.2 0.0 collective-permute-done.1.core_ref
  54.2 18.1 %all-to-all-done.1 = bf16[16,24,128]{2,1,0:T(8,128)(2,1)S(1)} async-done(((bf16[16,24,128]{2,1,0:T(8,128)(2,1)}), bf16[16,24,128]{2,1,0:T(8,128)(2,1)S(1)}, u32[]{:S(2)}, u32[]{:S(2)}) %all-to-all-start.1) | async-done | bytes 98336 | tf_op jit(solution)/shard_map/all_to_all | solution.py:184
  72.3 0.0 copy-done
  72.3 1.9 shard_map.131
  74.2 5.2 %all-to-all-start.2 = ((bf16[16,48,128]{2,1,0:T(8,128)(2,1)}), bf16[16,48,128]{2,1,0:T(8,128)(2,1)S(1)}, u32[]{:S(2)}, u32[]{:S(2)}) async-start(bf16[16,48,128]{2,1,0:T(8,128)(2,1)} %get-tuple-element.19), calls=%async_computation.2 | async-start | bytes 393216 | tf_op jit(solution)/shard_map/all_to_all | solution.py:184
  79.3 0.0 collective-permute-done.2.pair_ref
  79.3 1.1 pad_maximum_fusion
  80.4 1.9 collective-permute-start.3
  82.3 26.9 %all-to-all-done.2.parts_ref = bf16[16,48,128]{2,1,0:T(8,128)(2,1)S(1)} async-done(((bf16[16,48,128]{2,1,0:T(8,128)(2,1)}), bf16[16,48,128]{2,1,0:T(8,128)(2,1)S(1)}, u32[]{:S(2)}, u32[]{:S(2)}) %all-to-all-start.2) | async-done | bytes 196640 | tf_op jit(solution)/shard_map/all_to_all | solution.py:184
  109.3 37.3 %all_gather.3.grads_ref = bf16[16,144,128]{2,1,0:T(8,128)(2,1)S(1)} all-gather(bf16[1,144,128]{2,1,0:T(8,128)(2,1)S(1)} %shard_map.132), channel_id=1, replica_groups=mesh['m'=16,'p'=2,'core'=2,'expert'=16] {'m'}, dimensions={0}, use_global_device_ids=true | all-gather | bytes 626688 | tf_op jit(solution)/shard_map/all_gather | solution.py:220
  146.6 0.0 collective-permute-done.3.core_ref
  146.6 1.0 shard_map.133
  147.5 5.3 %collective-permute-start.4 = (bf16[2400,128]{1,0:T(8,128)(2,1)S(1)}, bf16[2400,128]{1,0:T(8,128)(2,1)S(1)}, u32[]{:S(2)}, u32[]{:S(2)}) collective-permute-start(bf16[2400,128]{1,0:T(8,128)(2,1)S(1)} %get-tuple-element.22), channel_id=1, source_target_pairs={{0,32},{32,0},{1,33},{33,1},{2,34},{34,2},{3,35},{35,3},{4,36},{36... | collective-permute-start | bytes 1843208 | tf_op jit(solution)/shard_map/ppermute | solution.py:175
  152.9 10.7 %all_to_all.21._ = bf16[16,8,128]{2,1,0:T(8,128)(2,1)S(1)} all-to-all(bf16[16,8,128]{2,1,0:T(8,128)(2,1)S(1)} %get-tuple-element.23), channel_id=1, replica_groups=mesh['m'=16,'p'=2,'core'=2,'expert'=16] {'expert'}, dimensions={0} | all-to-all | bytes 65536 | tf_op jit(solution)/shard_map/all_to_all | solution.py:184
  163.6 0.0 collective-permute-done.4.pair_ref
  163.6 0.0 copy-start.4
  163.6 1.1 shard_map.134
  164.7 1.9 collective-permute-start.5
  166.7 0.0 copy-done.4
  166.7 0.1 copy.18
  166.8 0.1 tile.9
  166.9 12.2 %collective-permute-start.6 = (bf16[16,8,128]{2,1,0:T(8,128)(2,1)S(1)}, bf16[16,8,128]{2,1,0:T(8,128)(2,1)S(1)}, u32[]{:S(2)}, u32[]{:S(2)}) collective-permute-start(bf16[16,8,128]{2,1,0:T(8,128)(2,1)S(1)} %all_to_all.21._), channel_id=1, source_target_pairs={{0,0},{1,64},{2,128},{3,192},{4,256},{5,320},{6,384},{7,448},{8,51... | collective-permute-start | bytes 98312 | tf_op jit(solution)/shard_map/ppermute | solution.py:180
  179.1 0.0 collective-permute-done.5.core_ref
  179.1 2.2 %shard_map.135 = (f32[64,2048]{1,0:T(8,128)}, f32[64,2048]{1,0:T(8,128)}, f32[64,2048]{1,0:T(8,128)}, f32[8,128]{1,0:T(8,128)S(1)}) custom-call(bf16[2,48,128]{2,1,0:T(8,128)(2,1)S(1)} %get-tuple-element.18.inner_ref, bf16[2304,128]{1,0:T(8,128)(2,1)S(1)} %bitcast.26, bf16[2400,128]{1,0:T(8,128)(2,1)S(1)} %collective-permute-done.4.pair_ref, ...), custom_call_target="tpu_custom_call" | custom-call | tf_op jit(solution)/shard_map/pallas_call | solution.py:234
  181.3 12.2 %collective-permute-done.6 = bf16[16,8,128]{2,1,0:T(8,128)(2,1)S(1)} collective-permute-done((bf16[16,8,128]{2,1,0:T(8,128)(2,1)S(1)}, bf16[16,8,128]{2,1,0:T(8,128)(2,1)S(1)}, u32[]{:S(2)}, u32[]{:S(2)}) %collective-permute-start.6) | collective-permute-done | bytes 32800 | tf_op jit(solution)/shard_map/ppermute | solution.py:180
  193.4 1.4 shard_map.136
  (8 shorter events, 0.1 us)
Async XLA Ops:
  0.6 47.5 %collective-permute-start = (bf16[64,2048]{1,0:T(8,128)(2,1)}, bf16[64,2048]{1,0:T(8,128)(2,1)S(1)}, u32[]{:S(2)}, u32[]{:S(2)}) collective-permute-start(bf16[64,2048]{1,0:T(8,128)(2,1)} %bitcast.29), channel_id=1, source_target_pairs={{0,32},{32,0},{1,33},{33,1},{2,34},{34,2},{3,35},{35,3},{4,36},{36... | collective-permute-start | bytes 786440 | tf_op jit(solution)/shard_map/ppermute | solution.py:175
  26.2 0.8 copy-start.1
  27.0 24.1 %copy-start.2 = (bf16[1,64,2048]{2,1,0:T(8,128)(2,1)S(1)}, bf16[1,64,2048]{2,1,0:T(8,128)(2,1)}, u32[]{:S(2)}) copy-start(bf16[1,64,2048]{2,1,0:T(8,128)(2,1)} %param.17) | copy-start | bytes 786436
  27.0 24.2 %copy-start.3 = (bf16[1,64,2048]{2,1,0:T(8,128)(2,1)S(1)}, bf16[1,64,2048]{2,1,0:T(8,128)(2,1)}, u32[]{:S(2)}) copy-start(bf16[1,64,2048]{2,1,0:T(8,128)(2,1)} %param.18) | copy-start | bytes 786436
  27.6 44.6 %copy-start = (bf16[1,2048,64]{1,2,0:T(8,128)(2,1)S(1)}, bf16[1,2048,64]{1,2,0:T(8,128)(2,1)}, u32[]{:S(2)}) copy-start(bf16[1,2048,64]{1,2,0:T(8,128)(2,1)} %param.19) | copy-start | bytes 786436
  27.6 44.6 %all-to-all-start.1 = ((bf16[16,24,128]{2,1,0:T(8,128)(2,1)}), bf16[16,24,128]{2,1,0:T(8,128)(2,1)S(1)}, u32[]{:S(2)}, u32[]{:S(2)}) async-start(bf16[16,24,128]{2,1,0:T(8,128)(2,1)} %shard_map.130), calls=%async_computation.1 | async-start | bytes 196608 | tf_op jit(solution)/shard_map/all_to_all | solution.py:184
  49.2 5.0 %collective-permute-start.1 = (bf16[2,64,2048]{2,1,0:T(8,128)(2,1)S(1)}, bf16[2,64,2048]{2,1,0:T(8,128)(2,1)S(1)}, u32[]{:S(2)}, u32[]{:S(2)}) collective-permute-start(bf16[2,64,2048]{2,1,0:T(8,128)(2,1)S(1)} %pad_maximum_fusion.1), channel_id=1, source_target_pairs={{0,16},{16,0},{1,17},{17,1},{2,18},{18,2},{3,19},{19,3},{4,20},{20... | collective-permute-start | bytes 1572872 | tf_op jit(solution)/shard_map/ppermute | solution.py:175
  51.2 28.2 %collective-permute-start.2 = (bf16[2,64,2048]{2,1,0:T(8,128)(2,1)S(1)}, bf16[2,64,2048]{2,1,0:T(8,128)(2,1)S(1)}, u32[]{:S(2)}, u32[]{:S(2)}) collective-permute-start(bf16[2,64,2048]{2,1,0:T(8,128)(2,1)S(1)} %constant_dynamic-update-slice_fusion.own_ref), channel_id=1, source_target_pairs={{0,32},{32,0},{1,33},{33,1},{2,34},{34,2},{3,35},{35,3},{4,36},{36... | collective-permute-start | bytes 1572872 | tf_op jit(solution)/shard_map/ppermute | solution.py:175
  74.2 35.1 %all-to-all-start.2 = ((bf16[16,48,128]{2,1,0:T(8,128)(2,1)}), bf16[16,48,128]{2,1,0:T(8,128)(2,1)S(1)}, u32[]{:S(2)}, u32[]{:S(2)}) async-start(bf16[16,48,128]{2,1,0:T(8,128)(2,1)} %get-tuple-element.19), calls=%async_computation.2 | async-start | bytes 393216 | tf_op jit(solution)/shard_map/all_to_all | solution.py:184
  80.4 66.1 %collective-permute-start.3 = (bf16[2,2,64,2048]{3,2,1,0:T(8,128)(2,1)}, bf16[2,2,64,2048]{3,2,1,0:T(8,128)(2,1)S(1)}, u32[]{:S(2)}, u32[]{:S(2)}) collective-permute-start(bf16[2,2,64,2048]{3,2,1,0:T(8,128)(2,1)} %pad_maximum_fusion), channel_id=1, source_target_pairs={{0,16},{16,0},{1,17},{17,1},{2,18},{18,2},{3,19},{19,3},{4,20},{20... | collective-permute-start | bytes 3145736 | tf_op jit(solution)/shard_map/ppermute | solution.py:175
  147.5 16.1 %collective-permute-start.4 = (bf16[2400,128]{1,0:T(8,128)(2,1)S(1)}, bf16[2400,128]{1,0:T(8,128)(2,1)S(1)}, u32[]{:S(2)}, u32[]{:S(2)}) collective-permute-start(bf16[2400,128]{1,0:T(8,128)(2,1)S(1)} %get-tuple-element.22), channel_id=1, source_target_pairs={{0,32},{32,0},{1,33},{33,1},{2,34},{34,2},{3,35},{35,3},{4,36},{36... | collective-permute-start | bytes 1843208 | tf_op jit(solution)/shard_map/ppermute | solution.py:175
  163.6 3.1 %copy-start.4 = (s32[1,16,3]{1,0,2:T(1,128)S(1)}, s32[1,16,3]{1,0,2:T(1,128)}, u32[]{:S(2)}) copy-start(s32[1,16,3]{1,0,2:T(1,128)} %param.12) | copy-start | bytes 580
  164.7 14.4 %collective-permute-start.5 = (bf16[2,2352,128]{2,1,0:T(8,128)(2,1)}, bf16[2,2352,128]{2,1,0:T(8,128)(2,1)S(1)}, u32[]{:S(2)}, u32[]{:S(2)}) collective-permute-start(bf16[2,2352,128]{2,1,0:T(8,128)(2,1)} %shard_map.134), channel_id=1, source_target_pairs={{0,16},{16,0},{1,17},{17,1},{2,18},{18,2},{3,19},{19,3},{4,20},{20... | collective-permute-start | bytes 3612680 | tf_op jit(solution)/shard_map/ppermute | solution.py:175
  166.9 26.5 %collective-permute-start.6 = (bf16[16,8,128]{2,1,0:T(8,128)(2,1)S(1)}, bf16[16,8,128]{2,1,0:T(8,128)(2,1)S(1)}, u32[]{:S(2)}, u32[]{:S(2)}) collective-permute-start(bf16[16,8,128]{2,1,0:T(8,128)(2,1)S(1)} %all_to_all.21._), channel_id=1, source_target_pairs={{0,0},{1,64},{2,128},{3,192},{4,256},{5,320},{6,384},{7,448},{8,51... | collective-permute-start | bytes 98312 | tf_op jit(solution)/shard_map/ppermute | solution.py:180

commit v6 on v5

--- a/solution.py
+++ b/solution.py
@@ -52,12 +52,15 @@
     return matmul(order.astype(BF16), x)
 
 
-def pick_body(picked_ref, counts_ref, weights_ref, tokens_ref, grads_ref, gate_ref, up_ref, out_ref, saved_ref, rows):
+def saved_body(gate_ref, up_ref, out_ref):
     blank = jnp.zeros((4 - CAP, LANES), F32)
-    for k in range(saved_ref.shape[0]):
+    for k in range(out_ref.shape[0]):
         columns = slice(k * LANES, (k + 1) * LANES)
         parts = [gate_ref[:, columns].astype(F32), blank, up_ref[:, columns].astype(F32), blank]
-        saved_ref[k] = jnp.concatenate(parts).astype(BF16)
+        out_ref[k] = jnp.concatenate(parts).astype(BF16)
+
+
+def pick_body(picked_ref, counts_ref, weights_ref, tokens_ref, grads_ref, out_ref, rows):
     experts = out_ref.shape[0]
     diagonal = iota((experts, experts), 0) == iota((experts, experts), 1)
     rows[...] = jnp.zeros_like(rows)
@@ -112,7 +115,7 @@
     out_ref[0, 2 * slots :, :] = (a * q * b).astype(BF16)
 
 
-def slot_body(grads_ref, outer_ref, own_ref, pair_ref, core_ref, out_ref, packed_ref):
+def slot_body(place_ref, grads_ref, outer_ref, own_ref, pair_ref, core_ref, out_ref, packed_ref):
     pairs = grads_ref.shape[0]
     packed_ref[: -2 * CAP * pairs, :] = grads_ref[...].reshape(-1, LANES)
     packed_ref[-2 * CAP * pairs :, :] = outer_ref[...].reshape(-1, LANES)
@@ -128,7 +131,7 @@
     row, slot = iota((8 * pairs, slots), 0), iota((8 * pairs, slots), 1)
     placed = 0.0
     for half in range(2):
-        place = (slot % pairs == row // 8) & (row % 8 == 4 * half + slot // pairs)
+        place = (slot % pairs == (row // 8) ^ place_ref[2]) & (row % 8 == 4 * half + slot // pairs)
         placed = placed + matmul(place.astype(BF16), total[half].astype(BF16))
     out_ref[...] = placed.astype(BF16).reshape(out_ref.shape)
 
@@ -176,7 +179,7 @@
 
 
 def transpose(x, pairs):
-    moves = [(m * pairs + f, f * pairs + m) for m in range(pairs) for f in range(pairs)]
+    moves = [(m * pairs + f, (m ^ f) * pairs + m) for m in range(pairs) for f in range(pairs)]
     return lax.ppermute(x, ("m", "expert"), moves)
 
 
@@ -189,15 +192,16 @@
     token_count, width = tokens.shape
     hidden = w_gate.shape[2]
     slots = CAP * pairs
-    place = jnp.stack([lax.axis_index("p"), lax.axis_index("core")]).astype(jnp.int32)
-
-    outgoing, saved = call(
+    place = jnp.stack([lax.axis_index("p"), lax.axis_index("core"), lax.axis_index("m")]).astype(jnp.int32)
+
+    outgoing = call(
         pick_body,
-        (struct(experts, 8, width), struct(pairs, 8, LANES)),
-        [FETCH] * 7,
+        struct(experts, 8, width),
+        [FETCH] * 5,
         scratch=(pltpu.VMEM((width // LANES, 8 * experts, LANES), F32),),
         limit=60,
-    )(picked.transpose(2, 0, 1), pick_counts, router_weights.transpose(2, 0, 1), tokens, grad_out, saved_gate[0], saved_up[0])
+    )(picked.transpose(2, 0, 1), pick_counts, router_weights.transpose(2, 0, 1), tokens, grad_out)
+    saved = call(saved_body, struct(pairs, 8, LANES), [VMEM] * 2)(saved_gate[0], saved_up[0])
     blocks = spread(outgoing, "expert")
 
     down = w_down[0].T
@@ -221,8 +225,8 @@
     flat = grads.reshape(3 * slots * pairs, LANES)
     packed_rows = 3 * slots * pairs + 2 * slots
     back, packed = call(
-        slot_body, (struct(pairs, 8, LANES), struct(packed_rows, LANES)), [VMEM] * 5
-    )(grads, outer, own, pair, core)
+        slot_body, (struct(pairs, 8, LANES), struct(packed_rows, LANES)), [SMEM] + [VMEM] * 5
+    )(place, grads, outer, own, pair, core)
     packed_pair = swap(packed, "p")
     back = spread(back, "expert")
     packed_core = call(join_body, struct(2, packed_rows - slots, LANES), [ANY] + [VMEM] * 3)(

time: 196 us -> 193 us (0.985)
  blocking collectives: 68.1 us -> 48.2 us
  starting transfers between devices: 55.6 us -> 70 us
    all_to_all x2 -> x1, blocking collectives: 30.8 us -> 11 us  [spread(): return lax.all_to_all(x, axis, split_axis=0, concat_axis=0, tiled=True)]
    all_to_all x2 -> x3, starting transfers between devices: 25.7 us -> 40.2 us  [spread(): return lax.all_to_all(x, axis, split_axis=0, concat_axis=0, tiled=True)]
    all_to_all x2 -> x3, waiting for transfers between devices: 45 us -> 49 us  [spread(): return lax.all_to_all(x, axis, split_axis=0, concat_axis=0, tiled=True)]
    ppermute x1, waiting for transfers between devices: 12.2 us -> 10.1 us  [transpose(): return lax.ppermute(x, ('m', 'expert'), moves)]
  transfers between devices with their start and end apart: 9 -> 10, of which waited for: 3 -> 4; matrix products, arithmetic and copies ran while one was open for 1% -> 1% of each run, Pallas kernels for 3% -> 3%
where the time goes in v6:
time: 193 us; the launch traced here: 192 us
  starting transfers between devices  70 us (36%)
  waiting for transfers between devices  59.1 us (31%)
  blocking collectives  48.2 us (25%)
  Pallas kernels  10.5 us (5%)
  other arithmetic  2.17 us (1%)
    all_to_all x3, waiting for transfers between devices, spread(): return lax.all_to_all(x, axis, split_axis=0, concat_axis=0, tiled=True)  49 us
    all_to_all x3, starting transfers between devices, spread(): return lax.all_to_all(x, axis, split_axis=0, concat_axis=0, tiled=True)  40.2 us
    all_gather x1, blocking collectives, local(): grads = lax.all_gather(grads, 'm', axis=0, tiled=True)  37.2 us
    ppermute x6, starting transfers between devices, swap(): return lax.ppermute(x, axis, [(0, 1), (1, 0)])  17.9 us
    ppermute x1, starting transfers between devices, transpose(): return lax.ppermute(x, ('m', 'expert'), moves)  11.9 us
    all_to_all x1, blocking collectives, spread(): return lax.all_to_all(x, axis, split_axis=0, concat_axis=0, tiled=True)  11 us
    ppermute x1, waiting for transfers between devices, transpose(): return lax.ppermute(x, ('m', 'expert'), moves)  10.1 us
  transfers between devices with their start and end apart: 10, of which 4 were waited for; matrix products, arithmetic and copies ran while one was open for 1% of the time, Pallas kernels for 3%

profile of v6, /device:TPU:4, one launch (start us, length us, event | category | flops | bytes accessed | tf_op | source)
XLA Modules:
  0.0 192.5 jit_solution(16771906267502246156)
XLA Ops:
  0.6 0.0 copy-start.3
  0.6 4.0 %collective-permute-start = (bf16[64,2048]{1,0:T(8,128)(2,1)}, bf16[64,2048]{1,0:T(8,128)(2,1)S(1)}, u32[]{:S(2)}, u32[]{:S(2)}) collective-permute-start(bf16[64,2048]{1,0:T(8,128)(2,1)} %bitcast.30), channel_id=1, source_target_pairs={{0,32},{32,0},{1,33},{33,1},{2,34},{34,2},{3,35},{35,3},{4,36},{36... | collective-permute-start | bytes 786440 | tf_op jit(solution)/shard_map/ppermute | solution.py:178
  4.6 1.7 shard_map.129
  6.3 14.6 %all-to-all-start = ((bf16[16,8,256]{2,1,0:T(8,128)(2,1)}), bf16[16,8,256]{2,1,0:T(8,128)(2,1)S(1)}, u32[]{:S(2)}, u32[]{:S(2)}) async-start(bf16[16,8,256]{2,1,0:T(8,128)(2,1)} %shard_map.129), calls=%async_computation | async-start | bytes 131072 | tf_op jit(solution)/shard_map/all_to_all | solution.py:187
  20.9 0.0 copy-start.1
  20.9 0.7 copy-done.1
  21.6 0.0 copy-start.2
  21.6 0.7 copy-done.2
  22.3 0.0 copy-start.4
  22.3 4.0 %all-to-all-done.blocks_ref = bf16[16,8,256]{2,1,0:T(8,128)(2,1)S(1)} async-done(((bf16[16,8,256]{2,1,0:T(8,128)(2,1)}), bf16[16,8,256]{2,1,0:T(8,128)(2,1)S(1)}, u32[]{:S(2)}, u32[]{:S(2)}) %all-to-all-start) | async-done | bytes 65568 | tf_op jit(solution)/shard_map/all_to_all | solution.py:187
  26.4 0.7 shard_map.131
  27.0 0.0 copy-start
  27.0 20.5 %all-to-all-start.1 = ((bf16[16,24,128]{2,1,0:T(8,128)(2,1)}), bf16[16,24,128]{2,1,0:T(8,128)(2,1)S(1)}, u32[]{:S(2)}, u32[]{:S(2)}) async-start(bf16[16,24,128]{2,1,0:T(8,128)(2,1)} %shard_map.131), calls=%async_computation.1 | async-start | bytes 196608 | tf_op jit(solution)/shard_map/all_to_all | solution.py:187
  47.5 0.0 collective-permute-done.pair_ref
  47.5 1.0 pad_maximum_fusion.1
  48.5 1.9 collective-permute-start.1
  50.5 0.0 copy-done.3
  50.5 0.0 copy-done.4
  50.5 2.9 %collective-permute-start.2 = (bf16[2,64,2048]{2,1,0:T(8,128)(2,1)S(1)}, bf16[2,64,2048]{2,1,0:T(8,128)(2,1)S(1)}, u32[]{:S(2)}, u32[]{:S(2)}) collective-permute-start(bf16[2,64,2048]{2,1,0:T(8,128)(2,1)S(1)} %constant_dynamic-update-slice_fusion.own_ref), channel_id=1, source_target_pairs={{0,32},{32,0},{1,33},{33,1},{2,34},{34,2},{3,35},{35,3},{4,36},{36... | collective-permute-start | bytes 1572872 | tf_op jit(solution)/shard_map/ppermute | solution.py:178
  53.5 0.1 pad_add_fusion.place_ref
  53.5 0.0 collective-permute-done.1.core_ref
  53.5 18.1 %all-to-all-done.1 = bf16[16,24,128]{2,1,0:T(8,128)(2,1)S(1)} async-done(((bf16[16,24,128]{2,1,0:T(8,128)(2,1)}), bf16[16,24,128]{2,1,0:T(8,128)(2,1)S(1)}, u32[]{:S(2)}, u32[]{:S(2)}) %all-to-all-start.1) | async-done | bytes 98336 | tf_op jit(solution)/shard_map/all_to_all | solution.py:187
  71.6 0.0 copy-done
  71.6 1.9 shard_map.132
  73.5 5.2 %all-to-all-start.2 = ((bf16[16,48,128]{2,1,0:T(8,128)(2,1)}), bf16[16,48,128]{2,1,0:T(8,128)(2,1)S(1)}, u32[]{:S(2)}, u32[]{:S(2)}) async-start(bf16[16,48,128]{2,1,0:T(8,128)(2,1)} %get-tuple-element.15), calls=%async_computation.2 | async-start | bytes 393216 | tf_op jit(solution)/shard_map/all_to_all | solution.py:187
  78.7 0.0 collective-permute-done.2.pair_ref
  78.7 1.1 pad_maximum_fusion
  79.8 1.9 collective-permute-start.3
  81.7 26.9 %all-to-all-done.2.parts_ref = bf16[16,48,128]{2,1,0:T(8,128)(2,1)S(1)} async-done(((bf16[16,48,128]{2,1,0:T(8,128)(2,1)}), bf16[16,48,128]{2,1,0:T(8,128)(2,1)S(1)}, u32[]{:S(2)}, u32[]{:S(2)}) %all-to-all-start.2) | async-done | bytes 196640 | tf_op jit(solution)/shard_map/all_to_all | solution.py:187
  108.7 37.2 %all_gather.3.grads_ref = bf16[16,144,128]{2,1,0:T(8,128)(2,1)S(1)} all-gather(bf16[1,144,128]{2,1,0:T(8,128)(2,1)S(1)} %shard_map.133), channel_id=1, replica_groups=mesh['m'=16,'p'=2,'core'=2,'expert'=16] {'m'}, dimensions={0}, use_global_device_ids=true | all-gather | bytes 626688 | tf_op jit(solution)/shard_map/all_gather | solution.py:224
  145.9 0.0 collective-permute-done.3.core_ref
  145.9 1.6 shard_map.134
  147.5 5.2 %collective-permute-start.4 = (bf16[2400,128]{1,0:T(8,128)(2,1)S(1)}, bf16[2400,128]{1,0:T(8,128)(2,1)S(1)}, u32[]{:S(2)}, u32[]{:S(2)}) collective-permute-start(bf16[2400,128]{1,0:T(8,128)(2,1)S(1)} %get-tuple-element.18), channel_id=1, source_target_pairs={{0,32},{32,0},{1,33},{33,1},{2,34},{34,2},{3,35},{35,3},{4,36},{36... | collective-permute-start | bytes 1843208 | tf_op jit(solution)/shard_map/ppermute | solution.py:178
  152.7 11.0 %all_to_all.20._ = bf16[16,8,128]{2,1,0:T(8,128)(2,1)S(1)} all-to-all(bf16[16,8,128]{2,1,0:T(8,128)(2,1)S(1)} %get-tuple-element.19), channel_id=1, replica_groups=mesh['m'=16,'p'=2,'core'=2,'expert'=16] {'expert'}, dimensions={0} | all-to-all | bytes 65536 | tf_op jit(solution)/shard_map/all_to_all | solution.py:187
  163.7 0.0 collective-permute-done.4.pair_ref
  163.7 0.0 copy-start.5
  163.7 1.1 shard_map.135
  164.8 1.9 collective-permute-start.5
  166.7 0.0 copy-done.5
  166.7 0.1 copy.18
  166.8 0.1 tile.9
  167.0 11.9 %collective-permute-start.6 = (bf16[16,8,128]{2,1,0:T(8,128)(2,1)S(1)}, bf16[16,8,128]{2,1,0:T(8,128)(2,1)S(1)}, u32[]{:S(2)}, u32[]{:S(2)}) collective-permute-start(bf16[16,8,128]{2,1,0:T(8,128)(2,1)S(1)} %all_to_all.20._), channel_id=1, source_target_pairs={{0,0},{1,64},{2,128},{3,192},{4,256},{5,320},{6,384},{7,448},{8,51... | collective-permute-start | bytes 98312 | tf_op jit(solution)/shard_map/ppermute | solution.py:183
  178.8 0.0 collective-permute-done.5.core_ref
  178.8 2.2 %shard_map.136 = (f32[64,2048]{1,0:T(8,128)}, f32[64,2048]{1,0:T(8,128)}, f32[64,2048]{1,0:T(8,128)}, f32[8,128]{1,0:T(8,128)S(1)}) custom-call(bf16[2,48,128]{2,1,0:T(8,128)(2,1)S(1)} %get-tuple-element.14.inner_ref, bf16[2304,128]{1,0:T(8,128)(2,1)S(1)} %bitcast.27, bf16[2400,128]{1,0:T(8,128)(2,1)S(1)} %collective-permute-done.4.pair_ref, ...), custom_call_target="tpu_custom_call" | custom-call | tf_op jit(solution)/shard_map/pallas_call | solution.py:238
  181.0 10.1 %collective-permute-done.6 = bf16[16,8,128]{2,1,0:T(8,128)(2,1)S(1)} collective-permute-done((bf16[16,8,128]{2,1,0:T(8,128)(2,1)S(1)}, bf16[16,8,128]{2,1,0:T(8,128)(2,1)S(1)}, u32[]{:S(2)}, u32[]{:S(2)}) %collective-permute-start.6) | collective-permute-done | bytes 32800 | tf_op jit(solution)/shard_map/ppermute | solution.py:183
  191.1 1.4 shard_map.137
  (9 shorter events, 0.1 us)
Async XLA Ops:
  0.6 49.8 %copy-start.3 = (bf16[1,64,2048]{2,1,0:T(8,128)(2,1)S(1)}, bf16[1,64,2048]{2,1,0:T(8,128)(2,1)}, u32[]{:S(2)}) copy-start(bf16[1,64,2048]{2,1,0:T(8,128)(2,1)} %param.17) | copy-start | bytes 786436
  0.6 46.9 %collective-permute-start = (bf16[64,2048]{1,0:T(8,128)(2,1)}, bf16[64,2048]{1,0:T(8,128)(2,1)S(1)}, u32[]{:S(2)}, u32[]{:S(2)}) collective-permute-start(bf16[64,2048]{1,0:T(8,128)(2,1)} %bitcast.30), channel_id=1, source_target_pairs={{0,32},{32,0},{1,33},{33,1},{2,34},{34,2},{3,35},{35,3},{4,36},{36... | collective-permute-start | bytes 786440 | tf_op jit(solution)/shard_map/ppermute | solution.py:178
  6.3 20.1 %all-to-all-start = ((bf16[16,8,256]{2,1,0:T(8,128)(2,1)}), bf16[16,8,256]{2,1,0:T(8,128)(2,1)S(1)}, u32[]{:S(2)}, u32[]{:S(2)}) async-start(bf16[16,8,256]{2,1,0:T(8,128)(2,1)} %shard_map.129), calls=%async_computation | async-start | bytes 131072 | tf_op jit(solution)/shard_map/all_to_all | solution.py:187
  20.9 0.7 copy-start.1
  21.6 0.7 copy-start.2
  22.3 28.2 %copy-start.4 = (bf16[1,64,2048]{2,1,0:T(8,128)(2,1)S(1)}, bf16[1,64,2048]{2,1,0:T(8,128)(2,1)}, u32[]{:S(2)}) copy-start(bf16[1,64,2048]{2,1,0:T(8,128)(2,1)} %param.18) | copy-start | bytes 786436
  27.0 44.6 %copy-start = (bf16[1,2048,64]{1,2,0:T(8,128)(2,1)S(1)}, bf16[1,2048,64]{1,2,0:T(8,128)(2,1)}, u32[]{:S(2)}) copy-start(bf16[1,2048,64]{1,2,0:T(8,128)(2,1)} %param.19) | copy-start | bytes 786436
  27.0 44.6 %all-to-all-start.1 = ((bf16[16,24,128]{2,1,0:T(8,128)(2,1)}), bf16[16,24,128]{2,1,0:T(8,128)(2,1)S(1)}, u32[]{:S(2)}, u32[]{:S(2)}) async-start(bf16[16,24,128]{2,1,0:T(8,128)(2,1)} %shard_map.131), calls=%async_computation.1 | async-start | bytes 196608 | tf_op jit(solution)/shard_map/all_to_all | solution.py:187
  48.5 5.0 %collective-permute-start.1 = (bf16[2,64,2048]{2,1,0:T(8,128)(2,1)S(1)}, bf16[2,64,2048]{2,1,0:T(8,128)(2,1)S(1)}, u32[]{:S(2)}, u32[]{:S(2)}) collective-permute-start(bf16[2,64,2048]{2,1,0:T(8,128)(2,1)S(1)} %pad_maximum_fusion.1), channel_id=1, source_target_pairs={{0,16},{16,0},{1,17},{17,1},{2,18},{18,2},{3,19},{19,3},{4,20},{20... | collective-permute-start | bytes 1572872 | tf_op jit(solution)/shard_map/ppermute | solution.py:178
  50.5 28.2 %collective-permute-start.2 = (bf16[2,64,2048]{2,1,0:T(8,128)(2,1)S(1)}, bf16[2,64,2048]{2,1,0:T(8,128)(2,1)S(1)}, u32[]{:S(2)}, u32[]{:S(2)}) collective-permute-start(bf16[2,64,2048]{2,1,0:T(8,128)(2,1)S(1)} %constant_dynamic-update-slice_fusion.own_ref), channel_id=1, source_target_pairs={{0,32},{32,0},{1,33},{33,1},{2,34},{34,2},{3,35},{35,3},{4,36},{36... | collective-permute-start | bytes 1572872 | tf_op jit(solution)/shard_map/ppermute | solution.py:178
  73.5 35.1 %all-to-all-start.2 = ((bf16[16,48,128]{2,1,0:T(8,128)(2,1)}), bf16[16,48,128]{2,1,0:T(8,128)(2,1)S(1)}, u32[]{:S(2)}, u32[]{:S(2)}) async-start(bf16[16,48,128]{2,1,0:T(8,128)(2,1)} %get-tuple-element.15), calls=%async_computation.2 | async-start | bytes 393216 | tf_op jit(solution)/shard_map/all_to_all | solution.py:187
  79.8 66.1 %collective-permute-start.3 = (bf16[2,2,64,2048]{3,2,1,0:T(8,128)(2,1)}, bf16[2,2,64,2048]{3,2,1,0:T(8,128)(2,1)S(1)}, u32[]{:S(2)}, u32[]{:S(2)}) collective-permute-start(bf16[2,2,64,2048]{3,2,1,0:T(8,128)(2,1)} %pad_maximum_fusion), channel_id=1, source_target_pairs={{0,16},{16,0},{1,17},{17,1},{2,18},{18,2},{3,19},{19,3},{4,20},{20... | collective-permute-start | bytes 3145736 | tf_op jit(solution)/shard_map/ppermute | solution.py:178
  147.5 16.2 %collective-permute-start.4 = (bf16[2400,128]{1,0:T(8,128)(2,1)S(1)}, bf16[2400,128]{1,0:T(8,128)(2,1)S(1)}, u32[]{:S(2)}, u32[]{:S(2)}) collective-permute-start(bf16[2400,128]{1,0:T(8,128)(2,1)S(1)} %get-tuple-element.18), channel_id=1, source_target_pairs={{0,32},{32,0},{1,33},{33,1},{2,34},{34,2},{3,35},{35,3},{4,36},{36... | collective-permute-start | bytes 1843208 | tf_op jit(solution)/shard_map/ppermute | solution.py:178
  163.7 3.0 %copy-start.5 = (s32[1,16,3]{1,0,2:T(1,128)S(1)}, s32[1,16,3]{1,0,2:T(1,128)}, u32[]{:S(2)}) copy-start(s32[1,16,3]{1,0,2:T(1,128)} %param.12) | copy-start | bytes 580
  164.8 14.0 %collective-permute-start.5 = (bf16[2,2352,128]{2,1,0:T(8,128)(2,1)}, bf16[2,2352,128]{2,1,0:T(8,128)(2,1)S(1)}, u32[]{:S(2)}, u32[]{:S(2)}) collective-permute-start(bf16[2,2352,128]{2,1,0:T(8,128)(2,1)} %shard_map.135), channel_id=1, source_target_pairs={{0,16},{16,0},{1,17},{17,1},{2,18},{18,2},{3,19},{19,3},{4,20},{20... | collective-permute-start | bytes 3612680 | tf_op jit(solution)/shard_map/ppermute | solution.py:178
  167.0 24.1 %collective-permute-start.6 = (bf16[16,8,128]{2,1,0:T(8,128)(2,1)S(1)}, bf16[16,8,128]{2,1,0:T(8,128)(2,1)S(1)}, u32[]{:S(2)}, u32[]{:S(2)}) collective-permute-start(bf16[16,8,128]{2,1,0:T(8,128)(2,1)S(1)} %all_to_all.20._), channel_id=1, source_target_pairs={{0,0},{1,64},{2,128},{3,192},{4,256},{5,320},{6,384},{7,448},{8,51... | collective-permute-start | bytes 98312 | tf_op jit(solution)/shard_map/ppermute | solution.py:183

commit v7 on v6

--- a/solution.py
+++ b/solution.py
@@ -16,7 +16,6 @@
 NT = (((1,), (1,)), ((), ()))
 TN = (((0,), (0,)), ((), ()))
 VMEM = pl.BlockSpec(memory_space=pltpu.VMEM)
-SMEM = pl.BlockSpec(memory_space=pltpu.SMEM)
 ANY = pl.BlockSpec(memory_space=pl.ANY)
 FETCH = pl.BlockSpec()
 
@@ -83,8 +82,8 @@
     out_ref[:, 16:, :] = saved_ref[...]
 
 
-def partial_body(place_ref, rows_ref, own_ref, pair_ref, core_ref, out_ref, saved_ref, inner_ref, outer_ref):
-    parity, core = place_ref[0], place_ref[1]
+def partial_body(rows_ref, own_ref, pair_ref, core_ref, out_ref, saved_ref, inner_ref, outer_ref):
+    parity, core = lax.axis_index("p"), lax.axis_index("core")
     pairs = out_ref.shape[0]
     slots = CAP * pairs
     rows = ordered(rows_ref[...], pairs)
@@ -115,7 +114,7 @@
     out_ref[0, 2 * slots :, :] = (a * q * b).astype(BF16)
 
 
-def slot_body(place_ref, grads_ref, outer_ref, own_ref, pair_ref, core_ref, out_ref, packed_ref):
+def slot_body(grads_ref, outer_ref, own_ref, pair_ref, core_ref, out_ref, packed_ref):
     pairs = grads_ref.shape[0]
     packed_ref[: -2 * CAP * pairs, :] = grads_ref[...].reshape(-1, LANES)
     packed_ref[-2 * CAP * pairs :, :] = outer_ref[...].reshape(-1, LANES)
@@ -131,7 +130,7 @@
     row, slot = iota((8 * pairs, slots), 0), iota((8 * pairs, slots), 1)
     placed = 0.0
     for half in range(2):
-        place = (slot % pairs == (row // 8) ^ place_ref[2]) & (row % 8 == 4 * half + slot // pairs)
+        place = (slot % pairs == (row // 8) ^ lax.axis_index("m")) & (row % 8 == 4 * half + slot // pairs)
         placed = placed + matmul(place.astype(BF16), total[half].astype(BF16))
     out_ref[...] = placed.astype(BF16).reshape(out_ref.shape)
 
@@ -161,8 +160,8 @@
     done_ref[...] = jnp.zeros_like(done_ref)
 
 
-def token_body(place_ref, _, index_ref, rows_ref, out_ref):
-    parity, core = place_ref[0], place_ref[1]
+def token_body(_, index_ref, rows_ref, out_ref):
+    parity, core = lax.axis_index("p"), lax.axis_index("core")
     tokens = iota((out_ref.shape[0], index_ref.shape[1]), 0)
     sides = []
     for side in range(2):
@@ -192,7 +191,6 @@
     token_count, width = tokens.shape
     hidden = w_gate.shape[2]
     slots = CAP * pairs
-    place = jnp.stack([lax.axis_index("p"), lax.axis_index("core"), lax.axis_index("m")]).astype(jnp.int32)
 
     outgoing = call(
         pick_body,
@@ -216,8 +214,8 @@
     parts, saved, inner, outer = call(
         partial_body,
         (struct(pairs, slots, LANES),) + (struct(2, slots, LANES),) * 3,
-        [SMEM] + [VMEM] * 4,
-    )(place, rows.reshape(24 * pairs, LANES), down, down_pair, down_core)
+        [VMEM] * 4,
+    )(rows.reshape(24 * pairs, LANES), down, down_pair, down_core)
 
     parts = spread(parts, "m")
     grads = call(hidden_body, struct(1, 3 * slots, LANES), [VMEM] * 2)(parts, saved)
@@ -225,8 +223,8 @@
     flat = grads.reshape(3 * slots * pairs, LANES)
     packed_rows = 3 * slots * pairs + 2 * slots
     back, packed = call(
-        slot_body, (struct(pairs, 8, LANES), struct(packed_rows, LANES)), [SMEM] + [VMEM] * 5
-    )(place, grads, outer, own, pair, core)
+        slot_body, (struct(pairs, 8, LANES), struct(packed_rows, LANES)), [VMEM] * 5
+    )(grads, outer, own, pair, core)
     packed_pair = swap(packed, "p")
     back = spread(back, "expert")
     packed_core = call(join_body, struct(2, packed_rows - slots, LANES), [ANY] + [VMEM] * 3)(
@@ -243,8 +241,8 @@
     index = jnp.tile(index, (1, 2)).reshape(1, -1)
     upper = jnp.arange(8 * experts, dtype=jnp.int32)[None, :] // 4 % 2
     index = jnp.where(upper == jnp.arange(2)[:, None], index, -1)
-    token_grad = call(token_body, struct(token_count, width), [SMEM] + [VMEM] * 3)(
-        place, done, index, back.reshape(8 * experts, LANES)
+    token_grad = call(token_body, struct(token_count, width), [VMEM] * 3)(
+        done, index, back.reshape(8 * experts, LANES)
     )
     return (token_grad, gate_grad[None], up_grad[None], down_grad.T[None])
 

time: 193 us -> 192 us (level)
  no operation moved by 1% of the time
where the time goes in v7:
time: 192 us; the launch traced here: 191 us
  starting transfers between devices  69.9 us (36%)
  waiting for transfers between devices  59.1 us (31%)
  blocking collectives  48.6 us (25%)
  Pallas kernels  8.85 us (5%)
  other arithmetic  2.09 us (1%)
    all_to_all x3, waiting for transfers between devices, spread(): return lax.all_to_all(x, axis, split_axis=0, concat_axis=0, tiled=True)  49 us
    all_to_all x3, starting transfers between devices, spread(): return lax.all_to_all(x, axis, split_axis=0, concat_axis=0, tiled=True)  40.1 us
    all_gather x1, blocking collectives, local(): grads = lax.all_gather(grads, 'm', axis=0, tiled=True)  37 us
    ppermute x6, starting transfers between devices, swap(): return lax.ppermute(x, axis, [(0, 1), (1, 0)])  18 us
    ppermute x1, starting transfers between devices, transpose(): return lax.ppermute(x, ('m', 'expert'), moves)  11.8 us
    all_to_all x1, blocking collectives, spread(): return lax.all_to_all(x, axis, split_axis=0, concat_axis=0, tiled=True)  11.5 us
    ppermute x1, waiting for transfers between devices, transpose(): return lax.ppermute(x, ('m', 'expert'), moves)  10.1 us
  transfers between devices with their start and end apart: 10, of which 4 were waited for; matrix products, arithmetic and copies ran while one was open for 1% of the time, Pallas kernels for 3%

profile of v7, /device:TPU:4, one launch (start us, length us, event | category | flops | bytes accessed | tf_op | source)
XLA Modules:
  0.0 191.1 jit_solution(15901738112163791319)
XLA Ops:
  0.6 0.0 copy-start.3
  0.6 4.0 %collective-permute-start = (bf16[64,2048]{1,0:T(8,128)(2,1)}, bf16[64,2048]{1,0:T(8,128)(2,1)S(1)}, u32[]{:S(2)}, u32[]{:S(2)}) collective-permute-start(bf16[64,2048]{1,0:T(8,128)(2,1)} %bitcast.27), channel_id=1, source_target_pairs={{0,32},{32,0},{1,33},{33,1},{2,34},{34,2},{3,35},{35,3},{4,36},{36... | collective-permute-start | bytes 786440 | tf_op jit(solution)/shard_map/ppermute | solution.py:177
  4.6 1.7 shard_map.129
  6.3 14.6 %all-to-all-start = ((bf16[16,8,256]{2,1,0:T(8,128)(2,1)}), bf16[16,8,256]{2,1,0:T(8,128)(2,1)S(1)}, u32[]{:S(2)}, u32[]{:S(2)}) async-start(bf16[16,8,256]{2,1,0:T(8,128)(2,1)} %shard_map.129), calls=%async_computation | async-start | bytes 131072 | tf_op jit(solution)/shard_map/all_to_all | solution.py:186
  20.9 0.0 copy-start.1
  20.9 0.7 copy-done.1
  21.6 0.0 copy-start.2
  21.6 0.7 copy-done.2
  22.3 0.0 copy-start.4
  22.3 0.0 copy-start
  22.3 4.0 %all-to-all-done.blocks_ref = bf16[16,8,256]{2,1,0:T(8,128)(2,1)S(1)} async-done(((bf16[16,8,256]{2,1,0:T(8,128)(2,1)}), bf16[16,8,256]{2,1,0:T(8,128)(2,1)S(1)}, u32[]{:S(2)}, u32[]{:S(2)}) %all-to-all-start) | async-done | bytes 65568 | tf_op jit(solution)/shard_map/all_to_all | solution.py:186
  26.4 0.7 shard_map.131
  27.0 20.4 %all-to-all-start.1 = ((bf16[16,24,128]{2,1,0:T(8,128)(2,1)}), bf16[16,24,128]{2,1,0:T(8,128)(2,1)S(1)}, u32[]{:S(2)}, u32[]{:S(2)}) async-start(bf16[16,24,128]{2,1,0:T(8,128)(2,1)} %shard_map.131), calls=%async_computation.1 | async-start | bytes 196608 | tf_op jit(solution)/shard_map/all_to_all | solution.py:186
  47.4 0.0 collective-permute-done.pair_ref
  47.4 1.0 pad_maximum_fusion.1
  48.4 1.9 %collective-permute-start.1 = (bf16[2,64,2048]{2,1,0:T(8,128)(2,1)S(1)}, bf16[2,64,2048]{2,1,0:T(8,128)(2,1)S(1)}, u32[]{:S(2)}, u32[]{:S(2)}) collective-permute-start(bf16[2,64,2048]{2,1,0:T(8,128)(2,1)S(1)} %pad_maximum_fusion.1), channel_id=1, source_target_pairs={{0,16},{16,0},{1,17},{17,1},{2,18},{18,2},{3,19},{19,3},{4,20},{20... | collective-permute-start | bytes 1572872 | tf_op jit(solution)/shard_map/ppermute | solution.py:177
  50.3 0.0 copy-done.3
  50.4 0.0 copy-done.4
  50.4 2.9 %collective-permute-start.2 = (bf16[2,64,2048]{2,1,0:T(8,128)(2,1)S(1)}, bf16[2,64,2048]{2,1,0:T(8,128)(2,1)S(1)}, u32[]{:S(2)}, u32[]{:S(2)}) collective-permute-start(bf16[2,64,2048]{2,1,0:T(8,128)(2,1)S(1)} %constant_dynamic-update-slice_fusion.own_ref), channel_id=1, source_target_pairs={{0,32},{32,0},{1,33},{33,1},{2,34},{34,2},{3,35},{35,3},{4,36},{36... | collective-permute-start | bytes 1572872 | tf_op jit(solution)/shard_map/ppermute | solution.py:177
  53.3 0.0 collective-permute-done.1.core_ref
  53.3 18.2 %all-to-all-done.1 = bf16[16,24,128]{2,1,0:T(8,128)(2,1)S(1)} async-done(((bf16[16,24,128]{2,1,0:T(8,128)(2,1)}), bf16[16,24,128]{2,1,0:T(8,128)(2,1)S(1)}, u32[]{:S(2)}, u32[]{:S(2)}) %all-to-all-start.1) | async-done | bytes 98336 | tf_op jit(solution)/shard_map/all_to_all | solution.py:186
  71.5 0.0 copy-done
  71.5 1.4 shard_map.132
  72.9 5.2 %all-to-all-start.2 = ((bf16[16,48,128]{2,1,0:T(8,128)(2,1)}), bf16[16,48,128]{2,1,0:T(8,128)(2,1)S(1)}, u32[]{:S(2)}, u32[]{:S(2)}) async-start(bf16[16,48,128]{2,1,0:T(8,128)(2,1)} %get-tuple-element.15), calls=%async_computation.2 | async-start | bytes 393216 | tf_op jit(solution)/shard_map/all_to_all | solution.py:186
  78.0 0.0 collective-permute-done.2.pair_ref
  78.0 1.1 pad_maximum_fusion
  79.1 1.9 collective-permute-start.3
  81.0 26.8 %all-to-all-done.2.parts_ref = bf16[16,48,128]{2,1,0:T(8,128)(2,1)S(1)} async-done(((bf16[16,48,128]{2,1,0:T(8,128)(2,1)}), bf16[16,48,128]{2,1,0:T(8,128)(2,1)S(1)}, u32[]{:S(2)}, u32[]{:S(2)}) %all-to-all-start.2) | async-done | bytes 196640 | tf_op jit(solution)/shard_map/all_to_all | solution.py:186
  107.9 37.0 %all_gather.3.grads_ref = bf16[16,144,128]{2,1,0:T(8,128)(2,1)S(1)} all-gather(bf16[1,144,128]{2,1,0:T(8,128)(2,1)S(1)} %shard_map.133), channel_id=1, replica_groups=mesh['m'=16,'p'=2,'core'=2,'expert'=16] {'m'}, dimensions={0}, use_global_device_ids=true | all-gather | bytes 626688 | tf_op jit(solution)/shard_map/all_gather | solution.py:222
  144.9 0.0 collective-permute-done.3.core_ref
  144.9 1.0 shard_map.134
  145.9 5.4 %collective-permute-start.4 = (bf16[2400,128]{1,0:T(8,128)(2,1)S(1)}, bf16[2400,128]{1,0:T(8,128)(2,1)S(1)}, u32[]{:S(2)}, u32[]{:S(2)}) collective-permute-start(bf16[2400,128]{1,0:T(8,128)(2,1)S(1)} %get-tuple-element.18), channel_id=1, source_target_pairs={{0,32},{32,0},{1,33},{33,1},{2,34},{34,2},{3,35},{35,3},{4,36},{36... | collective-permute-start | bytes 1843208 | tf_op jit(solution)/shard_map/ppermute | solution.py:177
  151.3 11.5 %all_to_all.20._ = bf16[16,8,128]{2,1,0:T(8,128)(2,1)S(1)} all-to-all(bf16[16,8,128]{2,1,0:T(8,128)(2,1)S(1)} %get-tuple-element.19), channel_id=1, replica_groups=mesh['m'=16,'p'=2,'core'=2,'expert'=16] {'expert'}, dimensions={0} | all-to-all | bytes 65536 | tf_op jit(solution)/shard_map/all_to_all | solution.py:186
  162.8 0.0 collective-permute-done.4.pair_ref
  162.8 0.0 copy-start.5
  162.8 1.1 shard_map.135
  164.0 1.9 collective-permute-start.5
  165.9 0.0 copy-done.5
  165.9 0.1 copy.18
  166.0 0.1 tile.9
  166.1 11.8 %collective-permute-start.6 = (bf16[16,8,128]{2,1,0:T(8,128)(2,1)S(1)}, bf16[16,8,128]{2,1,0:T(8,128)(2,1)S(1)}, u32[]{:S(2)}, u32[]{:S(2)}) collective-permute-start(bf16[16,8,128]{2,1,0:T(8,128)(2,1)S(1)} %all_to_all.20._), channel_id=1, source_target_pairs={{0,0},{1,64},{2,128},{3,192},{4,256},{5,320},{6,384},{7,448},{8,51... | collective-permute-start | bytes 98312 | tf_op jit(solution)/shard_map/ppermute | solution.py:182
  177.9 0.0 collective-permute-done.5.core_ref
  178.0 2.2 %shard_map.136 = (f32[64,2048]{1,0:T(8,128)}, f32[64,2048]{1,0:T(8,128)}, f32[64,2048]{1,0:T(8,128)}, f32[8,128]{1,0:T(8,128)S(1)}) custom-call(bf16[2,48,128]{2,1,0:T(8,128)(2,1)S(1)} %get-tuple-element.14.inner_ref, bf16[2304,128]{1,0:T(8,128)(2,1)S(1)} %bitcast.24, bf16[2400,128]{1,0:T(8,128)(2,1)S(1)} %collective-permute-done.4.pair_ref, ...), custom_call_target="tpu_custom_call" | custom-call | tf_op jit(solution)/shard_map/pallas_call | solution.py:236
  180.1 10.1 %collective-permute-done.6 = bf16[16,8,128]{2,1,0:T(8,128)(2,1)S(1)} collective-permute-done((bf16[16,8,128]{2,1,0:T(8,128)(2,1)S(1)}, bf16[16,8,128]{2,1,0:T(8,128)(2,1)S(1)}, u32[]{:S(2)}, u32[]{:S(2)}) %collective-permute-start.6) | collective-permute-done | bytes 32800 | tf_op jit(solution)/shard_map/ppermute | solution.py:182
  190.3 0.8 shard_map.137
  (9 shorter events, 0.1 us)
Async XLA Ops:
  0.6 49.7 %copy-start.3 = (bf16[1,64,2048]{2,1,0:T(8,128)(2,1)S(1)}, bf16[1,64,2048]{2,1,0:T(8,128)(2,1)}, u32[]{:S(2)}) copy-start(bf16[1,64,2048]{2,1,0:T(8,128)(2,1)} %param.17) | copy-start | bytes 786436
  0.6 46.7 %collective-permute-start = (bf16[64,2048]{1,0:T(8,128)(2,1)}, bf16[64,2048]{1,0:T(8,128)(2,1)S(1)}, u32[]{:S(2)}, u32[]{:S(2)}) collective-permute-start(bf16[64,2048]{1,0:T(8,128)(2,1)} %bitcast.27), channel_id=1, source_target_pairs={{0,32},{32,0},{1,33},{33,1},{2,34},{34,2},{3,35},{35,3},{4,36},{36... | collective-permute-start | bytes 786440 | tf_op jit(solution)/shard_map/ppermute | solution.py:177
  6.3 20.1 %all-to-all-start = ((bf16[16,8,256]{2,1,0:T(8,128)(2,1)}), bf16[16,8,256]{2,1,0:T(8,128)(2,1)S(1)}, u32[]{:S(2)}, u32[]{:S(2)}) async-start(bf16[16,8,256]{2,1,0:T(8,128)(2,1)} %shard_map.129), calls=%async_computation | async-start | bytes 131072 | tf_op jit(solution)/shard_map/all_to_all | solution.py:186
  20.9 0.7 copy-start.1
  21.6 0.7 copy-start.2
  22.3 28.1 %copy-start.4 = (bf16[1,64,2048]{2,1,0:T(8,128)(2,1)S(1)}, bf16[1,64,2048]{2,1,0:T(8,128)(2,1)}, u32[]{:S(2)}) copy-start(bf16[1,64,2048]{2,1,0:T(8,128)(2,1)} %param.18) | copy-start | bytes 786436
  22.3 49.2 %copy-start = (bf16[1,2048,64]{1,2,0:T(8,128)(2,1)S(1)}, bf16[1,2048,64]{1,2,0:T(8,128)(2,1)}, u32[]{:S(2)}) copy-start(bf16[1,2048,64]{1,2,0:T(8,128)(2,1)} %param.19) | copy-start | bytes 786436
  27.0 44.5 %all-to-all-start.1 = ((bf16[16,24,128]{2,1,0:T(8,128)(2,1)}), bf16[16,24,128]{2,1,0:T(8,128)(2,1)S(1)}, u32[]{:S(2)}, u32[]{:S(2)}) async-start(bf16[16,24,128]{2,1,0:T(8,128)(2,1)} %shard_map.131), calls=%async_computation.1 | async-start | bytes 196608 | tf_op jit(solution)/shard_map/all_to_all | solution.py:186
  48.4 4.9 %collective-permute-start.1 = (bf16[2,64,2048]{2,1,0:T(8,128)(2,1)S(1)}, bf16[2,64,2048]{2,1,0:T(8,128)(2,1)S(1)}, u32[]{:S(2)}, u32[]{:S(2)}) collective-permute-start(bf16[2,64,2048]{2,1,0:T(8,128)(2,1)S(1)} %pad_maximum_fusion.1), channel_id=1, source_target_pairs={{0,16},{16,0},{1,17},{17,1},{2,18},{18,2},{3,19},{19,3},{4,20},{20... | collective-permute-start | bytes 1572872 | tf_op jit(solution)/shard_map/ppermute | solution.py:177
  50.4 27.6 %collective-permute-start.2 = (bf16[2,64,2048]{2,1,0:T(8,128)(2,1)S(1)}, bf16[2,64,2048]{2,1,0:T(8,128)(2,1)S(1)}, u32[]{:S(2)}, u32[]{:S(2)}) collective-permute-start(bf16[2,64,2048]{2,1,0:T(8,128)(2,1)S(1)} %constant_dynamic-update-slice_fusion.own_ref), channel_id=1, source_target_pairs={{0,32},{32,0},{1,33},{33,1},{2,34},{34,2},{3,35},{35,3},{4,36},{36... | collective-permute-start | bytes 1572872 | tf_op jit(solution)/shard_map/ppermute | solution.py:177
  72.9 35.0 %all-to-all-start.2 = ((bf16[16,48,128]{2,1,0:T(8,128)(2,1)}), bf16[16,48,128]{2,1,0:T(8,128)(2,1)S(1)}, u32[]{:S(2)}, u32[]{:S(2)}) async-start(bf16[16,48,128]{2,1,0:T(8,128)(2,1)} %get-tuple-element.15), calls=%async_computation.2 | async-start | bytes 393216 | tf_op jit(solution)/shard_map/all_to_all | solution.py:186
  79.1 65.8 %collective-permute-start.3 = (bf16[2,2,64,2048]{3,2,1,0:T(8,128)(2,1)}, bf16[2,2,64,2048]{3,2,1,0:T(8,128)(2,1)S(1)}, u32[]{:S(2)}, u32[]{:S(2)}) collective-permute-start(bf16[2,2,64,2048]{3,2,1,0:T(8,128)(2,1)} %pad_maximum_fusion), channel_id=1, source_target_pairs={{0,16},{16,0},{1,17},{17,1},{2,18},{18,2},{3,19},{19,3},{4,20},{20... | collective-permute-start | bytes 3145736 | tf_op jit(solution)/shard_map/ppermute | solution.py:177
  145.9 16.9 %collective-permute-start.4 = (bf16[2400,128]{1,0:T(8,128)(2,1)S(1)}, bf16[2400,128]{1,0:T(8,128)(2,1)S(1)}, u32[]{:S(2)}, u32[]{:S(2)}) collective-permute-start(bf16[2400,128]{1,0:T(8,128)(2,1)S(1)} %get-tuple-element.18), channel_id=1, source_target_pairs={{0,32},{32,0},{1,33},{33,1},{2,34},{34,2},{3,35},{35,3},{4,36},{36... | collective-permute-start | bytes 1843208 | tf_op jit(solution)/shard_map/ppermute | solution.py:177
  162.8 3.0 %copy-start.5 = (s32[1,16,3]{1,0,2:T(1,128)S(1)}, s32[1,16,3]{1,0,2:T(1,128)}, u32[]{:S(2)}) copy-start(s32[1,16,3]{1,0,2:T(1,128)} %param.12) | copy-start | bytes 580
  164.0 14.0 %collective-permute-start.5 = (bf16[2,2352,128]{2,1,0:T(8,128)(2,1)}, bf16[2,2352,128]{2,1,0:T(8,128)(2,1)S(1)}, u32[]{:S(2)}, u32[]{:S(2)}) collective-permute-start(bf16[2,2352,128]{2,1,0:T(8,128)(2,1)} %shard_map.135), channel_id=1, source_target_pairs={{0,16},{16,0},{1,17},{17,1},{2,18},{18,2},{3,19},{19,3},{4,20},{20... | collective-permute-start | bytes 3612680 | tf_op jit(solution)/shard_map/ppermute | solution.py:177
  166.1 24.1 %collective-permute-start.6 = (bf16[16,8,128]{2,1,0:T(8,128)(2,1)S(1)}, bf16[16,8,128]{2,1,0:T(8,128)(2,1)S(1)}, u32[]{:S(2)}, u32[]{:S(2)}) collective-permute-start(bf16[16,8,128]{2,1,0:T(8,128)(2,1)S(1)} %all_to_all.20._), channel_id=1, source_target_pairs={{0,0},{1,64},{2,128},{3,192},{4,256},{5,320},{6,384},{7,448},{8,51... | collective-permute-start | bytes 98312 | tf_op jit(solution)/shard_map/ppermute | solution.py:182
